TPU v7x, 32 devices: a whole 2x2x4 slice. The times are simulated.
32 devices in a mesh: tile: 4 (over y, x), col: 8 (over z, core).
Axes of the slice: x: 2, y: 2, z: 4, core: 2. Of those that a mesh axis runs over, the one named last changes fastest.
Arguments:
- adjoint_in: float32 [25, 128, 1024], P(None, 'tile', 'col'), may hold values from -6 to 6
- centre: float32 [25, 128, 1024], P(None, 'tile', 'col'), may hold values from 0.2 to 0.6
- side_coeff: float32 [4, 25, 128, 1024], P(None, None, 'tile', 'col'), may hold values from 0.05 to 0.25
- vert_coeff: float32 [2, 25, 128, 1024], P(None, None, 'tile', 'col'), may hold values from 0.05 to 0.25
- land_mask: int32 [25, 128, 1024], P(None, 'tile', 'col'), may hold values 0 or 1
- obs_misfit: float32 [4, 8, 8, 128], P('tile', 'col'), may hold values from -6 to 6
- obs_cell: int32 [4, 8, 8, 128], P('tile', 'col'), may hold values from 0 to 102399
- obs_count: int32 [4, 8, 8], P('tile', 'col'), may hold values from 0 to 128, as said below
- fold_partner: int32 [8], replicated, may hold values from 0 to 7, as said below
- fold_flip: int32 [8], replicated, may hold values 0 or 1
Outputs:
- adjoint_out: float32 [25, 128, 1024], P(None, 'tile', 'col')
Inputs may be any that keep to these rules, and one draw needn't show every extreme that they name: `obs_count`: slots at and beyond the count hold values that are ignored; some destination gets 128 from some source in every draw. `fold_partner`: each tile column appears exactly once.
All inputs are finite; a program needn't handle non-finite values. No bound on the sum of `land_mask` on one device may be relied on, other than what follows from the above.
Results may differ from a plain program's by a relative error of at most 0.0003.
Values sent between devices are 32-bit elements; how exact they have to be, the bound alone decides.
No kernel may reach another device: no remote copies, remote signals or barrier semaphores. Data moves between devices by JAX's collectives and lax.ppermute only.
A program may use at most 64 MiB of HBM per device.

v0:
```python
import functools

import jax
import jax.numpy as jnp
from jax import lax
from jax.experimental import pallas as pl
from jax.experimental.pallas import tpu as pltpu
from jax.sharding import PartitionSpec as P

LEVELS = 25
ROWS = 32
COLS = 128
CAP = 128
GROUP = 8
PAD = 32
LINES = 4 * PAD
CORNER = 3 * LEVELS
SLOT = 80
EDGE = 32
OFFSET = (0, 50, 1, 51)
MIB = 1024 * 1024
VMEM = pl.BlockSpec(memory_space=pltpu.VMEM)
SMEM = pl.BlockSpec(memory_space=pltpu.SMEM)


def iota(shape, dim):
    return lax.broadcasted_iota(jnp.int32, shape, dim)


def turn(x, shift, axis=1):
    shift = shift % x.shape[axis]
    return pltpu.roll(x, shift, axis) if shift else x


def terms(k, value, centre, side, vert):
    row, lane = iota((ROWS, COLS), 0), iota((ROWS, COLS), 1)
    y = value[k]
    east, west = side[0, k] * y, side[1, k] * y
    north, south = turn(side[2, k] * y, 1, 0), turn(side[3, k] * y, -1, 0)
    r = centre[k] * y
    r = r + jnp.where(lane > 0, turn(east, 1), 0.0) + jnp.where(lane < COLS - 1, turn(west, -1), 0.0)
    r = r + jnp.where(row > 0, north, 0.0) + jnp.where(row < ROWS - 1, south, 0.0)
    if k + 1 < LEVELS:
        r = r + vert[0, k + 1] * value[k + 1]
    if k > 0:
        r = r + vert[1, k - 1] * value[k - 1]
    return r, east, west, north, south


def outer(lane, last, first):
    return jnp.where(lane == COLS - 1, last, jnp.where(lane == 0, first, 0.0))


def match_kernel(cell, hot):
    for s in range(cell.shape[0]):
        place = cell[s : s + 1, :] >> 7
        for k in range(LEVELS):
            match = (iota((ROWS, CAP), 0) + k * ROWS) == place
            hot[k * ROWS : (k + 1) * ROWS, s * CAP : (s + 1) * CAP] = jnp.where(match, 1.0, 0.0).astype(jnp.bfloat16)


def one_hot(sources, misfit, cell, count, hot, valued, forcing):
    group = min(GROUP, sources)
    lane = iota((1, CAP), 1)
    for first in range(0, sources, group):
        for s in range(group):
            at = slice(s * CAP, (s + 1) * CAP)
            cells = cell[first + s : first + s + 1, :]
            v = jnp.where(lane < count[0, first + s], misfit[first + s : first + s + 1, :], 0.0)
            high = v.astype(jnp.bfloat16).astype(jnp.float32)
            middle = (v - high).astype(jnp.bfloat16).astype(jnp.float32)
            low = v - high - middle
            column = iota((COLS, CAP), 0) == (cells & (COLS - 1))
            for i, part in enumerate((high, middle, low)):
                valued[i * COLS : (i + 1) * COLS, at] = jnp.where(column, part, 0.0).astype(jnp.bfloat16)
        matched = hot[:, first * CAP : (first + group) * CAP]
        part = lax.dot_general(matched, valued[...], (((1,), (1,)), ((), ())), preferred_element_type=jnp.float32)
        if first == 0:
            forcing[...] = part
        else:
            forcing[...] += part


def to_lanes(column, offset):
    level = iota((PAD, COLS), 0)
    spot = (iota((PAD, COLS), 1) == 2 * level + offset) & (level < LEVELS)
    return jnp.sum(jnp.where(spot, column, 0.0), axis=0, keepdims=True)


def to_rows(line, offset):
    level = iota((PAD, COLS), 0)
    spot = (iota((PAD, COLS), 1) == 2 * level + offset) & (level < LEVELS)
    return jnp.sum(jnp.where(spot, line, 0.0), axis=1, keepdims=True)


def spot_rows(first, last):
    row = iota((8, COLS), 0)
    return jnp.where(row == 0, first, 0.0) + jnp.where(row == 7, last, 0.0)


def ends(block):
    return block[:, COLS - 1 : COLS], block[:, 0:1]


def from_tiles(swapped, next_swapped, where, start):
    rows = slice(start, start + PAD)
    upward = where[4] == 0
    return (
        jnp.where(upward, next_swapped[rows, :], swapped[rows, :]),
        jnp.where(upward, swapped[rows, :], next_swapped[rows, :]),
    )


def first_kernel(sources, misfit, cell, count, where, hot, adjoint, side, centre, vert, mask, part, swap, next_swap, edges, slots, valued, forcing, held, up, down, base):
    one_hot(sources, misfit, cell, count, hot, valued, forcing)
    for i in range(4):
        for ref in (up, down):
            ref[i * PAD + 24 : (i + 1) * PAD, :] = jnp.zeros((8, COLS), jnp.float32)
    for k in range(LEVELS):
        rows = slice(k * ROWS, (k + 1) * ROWS)
        f = forcing[rows, 0:COLS] + forcing[rows, COLS : 2 * COLS] + forcing[rows, 2 * COLS : 3 * COLS]
        held[k] = adjoint[k] + f
    lane = iota((ROWS, COLS), 1)
    packed = [jnp.zeros((ROWS, COLS), jnp.float32)] * 3
    for k in range(LEVELS):
        r, east, west, north, south = terms(k, held, centre, side, vert)
        m = mask[k].astype(jnp.float32)
        part[k] = r
        sides = outer(lane, east, west)
        for ref, leaving, at, which, i in ((up, north[0:1], ROWS - 1, 2, 0), (down, south[ROWS - 1 : ROWS], 0, 3, 1)):
            ref[k : k + 1, :] = leaving
            ref[PAD + k : PAD + k + 1, :] = r[at : at + 1]
            ref[2 * PAD + k : 2 * PAD + k + 1, :] = (m * side[which, k])[at : at + 1]
            ref[3 * PAD + k : 3 * PAD + k + 1, :] = sides[at : at + 1]
        fields = (sides, outer(lane, r, r), m * outer(lane, side[0, k], side[1, k]))
        packed = [p + turn(x, 2 * k + 1) for p, x in zip(packed, fields)]
    for i in range(3):
        base[i * LEVELS : (i + 1) * LEVELS, :] = up[i * PAD : i * PAD + LEVELS, :]
    own_east, own_west = ends(up[3 * PAD : 4 * PAD, :])
    base[CORNER : CORNER + 1, :] = to_lanes(own_east, OFFSET[0]) + to_lanes(own_west, OFFSET[1])
    base[CORNER + 1 : SLOT, :] = jnp.zeros((SLOT - CORNER - 1, COLS), jnp.float32)
    for s in range(sources):
        slots[s] = base[...]
    upward = where[4] == 0
    swap[...] = jnp.where(upward, up[...], down[...])
    next_swap[...] = jnp.where(upward, down[...], up[...])
    even = (iota((8, COLS), 1) & 1) == 0
    for i, p in enumerate(packed):
        eastward = westward = jnp.zeros((8, COLS), jnp.float32)
        for g, offset in enumerate(OFFSET):
            rows = p[8 * g : 8 * g + 8]
            eastward = eastward + turn(jnp.where(even, rows, 0.0), offset)
            westward = westward + turn(jnp.where(even, 0.0, rows), offset - 1)
        edges[8 * i : 8 * i + 8, :] = eastward
        edges[24 + 8 * i : 32 + 8 * i, :] = westward


def corner_kernel(swapped, next_swapped, edges, where, swap, next_swap):
    low, high = from_tiles(swapped, next_swapped, where, 0)
    low_sides, high_sides = from_tiles(swapped, next_swapped, where, 3 * PAD)
    low_last, low_first = ends(low)
    high_last, high_first = ends(high)
    low_east, low_west = ends(low_sides)
    high_east, high_west = ends(high_sides)
    corners = (
        to_lanes(low_east, OFFSET[0]) + to_lanes(low_west, OFFSET[1]) + to_lanes(high_west, OFFSET[2]) + to_lanes(high_east, OFFSET[3])
    )
    eastward = spot_rows(to_lanes(low_last, OFFSET[0]), to_lanes(high_last, OFFSET[3]))
    westward = spot_rows(to_lanes(low_first, OFFSET[0]), to_lanes(high_first, OFFSET[3]))
    to_east = where[5] == 0
    for ref, chosen in ((swap, to_east), (next_swap, jnp.logical_not(to_east))):
        ref[0:24, :] = jnp.where(chosen, edges[0:24, :], edges[24:48, :])
        ref[8:16, :] += jnp.where(chosen, eastward, westward)
        ref[24:EDGE, :] = jnp.where(iota((EDGE - 24, COLS), 0) == 0, corners, 0.0)


def second_kernel(swapped, next_swapped, sent_first, sent_next, beside, next_beside, edges, got, partner, flip, where, part, mask, side, centre, vert, out, held, lines, near_sides, far_sides, west_side, east_side):
    sources = got.shape[0]
    below_near, above_near = from_tiles(swapped, next_swapped, where, 0)
    below_part, above_part = from_tiles(swapped, next_swapped, where, PAD)
    below_scale, above_scale = from_tiles(swapped, next_swapped, where, 2 * PAD)
    own_down, own_up = from_tiles(sent_first, sent_next, where, 0)
    sum_low, sum_high = below_part + own_down, above_part + own_up
    even_column = where[5] == 0
    west_side[...] = jnp.where(even_column, next_beside[...], beside[...])
    east_side[...] = jnp.where(even_column, beside[...], next_beside[...])
    column, top, left, right = where[0], where[1], where[2], where[3]
    at_top = top == 1

    def comes_from(target):
        source = 0
        for s in range(sources):
            source = jnp.where(partner[s] == target, s, source)
        return source

    def turned(rows, source):
        back = COLS - 1 - iota((PAD, COLS), 1)
        return jnp.where(flip[source] == 1, jnp.take_along_axis(rows, back, axis=1), rows)

    level_lane = iota((PAD, COLS), 1)
    source = comes_from(column)
    earlier = comes_from(source)
    before = jnp.where(source == 0, sources - 1, source - 1)
    after = jnp.where(source == sources - 1, 0, source + 1)
    corner_left = west_side[24:25, :]
    corner_right = east_side[24:25, :]
    sum_low = sum_low + jnp.where(level_lane == 0, to_rows(corner_left, OFFSET[0]), 0.0)
    sum_low = sum_low + jnp.where(level_lane == COLS - 1, to_rows(corner_right, OFFSET[1]), 0.0)
    sum_high = sum_high + jnp.where(level_lane == 0, to_rows(corner_left, OFFSET[3]), 0.0)
    sum_high = sum_high + jnp.where(level_lane == COLS - 1, to_rows(corner_right, OFFSET[2]), 0.0)
    fold_first = turned(got[source, 0:PAD, :], source)
    sum_fold = got[source, LEVELS : LEVELS + PAD, :] + turned(got[earlier, 0:PAD, :], earlier)
    cross_west = to_rows(got[before, CORNER : CORNER + 1, :], OFFSET[0])
    cross_east = to_rows(got[after, CORNER : CORNER + 1, :], OFFSET[1])
    sum_fold = sum_fold + jnp.where(level_lane == 0, cross_west, 0.0) + jnp.where(level_lane == COLS - 1, cross_east, 0.0)
    fold_second = turned(turn(got[source, SLOT - PAD : SLOT, :], SLOT - PAD - 2 * LEVELS, 0) * sum_fold, source)
    lines[0:PAD, :] = jnp.where(at_top, fold_first, above_near)
    lines[PAD : 2 * PAD, :] = below_scale * sum_low
    lines[2 * PAD : 3 * PAD, :] = jnp.where(at_top, fold_second, above_scale * sum_high)
    lines[3 * PAD : 4 * PAD, :] = below_near
    from_left = comes_from(left)
    from_right = comes_from(right)
    fold_left = turned(got[from_left, 0:PAD, :], from_left)[:, COLS - 1 : COLS]
    fold_right = turned(got[from_right, 0:PAD, :], from_right)[:, 0:1]
    fold_left = jnp.where(at_top, to_lanes(fold_left, OFFSET[3]), 0.0)
    fold_right = jnp.where(at_top, to_lanes(fold_right, OFFSET[3]), 0.0)
    near_left = west_side[0:8, :]
    near_right = east_side[0:8, :]
    next_left = west_side[16:24, :] * (west_side[8:16, :] + edges[24:32, :] + spot_rows(0.0, fold_left))
    next_right = east_side[16:24, :] * (east_side[8:16, :] + edges[0:8, :] + spot_rows(0.0, fold_right))
    even = (iota((8, COLS), 1) & 1) == 0
    for ref, from_west, from_east in ((near_sides, near_left, near_right), (far_sides, next_left, next_right)):
        for g, offset in enumerate(OFFSET):
            ref[8 * g : 8 * g + 8, :] = jnp.where(even, turn(from_west, -offset), turn(from_east, -offset - 1))

    row, lane = iota((ROWS, COLS), 0), iota((ROWS, COLS), 1)

    def joined(k, r, sides, first, last):
        r = r + jnp.where((lane == 0) | (lane == COLS - 1), turn(sides[...], -2 * k), 0.0)
        r = r + jnp.where(row == 0, first, 0.0) + jnp.where(row == ROWS - 1, last, 0.0)
        return mask[k].astype(jnp.float32) * r

    for k in range(LEVELS):
        held[k] = joined(k, part[k], near_sides, lines[3 * PAD + k : 3 * PAD + k + 1, :], lines[k : k + 1, :])
    for k in range(LEVELS):
        r = terms(k, held, centre, side, vert)[0]
        out[k] = joined(k, r, far_sides, lines[PAD + k : PAD + k + 1, :], lines[2 * PAD + k : 2 * PAD + k + 1, :])


def body(adjoint_in, centre, side_coeff, vert_coeff, land_mask, obs_misfit, obs_cell, obs_count, fold_partner, fold_flip):
    sources = obs_misfit.shape[2]
    tiles = lax.axis_size("tile")
    column, tile_row = lax.axis_index("col"), lax.axis_index("tile")
    where = jnp.stack(
        [
            column,
            (tile_row == tiles - 1).astype(jnp.int32),
            jnp.where(column == 0, sources - 1, column - 1),
            jnp.where(column == sources - 1, 0, column + 1),
            tile_row & 1,
            column & 1,
        ]
    )
    received = lax.all_to_all(obs_misfit, "col", split_axis=2, concat_axis=1, tiled=True)
    f32 = jnp.float32
    tile = jax.ShapeDtypeStruct((LEVELS, ROWS, COLS), f32)
    lines = jax.ShapeDtypeStruct((LINES, COLS), f32)
    field = pltpu.VMEM((LEVELS, ROWS, COLS), f32)
    group = min(GROUP, sources)
    small = sources <= GROUP
    cells = obs_cell.reshape(sources, CAP)
    hot = pl.pallas_call(
        match_kernel,
        out_shape=jax.ShapeDtypeStruct((LEVELS * ROWS, sources * CAP), jnp.bfloat16),
        in_specs=[VMEM],
        out_specs=VMEM,
        compiler_params=pltpu.CompilerParams(vmem_limit_bytes=(4 if small else 24) * MIB),
        cost_estimate=pl.CostEstimate(flops=10**10, bytes_accessed=2 * 10**8, transcendentals=0),
        name="match_rows",
    )(cells)
    part, swap, next_swap, edges, slots = pl.pallas_call(
        functools.partial(first_kernel, sources),
        out_shape=(tile, lines, lines, jax.ShapeDtypeStruct((48, COLS), f32), jax.ShapeDtypeStruct((sources, SLOT, COLS), f32)),
        in_specs=[VMEM, VMEM, SMEM, SMEM] + [VMEM] * 6,
        out_specs=(VMEM,) * 5,
        scratch_shapes=[
            pltpu.VMEM((3 * COLS, group * CAP), jnp.bfloat16),
            pltpu.VMEM((LEVELS * ROWS, 3 * COLS), f32),
            field,
            pltpu.VMEM((LINES, COLS), f32),
            pltpu.VMEM((LINES, COLS), f32),
            pltpu.VMEM((SLOT, COLS), f32),
        ],
        compiler_params=pltpu.CompilerParams(vmem_limit_bytes=(8 if small else 40) * MIB),
        name="first_step",
    )(
        received.reshape(sources, CAP),
        cells,
        obs_count.reshape(1, sources),
        where,
        hot,
        adjoint_in,
        side_coeff,
        centre,
        vert_coeff,
        land_mask,
    )
    got = lax.all_to_all(slots, "col", split_axis=0, concat_axis=0, tiled=True)
    next_swapped = lax.ppermute(next_swap, "tile", swaps(1, tiles - 1))
    swapped = lax.ppermute(swap, "tile", swaps(0, tiles))
    edge = jax.ShapeDtypeStruct((EDGE, COLS), f32)
    beside, next_beside = pl.pallas_call(
        corner_kernel,
        out_shape=(edge, edge),
        in_specs=[VMEM, VMEM, VMEM, SMEM],
        out_specs=(VMEM, VMEM),
        compiler_params=pltpu.CompilerParams(vmem_limit_bytes=4 * MIB),
        cost_estimate=pl.CostEstimate(flops=10**6, bytes_accessed=4 * 10**6, transcendentals=0),
        name="corners",
    )(swapped, next_swapped, edges, where)
    round_trip = [(sources - 1, 0), (0, sources - 1)]
    next_beside = lax.ppermute(next_beside, "col", swaps(1, sources - 1) + round_trip)
    beside = lax.ppermute(beside, "col", swaps(0, sources))
    return pl.pallas_call(
        second_kernel,
        out_shape=tile,
        in_specs=[VMEM] * 8 + [SMEM] * 3 + [VMEM] * 5,
        out_specs=VMEM,
        scratch_shapes=[
            field,
            pltpu.VMEM((4 * PAD, COLS), f32),
            pltpu.VMEM((ROWS, COLS), f32),
            pltpu.VMEM((ROWS, COLS), f32),
            pltpu.VMEM((EDGE, COLS), f32),
            pltpu.VMEM((EDGE, COLS), f32),
        ],
        compiler_params=pltpu.CompilerParams(vmem_limit_bytes=8 * MIB),
        name="second_step",
    )(
        swapped,
        next_swapped,
        swap,
        next_swap,
        beside,
        next_beside,
        edges,
        got,
        fold_partner,
        fold_flip,
        where,
        part,
        land_mask,
        side_coeff,
        centre,
        vert_coeff,
    )


def swaps(first, end):
    return [pair for i in range(first, end - 1, 2) for pair in ((i, i + 1), (i + 1, i))]


def solution(mesh):
    in_specs = (
        P(None, "tile", "col"),
        P(None, "tile", "col"),
        P(None, None, "tile", "col"),
        P(None, None, "tile", "col"),
        P(None, "tile", "col"),
        P("tile", "col", None, None),
        P("tile", "col", None, None),
        P("tile", "col", None),
        P(),
        P(),
    )
    out_specs = P(None, "tile", "col")
    return jax.shard_map(body, mesh=mesh, in_specs=in_specs, out_specs=out_specs, check_vma=False)
```

profile of v0, /device:TPU:29, one launch (start us, length us, event | category | flops | bytes accessed | tf_op | source)
XLA Modules:
  0.0 40.8 jit_solution(3038036165827416732)
XLA Ops:
  0.0 5.4 %all-to-all-start = ((f32[1,1,8,128]{3,1,0,2:T(1,128)}), f32[1,1,8,128]{3,1,0,2:T(1,128)S(1)}, u32[]{:S(2)}, u32[]{:S(2)}) async-start(f32[1,1,8,128]{3,1,0,2:T(1,128)} %bitcast.14), calls=%async_computation | async-start | bytes 8192 | tf_op jit(solution)/shard_map/all_to_all | solution.py:264
  5.4 0.0 copy-start.12
  5.4 0.7 %copy-done.12 = s32[1,1,8,128]{3,2,1,0:T(8,128)S(1)} copy-done((s32[1,1,8,128]{3,2,1,0:T(8,128)S(1)}, s32[1,1,8,128]{3,2,1,0:T(8,128)}, u32[]{:S(2)}) %copy-start.12) | copy-done | bytes 4120
  6.1 0.0 copy-start
  6.1 0.0 copy-start.1
  6.1 0.0 copy-start.4
  6.1 0.0 copy-start.5
  6.1 0.0 copy-start.13
  6.1 0.0 copy-start.14
  6.1 0.5 %match_rows.1.hot = bf16[800,1024]{1,0:T(8,128)(2,1)S(1)} custom-call(s32[8,128]{1,0:T(8,128)S(1)} %bitcast.11), custom_call_target="tpu_custom_call" | custom-call | flops 10000000000 | bytes 200000000 | tf_op jit(solution)/shard_map/match_rows/pallas_call | solution.py:272
  6.6 0.0 copy-start.2
  6.6 1.2 %copy-done.2 = bf16[800,1024]{1,0:T(8,128)(2,1)} copy-done((bf16[800,1024]{1,0:T(8,128)(2,1)}, bf16[800,1024]{1,0:T(8,128)(2,1)S(1)}, u32[]{:S(2)}) %copy-start.2) | copy-done | bytes 1638424
  7.8 0.1 stack.31.where
  7.9 0.0 all-to-all-done
  7.9 0.0 copy-done
  7.9 0.3 copy-done.1
  8.2 0.2 copy-done.4
  8.4 0.1 copy-done.5
  8.6 0.0 copy-done.13
  8.6 0.0 copy-done.14
  8.6 0.0 copy-start.3
  8.6 1.4 %copy-done.3 = bf16[800,1024]{1,0:T(8,128)(2,1)S(1)} copy-done((bf16[800,1024]{1,0:T(8,128)(2,1)S(1)}, bf16[800,1024]{1,0:T(8,128)(2,1)}, u32[]{:S(2)}) %copy-start.3) | copy-done | bytes 1638424
  10.0 0.0 copy-start.6
  10.0 1.0 %copy-done.6 = f32[25,32,128]{2,1,0:T(8,128)S(1)} copy-done((f32[25,32,128]{2,1,0:T(8,128)S(1)}, f32[25,32,128]{2,1,0:T(8,128)}, u32[]{:S(2)}) %copy-start.6) | copy-done | bytes 409624
  11.0 0.0 copy-start.15
  11.0 0.0 copy-start.16
  11.0 2.1 %first_step.1 = (f32[25,32,128]{2,1,0:T(8,128)S(1)}, f32[128,128]{1,0:T(8,128)S(1)}, f32[128,128]{1,0:T(8,128)S(1)}, f32[48,128]{1,0:T(8,128)S(1)}, f32[8,80,128]{2,1,0:T(8,128)S(1)}) custom-call(f32[8,128]{1,0:T(8,128)S(1)} %bitcast.10, s32[8,128]{1,0:T(8,128)S(1)} %bitcast.12, s32[1,8]{1,0:T(1,128)S(1)} %bitcast.13, s32[6]{0:T(128)S(1)} %stack.31.where, ...), custom_call_target="tpu_custom_call" | custom-call | tf_op jit(solution)/shard_map/first_step/pallas_call | solution.py:281
  13.1 0.0 copy-start.7
  13.1 0.8 %copy-done.7 = f32[25,32,128]{2,1,0:T(8,128)} copy-done((f32[25,32,128]{2,1,0:T(8,128)}, f32[25,32,128]{2,1,0:T(8,128)S(1)}, u32[]{:S(2)}) %copy-start.7) | copy-done | bytes 409624
  13.9 0.0 copy-start.9
  13.9 0.7 %copy-done.9 = f32[8,80,128]{2,1,0:T(8,128)} copy-done((f32[8,80,128]{2,1,0:T(8,128)}, f32[8,80,128]{2,1,0:T(8,128)S(1)}, u32[]{:S(2)}) %copy-start.9) | copy-done | bytes 327704
  14.6 0.0 copy-start.10
  14.6 0.6 %copy-done.10 = f32[128,128]{1,0:T(8,128)} copy-done((f32[128,128]{1,0:T(8,128)}, f32[128,128]{1,0:T(8,128)S(1)}, u32[]{:S(2)}) %copy-start.10) | copy-done | bytes 65560
  15.2 6.4 %all-to-all-start.1 = ((f32[8,80,128]{2,1,0:T(8,128)}), f32[8,80,128]{2,1,0:T(8,128)}, u32[]{:S(2)}, u32[]{:S(2)}) async-start(f32[8,80,128]{2,1,0:T(8,128)} %copy-done.9), calls=%async_computation.1 | async-start | bytes 655360 | tf_op jit(solution)/shard_map/all_to_all | solution.py:308
  21.6 1.2 %collective-permute-start = (f32[128,128]{1,0:T(8,128)S(1)}, f32[128,128]{1,0:T(8,128)S(1)}, u32[]{:S(2)}, u32[]{:S(2)}) collective-permute-start(f32[128,128]{1,0:T(8,128)S(1)} %get-tuple-element.12.sent_first), channel_id=1, source_target_pairs={{0,8},{8,0},{16,24},{24,16},{1,9},{9,1},{17,25},{25,17},{2,10},{10... | collective-permute-start | bytes 196616 | tf_op jit(solution)/shard_map/ppermute | solution.py:310
  22.8 2.1 %collective-permute-start.1 = (f32[128,128]{1,0:T(8,128)}, f32[128,128]{1,0:T(8,128)S(1)}, u32[]{:S(2)}, u32[]{:S(2)}) collective-permute-start(f32[128,128]{1,0:T(8,128)} %copy-done.10), channel_id=1, source_target_pairs={{8,16},{16,8},{9,17},{17,9},{10,18},{18,10},{11,19},{19,11},{12,20... | collective-permute-start | bytes 196616 | tf_op jit(solution)/shard_map/ppermute | solution.py:309
  24.9 0.2 collective-permute-done.swapped
  25.1 3.8 %collective-permute-done.1.next_swapped = f32[128,128]{1,0:T(8,128)S(1)} collective-permute-done((f32[128,128]{1,0:T(8,128)}, f32[128,128]{1,0:T(8,128)S(1)}, u32[]{:S(2)}, u32[]{:S(2)}) %collective-permute-start.1) | collective-permute-done | bytes 65568 | tf_op jit(solution)/shard_map/ppermute | solution.py:309
  28.9 0.7 %corners.1 = (f32[32,128]{1,0:T(8,128)S(1)}, f32[32,128]{1,0:T(8,128)S(1)}) custom-call(f32[128,128]{1,0:T(8,128)S(1)} %collective-permute-done.swapped, f32[128,128]{1,0:T(8,128)S(1)} %collective-permute-done.1.next_swapped, f32[48,128]{1,0:T(8,128)S(1)} %get-tuple-element.14.edges, s32[6]{0:T(128)S(1)} %stack.31.where), custom_call_target="tpu_custom_call" | custom-call | flops 1000000 | bytes 4000000 | tf_op jit(solution)/shard_map/corners/pallas_call | solution.py:312
  29.6 1.9 %collective-permute-start.2 = (f32[32,128]{1,0:T(8,128)S(1)}, f32[32,128]{1,0:T(8,128)S(1)}, u32[]{:S(2)}, u32[]{:S(2)}) collective-permute-start(f32[32,128]{1,0:T(8,128)S(1)} %get-tuple-element.15), channel_id=1, source_target_pairs={{0,1},{1,0},{2,3},{3,2},{4,5},{5,4},{6,7},{7,6},{8,9},{9,8},{10,11... | collective-permute-start | bytes 49160 | tf_op jit(solution)/shard_map/ppermute | solution.py:323
  31.4 0.0 collective-permute-start.3
  31.4 0.8 %collective-permute-done.2.beside = f32[32,128]{1,0:T(8,128)S(1)} collective-permute-done((f32[32,128]{1,0:T(8,128)S(1)}, f32[32,128]{1,0:T(8,128)S(1)}, u32[]{:S(2)}, u32[]{:S(2)}) %collective-permute-start.2) | collective-permute-done | bytes 16416 | tf_op jit(solution)/shard_map/ppermute | solution.py:323
  32.3 4.1 %collective-permute-done.3.next_beside = f32[32,128]{1,0:T(8,128)S(1)} collective-permute-done((f32[32,128]{1,0:T(8,128)S(1)}, f32[32,128]{1,0:T(8,128)S(1)}, u32[]{:S(2)}, u32[]{:S(2)}) %collective-permute-start.3) | collective-permute-done | bytes 16416 | tf_op jit(solution)/shard_map/ppermute | solution.py:322
  36.4 0.0 all-to-all-done.1.got
  36.4 0.0 copy-done.15
  36.4 0.0 copy-done.16
  36.4 0.0 copy-start.8
  36.4 1.0 %copy-done.8 = f32[25,32,128]{2,1,0:T(8,128)S(1)} copy-done((f32[25,32,128]{2,1,0:T(8,128)S(1)}, f32[25,32,128]{2,1,0:T(8,128)}, u32[]{:S(2)}) %copy-start.8) | copy-done | bytes 409624
  37.4 0.0 copy-start.11
  37.4 0.8 %copy-done.11 = f32[128,128]{1,0:T(8,128)S(1)} copy-done((f32[128,128]{1,0:T(8,128)S(1)}, f32[128,128]{1,0:T(8,128)}, u32[]{:S(2)}) %copy-start.11) | copy-done | bytes 65560
  38.3 2.5 %second_step.1 = f32[25,32,128]{2,1,0:T(8,128)} custom-call(f32[128,128]{1,0:T(8,128)S(1)} %collective-permute-done.swapped, f32[128,128]{1,0:T(8,128)S(1)} %collective-permute-done.1.next_swapped, f32[128,128]{1,0:T(8,128)S(1)} %get-tuple-element.12.sent_first, f32[128,128]{1,0:T(8,128)S(1)} %copy-done.11, f32[32,128]{1,0:T(8,128)S(1)} %collective-permute-done.2.beside, ...), custom_call_target="tpu_custom_call" | custom-call | tf_op jit(solution)/shard_map/second_step/pallas_call | solution.py:324
Async XLA Ops:
  0.0 7.9 %all-to-all-start = ((f32[1,1,8,128]{3,1,0,2:T(1,128)}), f32[1,1,8,128]{3,1,0,2:T(1,128)S(1)}, u32[]{:S(2)}, u32[]{:S(2)}) async-start(f32[1,1,8,128]{3,1,0,2:T(1,128)} %bitcast.14), calls=%async_computation | async-start | bytes 8192 | tf_op jit(solution)/shard_map/all_to_all | solution.py:264
  5.4 0.7 %copy-start.12 = (s32[1,1,8,128]{3,2,1,0:T(8,128)S(1)}, s32[1,1,8,128]{3,2,1,0:T(8,128)}, u32[]{:S(2)}) copy-start(s32[1,1,8,128]{3,2,1,0:T(8,128)} %param.16) | copy-start | bytes 12292
  6.1 1.8 %copy-start = (f32[4,25,32,128]{3,2,1,0:T(8,128)S(1)}, f32[4,25,32,128]{3,2,1,0:T(8,128)}, u32[]{:S(2)}) copy-start(f32[4,25,32,128]{3,2,1,0:T(8,128)} %side.3) | copy-start | bytes 4915204
  6.1 2.1 %copy-start.1 = (f32[2,25,32,128]{3,2,1,0:T(8,128)S(1)}, f32[2,25,32,128]{3,2,1,0:T(8,128)}, u32[]{:S(2)}) copy-start(f32[2,25,32,128]{3,2,1,0:T(8,128)} %vert.3) | copy-start | bytes 2457604
  6.1 2.3 %copy-start.4 = (f32[25,32,128]{2,1,0:T(8,128)S(1)}, f32[25,32,128]{2,1,0:T(8,128)}, u32[]{:S(2)}) copy-start(f32[25,32,128]{2,1,0:T(8,128)} %centre.3) | copy-start | bytes 1228804
  6.1 2.4 %copy-start.5 = (s32[25,32,128]{2,1,0:T(8,128)S(1)}, s32[25,32,128]{2,1,0:T(8,128)}, u32[]{:S(2)}) copy-start(s32[25,32,128]{2,1,0:T(8,128)} %mask.3) | copy-start | bytes 1228804
  6.1 2.4 %copy-start.13 = (s32[1,1,8,128]{3,2,1,0:T(8,128)S(1)}, s32[1,1,8,128]{3,2,1,0:T(8,128)}, u32[]{:S(2)}) copy-start(s32[1,1,8,128]{3,2,1,0:T(8,128)} %param.16) | copy-start | bytes 12292
  6.1 2.4 %copy-start.14 = (s32[1,1,8]{2,1,0:T(1,128)S(1)}, s32[1,1,8]{2,1,0:T(1,128)}, u32[]{:S(2)}) copy-start(s32[1,1,8]{2,1,0:T(1,128)} %param.17) | copy-start | bytes 100
  6.6 1.2 %copy-start.2 = (bf16[800,1024]{1,0:T(8,128)(2,1)}, bf16[800,1024]{1,0:T(8,128)(2,1)S(1)}, u32[]{:S(2)}) copy-start(bf16[800,1024]{1,0:T(8,128)(2,1)S(1)} %match_rows.1.hot) | copy-start | bytes 4915204
  8.6 1.4 %copy-start.3 = (bf16[800,1024]{1,0:T(8,128)(2,1)S(1)}, bf16[800,1024]{1,0:T(8,128)(2,1)}, u32[]{:S(2)}) copy-start(bf16[800,1024]{1,0:T(8,128)(2,1)} %copy-done.2) | copy-start | bytes 4915204
  10.0 1.0 %copy-start.6 = (f32[25,32,128]{2,1,0:T(8,128)S(1)}, f32[25,32,128]{2,1,0:T(8,128)}, u32[]{:S(2)}) copy-start(f32[25,32,128]{2,1,0:T(8,128)} %adjoint.1) | copy-start | bytes 1228804
  11.0 25.4 %copy-start.15 = (s32[8]{0:T(128)S(1)}, s32[8]{0:T(128)}, u32[]{:S(2)}) copy-start(s32[8]{0:T(128)} %partner.1) | copy-start | bytes 100
  11.0 25.4 %copy-start.16 = (s32[8]{0:T(128)S(1)}, s32[8]{0:T(128)}, u32[]{:S(2)}) copy-start(s32[8]{0:T(128)} %flip.1) | copy-start | bytes 100
  13.1 0.8 %copy-start.7 = (f32[25,32,128]{2,1,0:T(8,128)}, f32[25,32,128]{2,1,0:T(8,128)S(1)}, u32[]{:S(2)}) copy-start(f32[25,32,128]{2,1,0:T(8,128)S(1)} %get-tuple-element.18.part) | copy-start | bytes 1228804
  13.9 0.7 %copy-start.9 = (f32[8,80,128]{2,1,0:T(8,128)}, f32[8,80,128]{2,1,0:T(8,128)S(1)}, u32[]{:S(2)}) copy-start(f32[8,80,128]{2,1,0:T(8,128)S(1)} %get-tuple-element.17) | copy-start | bytes 983044
  14.6 0.6 %copy-start.10 = (f32[128,128]{1,0:T(8,128)}, f32[128,128]{1,0:T(8,128)S(1)}, u32[]{:S(2)}) copy-start(f32[128,128]{1,0:T(8,128)S(1)} %get-tuple-element.13.sent_next) | copy-start | bytes 196612
  15.2 21.2 %all-to-all-start.1 = ((f32[8,80,128]{2,1,0:T(8,128)}), f32[8,80,128]{2,1,0:T(8,128)}, u32[]{:S(2)}, u32[]{:S(2)}) async-start(f32[8,80,128]{2,1,0:T(8,128)} %copy-done.9), calls=%async_computation.1 | async-start | bytes 655360 | tf_op jit(solution)/shard_map/all_to_all | solution.py:308
  21.6 3.5 %collective-permute-start = (f32[128,128]{1,0:T(8,128)S(1)}, f32[128,128]{1,0:T(8,128)S(1)}, u32[]{:S(2)}, u32[]{:S(2)}) collective-permute-start(f32[128,128]{1,0:T(8,128)S(1)} %get-tuple-element.12.sent_first), channel_id=1, source_target_pairs={{0,8},{8,0},{16,24},{24,16},{1,9},{9,1},{17,25},{25,17},{2,10},{10... | collective-permute-start | bytes 196616 | tf_op jit(solution)/shard_map/ppermute | solution.py:310
  22.8 6.1 %collective-permute-start.1 = (f32[128,128]{1,0:T(8,128)}, f32[128,128]{1,0:T(8,128)S(1)}, u32[]{:S(2)}, u32[]{:S(2)}) collective-permute-start(f32[128,128]{1,0:T(8,128)} %copy-done.10), channel_id=1, source_target_pairs={{8,16},{16,8},{9,17},{17,9},{10,18},{18,10},{11,19},{19,11},{12,20... | collective-permute-start | bytes 196616 | tf_op jit(solution)/shard_map/ppermute | solution.py:309
  29.6 2.7 %collective-permute-start.2 = (f32[32,128]{1,0:T(8,128)S(1)}, f32[32,128]{1,0:T(8,128)S(1)}, u32[]{:S(2)}, u32[]{:S(2)}) collective-permute-start(f32[32,128]{1,0:T(8,128)S(1)} %get-tuple-element.15), channel_id=1, source_target_pairs={{0,1},{1,0},{2,3},{3,2},{4,5},{5,4},{6,7},{7,6},{8,9},{9,8},{10,11... | collective-permute-start | bytes 49160 | tf_op jit(solution)/shard_map/ppermute | solution.py:323
  31.4 5.0 %collective-permute-start.3 = (f32[32,128]{1,0:T(8,128)S(1)}, f32[32,128]{1,0:T(8,128)S(1)}, u32[]{:S(2)}, u32[]{:S(2)}) collective-permute-start(f32[32,128]{1,0:T(8,128)S(1)} %get-tuple-element.16), channel_id=1, source_target_pairs={{1,2},{2,1},{3,4},{4,3},{5,6},{6,5},{7,0},{0,7},{9,10},{10,9},{11,... | collective-permute-start | bytes 49160 | tf_op jit(solution)/shard_map/ppermute | solution.py:322
  36.4 1.0 %copy-start.8 = (f32[25,32,128]{2,1,0:T(8,128)S(1)}, f32[25,32,128]{2,1,0:T(8,128)}, u32[]{:S(2)}) copy-start(f32[25,32,128]{2,1,0:T(8,128)} %copy-done.7) | copy-start | bytes 1228804
  37.4 0.8 %copy-start.11 = (f32[128,128]{1,0:T(8,128)S(1)}, f32[128,128]{1,0:T(8,128)}, u32[]{:S(2)}) copy-start(f32[128,128]{1,0:T(8,128)} %copy-done.10) | copy-start | bytes 196612
where the time goes:
time: 41.2 us; the launch traced here: 40.8 us
  starting transfers between devices  16.9 us (41%)
  local copies, waits for them, and re-layouts  8.99 us (22%)
  waiting for transfers between devices  8.97 us (22%)
  Pallas kernels  5.78 us (14%)
    unnamed x34, local copies, waits for them, and re-layouts  8.91 us
    all_to_all x1, starting transfers between devices, body(): got = lax.all_to_all(slots, 'col', split_axis=0, concat_axis=0, tiled=True)  6.36 us
    all_to_all x1, starting transfers between devices, body(): lax.all_to_all(obs_misfit, 'col', split_axis=2, concat_axis=1, tiled=True)  5.41 us
    ppermute x1, waiting for transfers between devices, body(): lax.ppermute(next_beside, 'col', swaps(1, sources - 1) + round_trip)  4.12 us
    ppermute x1, waiting for transfers between devices, body(): next_swapped = lax.ppermute(next_swap, 'tile', swaps(1, tiles - 1))  3.8 us
    pallas_call x1, Pallas kernels, body(): pl.pallas_call(second_kernel, out_shape=tile, in_specs=[VMEM] * 8 + [SMEM...  2.51 us
    pallas_call x1, Pallas kernels, body(): pl.pallas_call(functools.partial(first_kernel, sources), out_shape=(tile,...  2.13 us
    ppermute x1, starting transfers between devices, body(): next_swapped = lax.ppermute(next_swap, 'tile', swaps(1, tiles - 1))  2.09 us
  transfers between devices with their start and end apart: 6, of which 4 were waited for; matrix products, arithmetic and copies ran while one was open for 0% of the time, Pallas kernels for 3%

commit v1 on v0

--- a/solution.py
+++ b/solution.py
@@ -18,6 +18,8 @@
 SLOT = 80
 EDGE = 32
 OFFSET = (0, 50, 1, 51)
+EDGES = 48 + 2 * PAD
+LAND = 1e38
 MIB = 1024 * 1024
 VMEM = pl.BlockSpec(memory_space=pltpu.VMEM)
 SMEM = pl.BlockSpec(memory_space=pltpu.SMEM)
@@ -51,15 +53,30 @@
     return jnp.where(lane == COLS - 1, last, jnp.where(lane == 0, first, 0.0))
 
 
-def match_kernel(cell, hot):
-    for s in range(cell.shape[0]):
-        place = cell[s : s + 1, :] >> 7
-        for k in range(LEVELS):
-            match = (iota((ROWS, CAP), 0) + k * ROWS) == place
-            hot[k * ROWS : (k + 1) * ROWS, s * CAP : (s + 1) * CAP] = jnp.where(match, 1.0, 0.0).astype(jnp.bfloat16)
-
-
-def one_hot(sources, misfit, cell, count, hot, valued, forcing):
+def scale_kernel(side, mask, scales):
+    lane = iota((ROWS, COLS), 1)
+    packed = jnp.zeros((ROWS, COLS), jnp.float32)
+    for at in (16, 16 + PAD):
+        scales[at + 24 : at + PAD, :] = jnp.zeros((8, COLS), jnp.float32)
+    for k in range(LEVELS):
+        m = mask[k].astype(jnp.float32)
+        packed = packed + turn(m * outer(lane, side[0, k], side[1, k]), 2 * k + 1)
+        scales[16 + k : 17 + k, :] = (m * side[2, k])[ROWS - 1 : ROWS]
+        scales[16 + PAD + k : 17 + PAD + k, :] = (m * side[3, k])[0:1]
+    scales[0:8, :], scales[8:16, :] = tight(packed)
+
+
+def tight(packed):
+    even = (iota((8, COLS), 1) & 1) == 0
+    eastward = westward = jnp.zeros((8, COLS), jnp.float32)
+    for g, offset in enumerate(OFFSET):
+        rows = packed[8 * g : 8 * g + 8]
+        eastward = eastward + turn(jnp.where(even, rows, 0.0), offset)
+        westward = westward + turn(jnp.where(even, 0.0, rows), offset - 1)
+    return eastward, westward
+
+
+def forcing_kernel(sources, misfit, cell, count, forcing, hot, valued):
     group = min(GROUP, sources)
     lane = iota((1, CAP), 1)
     for first in range(0, sources, group):
@@ -73,8 +90,12 @@
             column = iota((COLS, CAP), 0) == (cells & (COLS - 1))
             for i, part in enumerate((high, middle, low)):
                 valued[i * COLS : (i + 1) * COLS, at] = jnp.where(column, part, 0.0).astype(jnp.bfloat16)
-        matched = hot[:, first * CAP : (first + group) * CAP]
-        part = lax.dot_general(matched, valued[...], (((1,), (1,)), ((), ())), preferred_element_type=jnp.float32)
+            place = cells >> 7
+            for k in range(LEVELS):
+                match = (iota((ROWS, CAP), 0) + k * ROWS) == place
+                hot[k * ROWS : (k + 1) * ROWS, at] = jnp.where(match, 1.0, 0.0).astype(jnp.bfloat16)
+        part = lax.dot_general(hot[...], valued[...], (((1,), (1,)), ((), ())), preferred_element_type=jnp.float32)
+        part = part[:, 0:COLS] + part[:, COLS : 2 * COLS] + part[:, 2 * COLS : 3 * COLS]
         if first == 0:
             forcing[...] = part
         else:
@@ -111,48 +132,41 @@
     )
 
 
-def first_kernel(sources, misfit, cell, count, where, hot, adjoint, side, centre, vert, mask, part, swap, next_swap, edges, slots, valued, forcing, held, up, down, base):
-    one_hot(sources, misfit, cell, count, hot, valued, forcing)
+def first_kernel(forcing, where, scales, adjoint, side, centre, vert, mask, part, swap, next_swap, edges, slots, held, up, down, base):
     for i in range(4):
         for ref in (up, down):
             ref[i * PAD + 24 : (i + 1) * PAD, :] = jnp.zeros((8, COLS), jnp.float32)
     for k in range(LEVELS):
-        rows = slice(k * ROWS, (k + 1) * ROWS)
-        f = forcing[rows, 0:COLS] + forcing[rows, COLS : 2 * COLS] + forcing[rows, 2 * COLS : 3 * COLS]
-        held[k] = adjoint[k] + f
+        held[k] = adjoint[k] + forcing[k * ROWS : (k + 1) * ROWS, :]
     lane = iota((ROWS, COLS), 1)
-    packed = [jnp.zeros((ROWS, COLS), jnp.float32)] * 3
+    packed = [jnp.zeros((ROWS, COLS), jnp.float32)] * 2
     for k in range(LEVELS):
         r, east, west, north, south = terms(k, held, centre, side, vert)
-        m = mask[k].astype(jnp.float32)
-        part[k] = r
+        part[k] = jnp.where(mask[k] == 0, LAND, r)
         sides = outer(lane, east, west)
-        for ref, leaving, at, which, i in ((up, north[0:1], ROWS - 1, 2, 0), (down, south[ROWS - 1 : ROWS], 0, 3, 1)):
+        for ref, leaving, at in ((up, north[0:1], ROWS - 1), (down, south[ROWS - 1 : ROWS], 0)):
             ref[k : k + 1, :] = leaving
             ref[PAD + k : PAD + k + 1, :] = r[at : at + 1]
-            ref[2 * PAD + k : 2 * PAD + k + 1, :] = (m * side[which, k])[at : at + 1]
             ref[3 * PAD + k : 3 * PAD + k + 1, :] = sides[at : at + 1]
-        fields = (sides, outer(lane, r, r), m * outer(lane, side[0, k], side[1, k]))
-        packed = [p + turn(x, 2 * k + 1) for p, x in zip(packed, fields)]
+        packed = [p + turn(x, 2 * k + 1) for p, x in zip(packed, (sides, outer(lane, r, r)))]
+    up[2 * PAD : 3 * PAD, :] = scales[16 : 16 + PAD, :]
+    down[2 * PAD : 3 * PAD, :] = scales[16 + PAD : 16 + 2 * PAD, :]
     for i in range(3):
         base[i * LEVELS : (i + 1) * LEVELS, :] = up[i * PAD : i * PAD + LEVELS, :]
     own_east, own_west = ends(up[3 * PAD : 4 * PAD, :])
     base[CORNER : CORNER + 1, :] = to_lanes(own_east, OFFSET[0]) + to_lanes(own_west, OFFSET[1])
     base[CORNER + 1 : SLOT, :] = jnp.zeros((SLOT - CORNER - 1, COLS), jnp.float32)
-    for s in range(sources):
+    for s in range(slots.shape[0]):
         slots[s] = base[...]
     upward = where[4] == 0
     swap[...] = jnp.where(upward, up[...], down[...])
     next_swap[...] = jnp.where(upward, down[...], up[...])
-    even = (iota((8, COLS), 1) & 1) == 0
     for i, p in enumerate(packed):
-        eastward = westward = jnp.zeros((8, COLS), jnp.float32)
-        for g, offset in enumerate(OFFSET):
-            rows = p[8 * g : 8 * g + 8]
-            eastward = eastward + turn(jnp.where(even, rows, 0.0), offset)
-            westward = westward + turn(jnp.where(even, 0.0, rows), offset - 1)
-        edges[8 * i : 8 * i + 8, :] = eastward
-        edges[24 + 8 * i : 32 + 8 * i, :] = westward
+        edges[8 * i : 8 * i + 8, :], edges[24 + 8 * i : 32 + 8 * i, :] = tight(p)
+    edges[16:24, :] = scales[0:8, :]
+    edges[40:48, :] = scales[8:16, :]
+    edges[48 : 48 + PAD, :] = down[0:PAD, :]
+    edges[48 + PAD : EDGES, :] = up[0:PAD, :]
 
 
 def corner_kernel(swapped, next_swapped, edges, where, swap, next_swap):
@@ -174,13 +188,13 @@
         ref[24:EDGE, :] = jnp.where(iota((EDGE - 24, COLS), 0) == 0, corners, 0.0)
 
 
-def second_kernel(swapped, next_swapped, sent_first, sent_next, beside, next_beside, edges, got, partner, flip, where, part, mask, side, centre, vert, out, held, lines, near_sides, far_sides, west_side, east_side):
+def second_kernel(swapped, next_swapped, beside, next_beside, edges, got, partner, flip, where, part, side, centre, vert, out, held, lines, near_sides, far_sides, west_side, east_side):
     sources = got.shape[0]
     below_near, above_near = from_tiles(swapped, next_swapped, where, 0)
     below_part, above_part = from_tiles(swapped, next_swapped, where, PAD)
     below_scale, above_scale = from_tiles(swapped, next_swapped, where, 2 * PAD)
-    own_down, own_up = from_tiles(sent_first, sent_next, where, 0)
-    sum_low, sum_high = below_part + own_down, above_part + own_up
+    sum_low = below_part + edges[48 : 48 + PAD, :]
+    sum_high = above_part + edges[48 + PAD : EDGES, :]
     even_column = where[5] == 0
     west_side[...] = jnp.where(even_column, next_beside[...], beside[...])
     east_side[...] = jnp.where(even_column, beside[...], next_beside[...])
@@ -238,7 +252,7 @@
     def joined(k, r, sides, first, last):
         r = r + jnp.where((lane == 0) | (lane == COLS - 1), turn(sides[...], -2 * k), 0.0)
         r = r + jnp.where(row == 0, first, 0.0) + jnp.where(row == ROWS - 1, last, 0.0)
-        return mask[k].astype(jnp.float32) * r
+        return jnp.where(part[k] == LAND, 0.0, r)
 
     for k in range(LEVELS):
         held[k] = joined(k, part[k], near_sides, lines[3 * PAD + k : 3 * PAD + k + 1, :], lines[k : k + 1, :])
@@ -268,43 +282,43 @@
     field = pltpu.VMEM((LEVELS, ROWS, COLS), f32)
     group = min(GROUP, sources)
     small = sources <= GROUP
-    cells = obs_cell.reshape(sources, CAP)
-    hot = pl.pallas_call(
-        match_kernel,
-        out_shape=jax.ShapeDtypeStruct((LEVELS * ROWS, sources * CAP), jnp.bfloat16),
-        in_specs=[VMEM],
+    ahead = pl.CostEstimate(flops=10**10, bytes_accessed=2 * 10**8, transcendentals=0)
+    scales = pl.pallas_call(
+        scale_kernel,
+        out_shape=jax.ShapeDtypeStruct((16 + 2 * PAD, COLS), f32),
+        in_specs=[VMEM, VMEM],
         out_specs=VMEM,
-        compiler_params=pltpu.CompilerParams(vmem_limit_bytes=(4 if small else 24) * MIB),
-        cost_estimate=pl.CostEstimate(flops=10**10, bytes_accessed=2 * 10**8, transcendentals=0),
-        name="match_rows",
-    )(cells)
+        compiler_params=pltpu.CompilerParams(vmem_limit_bytes=4 * MIB),
+        cost_estimate=ahead,
+        name="edge_scales",
+    )(side_coeff, land_mask)
+    forcing = pl.pallas_call(
+        functools.partial(forcing_kernel, sources),
+        out_shape=jax.ShapeDtypeStruct((LEVELS * ROWS, COLS), f32),
+        in_specs=[VMEM, VMEM, SMEM],
+        out_specs=VMEM,
+        scratch_shapes=[
+            pltpu.VMEM((LEVELS * ROWS, group * CAP), jnp.bfloat16),
+            pltpu.VMEM((3 * COLS, group * CAP), jnp.bfloat16),
+        ],
+        compiler_params=pltpu.CompilerParams(vmem_limit_bytes=(8 if small else 24) * MIB),
+        cost_estimate=pl.CostEstimate(flops=10**8, bytes_accessed=4 * 10**6, transcendentals=0),
+        name="forcing",
+    )(received.reshape(sources, CAP), obs_cell.reshape(sources, CAP), obs_count.reshape(1, sources))
     part, swap, next_swap, edges, slots = pl.pallas_call(
-        functools.partial(first_kernel, sources),
-        out_shape=(tile, lines, lines, jax.ShapeDtypeStruct((48, COLS), f32), jax.ShapeDtypeStruct((sources, SLOT, COLS), f32)),
-        in_specs=[VMEM, VMEM, SMEM, SMEM] + [VMEM] * 6,
+        first_kernel,
+        out_shape=(tile, lines, lines, jax.ShapeDtypeStruct((EDGES, COLS), f32), jax.ShapeDtypeStruct((sources, SLOT, COLS), f32)),
+        in_specs=[VMEM, SMEM] + [VMEM] * 6,
         out_specs=(VMEM,) * 5,
         scratch_shapes=[
-            pltpu.VMEM((3 * COLS, group * CAP), jnp.bfloat16),
-            pltpu.VMEM((LEVELS * ROWS, 3 * COLS), f32),
             field,
             pltpu.VMEM((LINES, COLS), f32),
             pltpu.VMEM((LINES, COLS), f32),
             pltpu.VMEM((SLOT, COLS), f32),
         ],
-        compiler_params=pltpu.CompilerParams(vmem_limit_bytes=(8 if small else 40) * MIB),
+        compiler_params=pltpu.CompilerParams(vmem_limit_bytes=(8 if small else 24) * MIB),
         name="first_step",
-    )(
-        received.reshape(sources, CAP),
-        cells,
-        obs_count.reshape(1, sources),
-        where,
-        hot,
-        adjoint_in,
-        side_coeff,
-        centre,
-        vert_coeff,
-        land_mask,
-    )
+    )(forcing, where, scales, adjoint_in, side_coeff, centre, vert_coeff, land_mask)
     got = lax.all_to_all(slots, "col", split_axis=0, concat_axis=0, tiled=True)
     next_swapped = lax.ppermute(next_swap, "tile", swaps(1, tiles - 1))
     swapped = lax.ppermute(swap, "tile", swaps(0, tiles))
@@ -324,7 +338,7 @@
     return pl.pallas_call(
         second_kernel,
         out_shape=tile,
-        in_specs=[VMEM] * 8 + [SMEM] * 3 + [VMEM] * 5,
+        in_specs=[VMEM] * 6 + [SMEM] * 3 + [VMEM] * 4,
         out_specs=VMEM,
         scratch_shapes=[
             field,
@@ -339,8 +353,6 @@
     )(
         swapped,
         next_swapped,
-        swap,
-        next_swap,
         beside,
         next_beside,
         edges,
@@ -349,7 +361,6 @@
         fold_flip,
         where,
         part,
-        land_mask,
         side_coeff,
         centre,
         vert_coeff,

time: 41.2 us -> 39.4 us (0.956)
  local copies, waits for them, and re-layouts: 8.99 us -> 6.96 us
  Pallas kernels: 5.78 us -> 6.79 us
  starting transfers between devices: 16.9 us -> 16.3 us
    unnamed x34 -> x30, local copies, waits for them, and re-layouts: 8.91 us -> 6.88 us
    pallas_call x3 -> x4, Pallas kernels: 5.12 us -> 6.13 us  [the longest x1 2.12 us: body(): pl.pallas_call(first_kernel, out_shape=(tile, lines, lines, jax.ShapeDtyp...]
    all_to_all x1, starting transfers between devices: 6.36 us -> 5.74 us  [body(): got = lax.all_to_all(slots, 'col', split_axis=0, concat_axis=0, tiled=True)]
  transfers between devices with their start and end apart: 6 -> 6, of which waited for: 4 -> 4; matrix products, arithmetic and copies ran while one was open for 0% -> 0% of each run, Pallas kernels for 3% -> 2%
where the time goes in v1:
time: 39.4 us; the launch traced here: 38.9 us
  starting transfers between devices  16.3 us (41%)
  waiting for transfers between devices  8.76 us (22%)
  local copies, waits for them, and re-layouts  6.96 us (18%)
  Pallas kernels  6.79 us (17%)
    unnamed x30, local copies, waits for them, and re-layouts  6.88 us
    all_to_all x1, starting transfers between devices, body(): got = lax.all_to_all(slots, 'col', split_axis=0, concat_axis=0, tiled=True)  5.74 us
    all_to_all x1, starting transfers between devices, body(): lax.all_to_all(obs_misfit, 'col', split_axis=2, concat_axis=1, tiled=True)  5.41 us
    ppermute x1, waiting for transfers between devices, body(): lax.ppermute(next_beside, 'col', swaps(1, sources - 1) + round_trip)  4.12 us
    ppermute x1, waiting for transfers between devices, body(): next_swapped = lax.ppermute(next_swap, 'tile', swaps(1, tiles - 1))  3.48 us
    pallas_call x1, Pallas kernels, body(): pl.pallas_call(first_kernel, out_shape=(tile, lines, lines, jax.ShapeDtyp...  2.12 us
    ppermute x1, starting transfers between devices, body(): next_swapped = lax.ppermute(next_swap, 'tile', swaps(1, tiles - 1))  2.1 us
    pallas_call x1, Pallas kernels, body(): pl.pallas_call(second_kernel, out_shape=tile, in_specs=[VMEM] * 6 + [SMEM...  2.06 us
  transfers between devices with their start and end apart: 6, of which 4 were waited for; matrix products, arithmetic and copies ran while one was open for 0% of the time, Pallas kernels for 2%

profile of v1, /device:TPU:29, one launch (start us, length us, event | category | flops | bytes accessed | tf_op | source)
XLA Modules:
  0.0 38.9 jit_solution(2827520954822020660)
XLA Ops:
  0.0 5.4 %all-to-all-start = ((f32[1,1,8,128]{3,1,0,2:T(1,128)}), f32[1,1,8,128]{3,1,0,2:T(1,128)S(1)}, u32[]{:S(2)}, u32[]{:S(2)}) async-start(f32[1,1,8,128]{3,1,0,2:T(1,128)} %bitcast.13), calls=%async_computation | async-start | bytes 8192 | tf_op jit(solution)/shard_map/all_to_all | solution.py:278
  5.4 0.0 copy-start
  5.4 1.4 %copy-done = f32[4,25,32,128]{3,2,1,0:T(8,128)S(1)} copy-done((f32[4,25,32,128]{3,2,1,0:T(8,128)S(1)}, f32[4,25,32,128]{3,2,1,0:T(8,128)}, u32[]{:S(2)}) %copy-start) | copy-done | bytes 1638424
  6.8 0.0 copy-start.4
  6.8 1.0 %copy-done.4 = s32[25,32,128]{2,1,0:T(8,128)S(1)} copy-done((s32[25,32,128]{2,1,0:T(8,128)S(1)}, s32[25,32,128]{2,1,0:T(8,128)}, u32[]{:S(2)}) %copy-start.4) | copy-done | bytes 409624
  7.8 0.0 copy-start.10
  7.8 0.0 copy-start.11
  7.9 0.0 copy-start.1
  7.9 0.0 copy-start.2
  7.9 0.0 copy-start.3
  7.9 0.0 copy-start.5
  7.9 0.2 edge_scales.1.scales
  8.1 0.1 stack.31.where
  8.2 0.0 all-to-all-done
  8.2 0.3 copy-done.10
  8.5 0.0 copy-done.11
  8.5 1.7 %forcing.1 = f32[800,128]{1,0:T(8,128)S(1)} custom-call(f32[8,128]{1,0:T(8,128)S(1)} %bitcast.10, s32[8,128]{1,0:T(8,128)S(1)} %bitcast.11, s32[1,8]{1,0:T(1,128)S(1)} %bitcast.12), custom_call_target="tpu_custom_call" | custom-call | flops 100000000 | bytes 4000000 | tf_op jit(solution)/shard_map/forcing/pallas_call | solution.py:295
  10.2 0.0 copy-done.1
  10.3 0.0 copy-done.2
  10.3 0.0 copy-done.3
  10.3 0.0 copy-done.5
  10.3 0.0 copy-start.6
  10.3 1.0 %copy-done.6 = f32[25,32,128]{2,1,0:T(8,128)S(1)} copy-done((f32[25,32,128]{2,1,0:T(8,128)S(1)}, f32[25,32,128]{2,1,0:T(8,128)}, u32[]{:S(2)}) %copy-start.6) | copy-done | bytes 409624
  11.3 0.0 copy-start.12
  11.3 0.0 copy-start.13
  11.3 2.1 %first_step.1 = (f32[25,32,128]{2,1,0:T(8,128)S(1)}, f32[128,128]{1,0:T(8,128)S(1)}, f32[128,128]{1,0:T(8,128)S(1)}, f32[112,128]{1,0:T(8,128)S(1)}, f32[8,80,128]{2,1,0:T(8,128)S(1)}) custom-call(f32[800,128]{1,0:T(8,128)S(1)} %forcing.1, s32[6]{0:T(128)S(1)} %stack.31.where, f32[80,128]{1,0:T(8,128)S(1)} %edge_scales.1.scales, ...), custom_call_target="tpu_custom_call" | custom-call | tf_op jit(solution)/shard_map/first_step/pallas_call | solution.py:308
  13.4 0.0 copy-start.7
  13.4 0.7 %copy-done.7 = f32[25,32,128]{2,1,0:T(8,128)} copy-done((f32[25,32,128]{2,1,0:T(8,128)}, f32[25,32,128]{2,1,0:T(8,128)S(1)}, u32[]{:S(2)}) %copy-start.7) | copy-done | bytes 409624
  14.2 0.0 copy-start.9
  14.2 0.7 %copy-done.9 = f32[8,80,128]{2,1,0:T(8,128)} copy-done((f32[8,80,128]{2,1,0:T(8,128)}, f32[8,80,128]{2,1,0:T(8,128)S(1)}, u32[]{:S(2)}) %copy-start.9) | copy-done | bytes 327704
  14.9 0.0 copy-start.14
  14.9 0.6 %copy-done.14 = f32[128,128]{1,0:T(8,128)} copy-done((f32[128,128]{1,0:T(8,128)}, f32[128,128]{1,0:T(8,128)S(1)}, u32[]{:S(2)}) %copy-start.14) | copy-done | bytes 65560
  15.5 5.7 %all-to-all-start.1 = ((f32[8,80,128]{2,1,0:T(8,128)}), f32[8,80,128]{2,1,0:T(8,128)S(1)}, u32[]{:S(2)}, u32[]{:S(2)}) async-start(f32[8,80,128]{2,1,0:T(8,128)} %copy-done.9), calls=%async_computation.1 | async-start | bytes 655360 | tf_op jit(solution)/shard_map/all_to_all | solution.py:322
  21.3 1.2 %collective-permute-start = (f32[128,128]{1,0:T(8,128)}, f32[128,128]{1,0:T(8,128)S(1)}, u32[]{:S(2)}, u32[]{:S(2)}) collective-permute-start(f32[128,128]{1,0:T(8,128)} %copy-done.14), channel_id=1, source_target_pairs={{0,8},{8,0},{16,24},{24,16},{1,9},{9,1},{17,25},{25,17},{2,10},{10... | collective-permute-start | bytes 196616 | tf_op jit(solution)/shard_map/ppermute | solution.py:324
  22.5 2.1 %collective-permute-start.1 = (f32[128,128]{1,0:T(8,128)S(1)}, f32[128,128]{1,0:T(8,128)S(1)}, u32[]{:S(2)}, u32[]{:S(2)}) collective-permute-start(f32[128,128]{1,0:T(8,128)S(1)} %get-tuple-element.13), channel_id=1, source_target_pairs={{8,16},{16,8},{9,17},{17,9},{10,18},{18,10},{11,19},{19,11},{12,20... | collective-permute-start | bytes 196616 | tf_op jit(solution)/shard_map/ppermute | solution.py:323
  24.6 0.3 collective-permute-done.swapped
  24.9 3.5 %collective-permute-done.1.next_swapped = f32[128,128]{1,0:T(8,128)S(1)} collective-permute-done((f32[128,128]{1,0:T(8,128)S(1)}, f32[128,128]{1,0:T(8,128)S(1)}, u32[]{:S(2)}, u32[]{:S(2)}) %collective-permute-start.1) | collective-permute-done | bytes 65568 | tf_op jit(solution)/shard_map/ppermute | solution.py:323
  28.4 0.7 %corners.1 = (f32[32,128]{1,0:T(8,128)S(1)}, f32[32,128]{1,0:T(8,128)S(1)}) custom-call(f32[128,128]{1,0:T(8,128)S(1)} %collective-permute-done.swapped, f32[128,128]{1,0:T(8,128)S(1)} %collective-permute-done.1.next_swapped, f32[112,128]{1,0:T(8,128)S(1)} %get-tuple-element.14.edges, s32[6]{0:T(128)S(1)} %stack.31.where), custom_call_target="tpu_custom_call" | custom-call | flops 1000000 | bytes 4000000 | tf_op jit(solution)/shard_map/corners/pallas_call | solution.py:326
  29.0 1.9 %collective-permute-start.2 = (f32[32,128]{1,0:T(8,128)S(1)}, f32[32,128]{1,0:T(8,128)S(1)}, u32[]{:S(2)}, u32[]{:S(2)}) collective-permute-start(f32[32,128]{1,0:T(8,128)S(1)} %get-tuple-element.15), channel_id=1, source_target_pairs={{0,1},{1,0},{2,3},{3,2},{4,5},{5,4},{6,7},{7,6},{8,9},{9,8},{10,11... | collective-permute-start | bytes 49160 | tf_op jit(solution)/shard_map/ppermute | solution.py:337
  30.9 0.0 collective-permute-start.3
  30.9 0.8 %collective-permute-done.2.beside = f32[32,128]{1,0:T(8,128)S(1)} collective-permute-done((f32[32,128]{1,0:T(8,128)S(1)}, f32[32,128]{1,0:T(8,128)S(1)}, u32[]{:S(2)}, u32[]{:S(2)}) %collective-permute-start.2) | collective-permute-done | bytes 16416 | tf_op jit(solution)/shard_map/ppermute | solution.py:337
  31.7 4.1 %collective-permute-done.3.next_beside = f32[32,128]{1,0:T(8,128)S(1)} collective-permute-done((f32[32,128]{1,0:T(8,128)S(1)}, f32[32,128]{1,0:T(8,128)S(1)}, u32[]{:S(2)}, u32[]{:S(2)}) %collective-permute-start.3) | collective-permute-done | bytes 16416 | tf_op jit(solution)/shard_map/ppermute | solution.py:336
  35.9 0.0 all-to-all-done.1.got
  35.9 0.0 copy-done.12
  35.9 0.0 copy-done.13
  35.9 0.0 copy-start.8
  35.9 1.0 %copy-done.8 = f32[25,32,128]{2,1,0:T(8,128)S(1)} copy-done((f32[25,32,128]{2,1,0:T(8,128)S(1)}, f32[25,32,128]{2,1,0:T(8,128)}, u32[]{:S(2)}) %copy-start.8) | copy-done | bytes 409624
  36.9 2.1 %second_step.1 = f32[25,32,128]{2,1,0:T(8,128)} custom-call(f32[128,128]{1,0:T(8,128)S(1)} %collective-permute-done.swapped, f32[128,128]{1,0:T(8,128)S(1)} %collective-permute-done.1.next_swapped, f32[32,128]{1,0:T(8,128)S(1)} %collective-permute-done.2.beside, f32[32,128]{1,0:T(8,128)S(1)} %collective-permute-done.3.next_beside, ...), custom_call_target="tpu_custom_call" | custom-call | tf_op jit(solution)/shard_map/second_step/pallas_call | solution.py:338
Async XLA Ops:
  0.0 8.2 %all-to-all-start = ((f32[1,1,8,128]{3,1,0,2:T(1,128)}), f32[1,1,8,128]{3,1,0,2:T(1,128)S(1)}, u32[]{:S(2)}, u32[]{:S(2)}) async-start(f32[1,1,8,128]{3,1,0,2:T(1,128)} %bitcast.13), calls=%async_computation | async-start | bytes 8192 | tf_op jit(solution)/shard_map/all_to_all | solution.py:278
  5.4 1.4 %copy-start = (f32[4,25,32,128]{3,2,1,0:T(8,128)S(1)}, f32[4,25,32,128]{3,2,1,0:T(8,128)}, u32[]{:S(2)}) copy-start(f32[4,25,32,128]{3,2,1,0:T(8,128)} %side.5) | copy-start | bytes 4915204
  6.8 1.0 %copy-start.4 = (s32[25,32,128]{2,1,0:T(8,128)S(1)}, s32[25,32,128]{2,1,0:T(8,128)}, u32[]{:S(2)}) copy-start(s32[25,32,128]{2,1,0:T(8,128)} %mask.3) | copy-start | bytes 1228804
  7.8 0.7 %copy-start.10 = (s32[1,1,8,128]{3,2,1,0:T(8,128)S(1)}, s32[1,1,8,128]{3,2,1,0:T(8,128)}, u32[]{:S(2)}) copy-start(s32[1,1,8,128]{3,2,1,0:T(8,128)} %param.16) | copy-start | bytes 12292
  7.8 0.7 %copy-start.11 = (s32[1,1,8]{2,1,0:T(1,128)S(1)}, s32[1,1,8]{2,1,0:T(1,128)}, u32[]{:S(2)}) copy-start(s32[1,1,8]{2,1,0:T(1,128)} %param.17) | copy-start | bytes 100
  7.9 2.4 %copy-start.1 = (f32[4,25,32,128]{3,2,1,0:T(8,128)S(1)}, f32[4,25,32,128]{3,2,1,0:T(8,128)}, u32[]{:S(2)}) copy-start(f32[4,25,32,128]{3,2,1,0:T(8,128)} %side.5) | copy-start | bytes 4915204
  7.9 2.4 %copy-start.2 = (f32[2,25,32,128]{3,2,1,0:T(8,128)S(1)}, f32[2,25,32,128]{3,2,1,0:T(8,128)}, u32[]{:S(2)}) copy-start(f32[2,25,32,128]{3,2,1,0:T(8,128)} %vert.3) | copy-start | bytes 2457604
  7.9 2.4 %copy-start.3 = (f32[25,32,128]{2,1,0:T(8,128)S(1)}, f32[25,32,128]{2,1,0:T(8,128)}, u32[]{:S(2)}) copy-start(f32[25,32,128]{2,1,0:T(8,128)} %centre.3) | copy-start | bytes 1228804
  7.9 2.4 %copy-start.5 = (s32[25,32,128]{2,1,0:T(8,128)S(1)}, s32[25,32,128]{2,1,0:T(8,128)}, u32[]{:S(2)}) copy-start(s32[25,32,128]{2,1,0:T(8,128)} %mask.3) | copy-start | bytes 1228804
  10.3 1.0 %copy-start.6 = (f32[25,32,128]{2,1,0:T(8,128)S(1)}, f32[25,32,128]{2,1,0:T(8,128)}, u32[]{:S(2)}) copy-start(f32[25,32,128]{2,1,0:T(8,128)} %adjoint.1) | copy-start | bytes 1228804
  11.3 24.6 %copy-start.12 = (s32[8]{0:T(128)S(1)}, s32[8]{0:T(128)}, u32[]{:S(2)}) copy-start(s32[8]{0:T(128)} %partner.1) | copy-start | bytes 100
  11.3 24.6 %copy-start.13 = (s32[8]{0:T(128)S(1)}, s32[8]{0:T(128)}, u32[]{:S(2)}) copy-start(s32[8]{0:T(128)} %flip.1) | copy-start | bytes 100
  13.4 0.8 %copy-start.7 = (f32[25,32,128]{2,1,0:T(8,128)}, f32[25,32,128]{2,1,0:T(8,128)S(1)}, u32[]{:S(2)}) copy-start(f32[25,32,128]{2,1,0:T(8,128)S(1)} %get-tuple-element.18.part) | copy-start | bytes 1228804
  14.2 0.7 %copy-start.9 = (f32[8,80,128]{2,1,0:T(8,128)}, f32[8,80,128]{2,1,0:T(8,128)S(1)}, u32[]{:S(2)}) copy-start(f32[8,80,128]{2,1,0:T(8,128)S(1)} %get-tuple-element.17) | copy-start | bytes 983044
  14.9 0.6 %copy-start.14 = (f32[128,128]{1,0:T(8,128)}, f32[128,128]{1,0:T(8,128)S(1)}, u32[]{:S(2)}) copy-start(f32[128,128]{1,0:T(8,128)S(1)} %get-tuple-element.12) | copy-start | bytes 196612
  15.5 20.3 %all-to-all-start.1 = ((f32[8,80,128]{2,1,0:T(8,128)}), f32[8,80,128]{2,1,0:T(8,128)S(1)}, u32[]{:S(2)}, u32[]{:S(2)}) async-start(f32[8,80,128]{2,1,0:T(8,128)} %copy-done.9), calls=%async_computation.1 | async-start | bytes 655360 | tf_op jit(solution)/shard_map/all_to_all | solution.py:322
  21.3 3.6 %collective-permute-start = (f32[128,128]{1,0:T(8,128)}, f32[128,128]{1,0:T(8,128)S(1)}, u32[]{:S(2)}, u32[]{:S(2)}) collective-permute-start(f32[128,128]{1,0:T(8,128)} %copy-done.14), channel_id=1, source_target_pairs={{0,8},{8,0},{16,24},{24,16},{1,9},{9,1},{17,25},{25,17},{2,10},{10... | collective-permute-start | bytes 196616 | tf_op jit(solution)/shard_map/ppermute | solution.py:324
  22.5 5.9 %collective-permute-start.1 = (f32[128,128]{1,0:T(8,128)S(1)}, f32[128,128]{1,0:T(8,128)S(1)}, u32[]{:S(2)}, u32[]{:S(2)}) collective-permute-start(f32[128,128]{1,0:T(8,128)S(1)} %get-tuple-element.13), channel_id=1, source_target_pairs={{8,16},{16,8},{9,17},{17,9},{10,18},{18,10},{11,19},{19,11},{12,20... | collective-permute-start | bytes 196616 | tf_op jit(solution)/shard_map/ppermute | solution.py:323
  29.0 2.7 %collective-permute-start.2 = (f32[32,128]{1,0:T(8,128)S(1)}, f32[32,128]{1,0:T(8,128)S(1)}, u32[]{:S(2)}, u32[]{:S(2)}) collective-permute-start(f32[32,128]{1,0:T(8,128)S(1)} %get-tuple-element.15), channel_id=1, source_target_pairs={{0,1},{1,0},{2,3},{3,2},{4,5},{5,4},{6,7},{7,6},{8,9},{9,8},{10,11... | collective-permute-start | bytes 49160 | tf_op jit(solution)/shard_map/ppermute | solution.py:337
  30.9 5.0 %collective-permute-start.3 = (f32[32,128]{1,0:T(8,128)S(1)}, f32[32,128]{1,0:T(8,128)S(1)}, u32[]{:S(2)}, u32[]{:S(2)}) collective-permute-start(f32[32,128]{1,0:T(8,128)S(1)} %get-tuple-element.16), channel_id=1, source_target_pairs={{1,2},{2,1},{3,4},{4,3},{5,6},{6,5},{7,0},{0,7},{9,10},{10,9},{11,... | collective-permute-start | bytes 49160 | tf_op jit(solution)/shard_map/ppermute | solution.py:336
  35.9 1.0 %copy-start.8 = (f32[25,32,128]{2,1,0:T(8,128)S(1)}, f32[25,32,128]{2,1,0:T(8,128)}, u32[]{:S(2)}) copy-start(f32[25,32,128]{2,1,0:T(8,128)} %copy-done.7) | copy-start | bytes 1228804

commit v2 on v1

--- a/solution.py
+++ b/solution.py
@@ -12,6 +12,7 @@
 COLS = 128
 CAP = 128
 GROUP = 8
+CHUNK = 5
 PAD = 32
 LINES = 4 * PAD
 CORNER = 3 * LEVELS
@@ -22,6 +23,7 @@
 LAND = 1e38
 MIB = 1024 * 1024
 VMEM = pl.BlockSpec(memory_space=pltpu.VMEM)
+FAR = pl.BlockSpec(memory_space=pltpu.HBM)
 SMEM = pl.BlockSpec(memory_space=pltpu.SMEM)
 
 
@@ -132,7 +134,12 @@
     )
 
 
-def first_kernel(forcing, where, scales, adjoint, side, centre, vert, mask, part, swap, next_swap, edges, slots, held, up, down, base):
+def chunk(source, target, semaphores, i):
+    levels = pl.ds(i * CHUNK, CHUNK)
+    return pltpu.make_async_copy(source.at[levels], target.at[levels], semaphores.at[i])
+
+
+def first_kernel(forcing, where, scales, adjoint, side, centre, vert, mask, part_far, swap, next_swap, edges, slots, held, part, up, down, base, sent):
     for i in range(4):
         for ref in (up, down):
             ref[i * PAD + 24 : (i + 1) * PAD, :] = jnp.zeros((8, COLS), jnp.float32)
@@ -149,6 +156,8 @@
             ref[PAD + k : PAD + k + 1, :] = r[at : at + 1]
             ref[3 * PAD + k : 3 * PAD + k + 1, :] = sides[at : at + 1]
         packed = [p + turn(x, 2 * k + 1) for p, x in zip(packed, (sides, outer(lane, r, r)))]
+        if (k + 1) % CHUNK == 0:
+            chunk(part, part_far, sent, k // CHUNK).start()
     up[2 * PAD : 3 * PAD, :] = scales[16 : 16 + PAD, :]
     down[2 * PAD : 3 * PAD, :] = scales[16 + PAD : 16 + 2 * PAD, :]
     for i in range(3):
@@ -167,6 +176,8 @@
     edges[40:48, :] = scales[8:16, :]
     edges[48 : 48 + PAD, :] = down[0:PAD, :]
     edges[48 + PAD : EDGES, :] = up[0:PAD, :]
+    for i in range(LEVELS // CHUNK):
+        chunk(part, part_far, sent, i).wait()
 
 
 def corner_kernel(swapped, next_swapped, edges, where, swap, next_swap):
@@ -188,7 +199,9 @@
         ref[24:EDGE, :] = jnp.where(iota((EDGE - 24, COLS), 0) == 0, corners, 0.0)
 
 
-def second_kernel(swapped, next_swapped, beside, next_beside, edges, got, partner, flip, where, part, side, centre, vert, out, held, lines, near_sides, far_sides, west_side, east_side):
+def second_kernel(swapped, next_swapped, beside, next_beside, edges, got, partner, flip, where, part_far, side, centre, vert, out, held, part, result, lines, near_sides, far_sides, west_side, east_side, loaded, sent):
+    for i in range(LEVELS // CHUNK):
+        chunk(part_far, part, loaded, i).start()
     sources = got.shape[0]
     below_near, above_near = from_tiles(swapped, next_swapped, where, 0)
     below_part, above_part = from_tiles(swapped, next_swapped, where, PAD)
@@ -255,10 +268,16 @@
         return jnp.where(part[k] == LAND, 0.0, r)
 
     for k in range(LEVELS):
+        if k % CHUNK == 0:
+            chunk(part_far, part, loaded, k // CHUNK).wait()
         held[k] = joined(k, part[k], near_sides, lines[3 * PAD + k : 3 * PAD + k + 1, :], lines[k : k + 1, :])
     for k in range(LEVELS):
         r = terms(k, held, centre, side, vert)[0]
-        out[k] = joined(k, r, far_sides, lines[PAD + k : PAD + k + 1, :], lines[2 * PAD + k : 2 * PAD + k + 1, :])
+        result[k] = joined(k, r, far_sides, lines[PAD + k : PAD + k + 1, :], lines[2 * PAD + k : 2 * PAD + k + 1, :])
+        if (k + 1) % CHUNK == 0:
+            chunk(result, out, sent, k // CHUNK).start()
+    for i in range(LEVELS // CHUNK):
+        chunk(result, out, sent, i).wait()
 
 
 def body(adjoint_in, centre, side_coeff, vert_coeff, land_mask, obs_misfit, obs_cell, obs_count, fold_partner, fold_flip):
@@ -280,6 +299,7 @@
     tile = jax.ShapeDtypeStruct((LEVELS, ROWS, COLS), f32)
     lines = jax.ShapeDtypeStruct((LINES, COLS), f32)
     field = pltpu.VMEM((LEVELS, ROWS, COLS), f32)
+    chunks = pltpu.SemaphoreType.DMA((LEVELS // CHUNK,))
     group = min(GROUP, sources)
     small = sources <= GROUP
     ahead = pl.CostEstimate(flops=10**10, bytes_accessed=2 * 10**8, transcendentals=0)
@@ -302,19 +322,21 @@
             pltpu.VMEM((3 * COLS, group * CAP), jnp.bfloat16),
         ],
         compiler_params=pltpu.CompilerParams(vmem_limit_bytes=(8 if small else 24) * MIB),
-        cost_estimate=pl.CostEstimate(flops=10**8, bytes_accessed=4 * 10**6, transcendentals=0),
+        cost_estimate=pl.CostEstimate(flops=10**8, bytes_accessed=8 * 10**6, transcendentals=0),
         name="forcing",
     )(received.reshape(sources, CAP), obs_cell.reshape(sources, CAP), obs_count.reshape(1, sources))
     part, swap, next_swap, edges, slots = pl.pallas_call(
         first_kernel,
         out_shape=(tile, lines, lines, jax.ShapeDtypeStruct((EDGES, COLS), f32), jax.ShapeDtypeStruct((sources, SLOT, COLS), f32)),
         in_specs=[VMEM, SMEM] + [VMEM] * 6,
-        out_specs=(VMEM,) * 5,
+        out_specs=(FAR,) + (VMEM,) * 4,
         scratch_shapes=[
+            field,
             field,
             pltpu.VMEM((LINES, COLS), f32),
             pltpu.VMEM((LINES, COLS), f32),
             pltpu.VMEM((SLOT, COLS), f32),
+            chunks,
         ],
         compiler_params=pltpu.CompilerParams(vmem_limit_bytes=(8 if small else 24) * MIB),
         name="first_step",
@@ -338,15 +360,20 @@
     return pl.pallas_call(
         second_kernel,
         out_shape=tile,
-        in_specs=[VMEM] * 6 + [SMEM] * 3 + [VMEM] * 4,
-        out_specs=VMEM,
+        in_specs=[VMEM] * 6 + [SMEM] * 3 + [FAR] + [VMEM] * 3,
+        out_specs=FAR,
+        input_output_aliases={9: 0},
         scratch_shapes=[
+            field,
+            field,
             field,
             pltpu.VMEM((4 * PAD, COLS), f32),
             pltpu.VMEM((ROWS, COLS), f32),
             pltpu.VMEM((ROWS, COLS), f32),
             pltpu.VMEM((EDGE, COLS), f32),
             pltpu.VMEM((EDGE, COLS), f32),
+            chunks,
+            chunks,
         ],
         compiler_params=pltpu.CompilerParams(vmem_limit_bytes=8 * MIB),
         name="second_step",

time: 39.4 us -> 39.2 us (level)
  local copies, waits for them, and re-layouts: 6.96 us -> 5.2 us
  Pallas kernels: 6.79 us -> 8.4 us
    unnamed x30 -> x26, local copies, waits for them, and re-layouts: 6.88 us -> 5.12 us
    pallas_call x1, Pallas kernels: 2.06 us -> 3.05 us  [body(): pl.pallas_call(second_kernel, out_shape=tile, in_specs=[VMEM] * 6 + [SMEM...]
    pallas_call x1, Pallas kernels: 2.12 us -> 2.73 us  [body(): pl.pallas_call(first_kernel, out_shape=(tile, lines, lines, jax.ShapeDtyp...]
where the time goes in v2:
time: 39.2 us; the launch traced here: 38.8 us
  starting transfers between devices  16.3 us (42%)
  waiting for transfers between devices  8.76 us (22%)
  Pallas kernels  8.4 us (21%)
  local copies, waits for them, and re-layouts  5.2 us (13%)
    all_to_all x1, starting transfers between devices, body(): got = lax.all_to_all(slots, 'col', split_axis=0, concat_axis=0, tiled=True)  5.74 us
    all_to_all x1, starting transfers between devices, body(): lax.all_to_all(obs_misfit, 'col', split_axis=2, concat_axis=1, tiled=True)  5.41 us
    unnamed x26, local copies, waits for them, and re-layouts  5.12 us
    ppermute x1, waiting for transfers between devices, body(): lax.ppermute(next_beside, 'col', swaps(1, sources - 1) + round_trip)  4.12 us
    ppermute x1, waiting for transfers between devices, body(): next_swapped = lax.ppermute(next_swap, 'tile', swaps(1, tiles - 1))  3.48 us
    pallas_call x1, Pallas kernels, body(): pl.pallas_call(second_kernel, out_shape=tile, in_specs=[VMEM] * 6 + [SMEM...  3.05 us
    pallas_call x1, Pallas kernels, body(): pl.pallas_call(first_kernel, out_shape=(tile, lines, lines, jax.ShapeDtyp...  2.73 us
    ppermute x1, starting transfers between devices, body(): next_swapped = lax.ppermute(next_swap, 'tile', swaps(1, tiles - 1))  2.1 us
  transfers between devices with their start and end apart: 6, of which 4 were waited for; matrix products, arithmetic and copies ran while one was open for 0% of the time, Pallas kernels for 2%

profile of v2, /device:TPU:29, one launch (start us, length us, event | category | flops | bytes accessed | tf_op | source)
XLA Modules:
  0.0 38.8 jit_solution(17222788707105423075)
XLA Ops:
  0.0 5.4 %all-to-all-start = ((f32[1,1,8,128]{3,1,0,2:T(1,128)}), f32[1,1,8,128]{3,1,0,2:T(1,128)S(1)}, u32[]{:S(2)}, u32[]{:S(2)}) async-start(f32[1,1,8,128]{3,1,0,2:T(1,128)} %bitcast.13), calls=%async_computation | async-start | bytes 8192 | tf_op jit(solution)/shard_map/all_to_all | solution.py:297
  5.4 0.0 copy-start
  5.4 1.4 %copy-done = f32[4,25,32,128]{3,2,1,0:T(8,128)S(1)} copy-done((f32[4,25,32,128]{3,2,1,0:T(8,128)S(1)}, f32[4,25,32,128]{3,2,1,0:T(8,128)}, u32[]{:S(2)}) %copy-start) | copy-done | bytes 1638424
  6.8 0.0 copy-start.4
  6.8 1.0 %copy-done.4 = s32[25,32,128]{2,1,0:T(8,128)S(1)} copy-done((s32[25,32,128]{2,1,0:T(8,128)S(1)}, s32[25,32,128]{2,1,0:T(8,128)}, u32[]{:S(2)}) %copy-start.4) | copy-done | bytes 409624
  7.8 0.0 copy-start.8
  7.8 0.0 copy-start.9
  7.9 0.0 copy-start.1
  7.9 0.0 copy-start.2
  7.9 0.0 copy-start.3
  7.9 0.0 copy-start.5
  7.9 0.2 edge_scales.1.scales
  8.1 0.1 stack.31.where
  8.2 0.0 all-to-all-done
  8.2 0.3 copy-done.8
  8.5 0.0 copy-done.9
  8.5 1.7 %forcing.1 = f32[800,128]{1,0:T(8,128)S(1)} custom-call(f32[8,128]{1,0:T(8,128)S(1)} %bitcast.10, s32[8,128]{1,0:T(8,128)S(1)} %bitcast.11, s32[1,8]{1,0:T(1,128)S(1)} %bitcast.12), custom_call_target="tpu_custom_call" | custom-call | flops 100000000 | bytes 8000000 | tf_op jit(solution)/shard_map/forcing/pallas_call | solution.py:315
  10.2 0.0 copy-done.1
  10.3 0.0 copy-done.2
  10.3 0.0 copy-done.3
  10.3 0.0 copy-done.5
  10.3 0.0 copy-start.6
  10.3 1.0 %copy-done.6 = f32[25,32,128]{2,1,0:T(8,128)S(1)} copy-done((f32[25,32,128]{2,1,0:T(8,128)S(1)}, f32[25,32,128]{2,1,0:T(8,128)}, u32[]{:S(2)}) %copy-start.6) | copy-done | bytes 409624
  11.3 0.0 copy-start.10
  11.3 0.0 copy-start.11
  11.3 2.7 %first_step.1 = (f32[25,32,128]{2,1,0:T(8,128)}, f32[128,128]{1,0:T(8,128)S(1)}, f32[128,128]{1,0:T(8,128)S(1)}, f32[112,128]{1,0:T(8,128)S(1)}, f32[8,80,128]{2,1,0:T(8,128)S(1)}) custom-call(f32[800,128]{1,0:T(8,128)S(1)} %forcing.1, s32[6]{0:T(128)S(1)} %stack.31.where, f32[80,128]{1,0:T(8,128)S(1)} %edge_scales.1.scales, f32[25,32,128]{2,1,0:T(8,128)S(1)} %copy-done.6, ...), custom_call_target="tpu_custom_call" | custom-call | tf_op jit(solution)/shard_map/first_step/pallas_call | solution.py:328
  14.0 0.0 copy-start.7
  14.0 0.7 %copy-done.7 = f32[8,80,128]{2,1,0:T(8,128)} copy-done((f32[8,80,128]{2,1,0:T(8,128)}, f32[8,80,128]{2,1,0:T(8,128)S(1)}, u32[]{:S(2)}) %copy-start.7) | copy-done | bytes 327704
  14.8 0.0 copy-start.12
  14.8 0.6 %copy-done.12 = f32[128,128]{1,0:T(8,128)} copy-done((f32[128,128]{1,0:T(8,128)}, f32[128,128]{1,0:T(8,128)S(1)}, u32[]{:S(2)}) %copy-start.12) | copy-done | bytes 65560
  15.4 5.7 %all-to-all-start.1 = ((f32[8,80,128]{2,1,0:T(8,128)}), f32[8,80,128]{2,1,0:T(8,128)S(1)}, u32[]{:S(2)}, u32[]{:S(2)}) async-start(f32[8,80,128]{2,1,0:T(8,128)} %copy-done.7), calls=%async_computation.1 | async-start | bytes 655360 | tf_op jit(solution)/shard_map/all_to_all | solution.py:344
  21.1 1.2 %collective-permute-start = (f32[128,128]{1,0:T(8,128)}, f32[128,128]{1,0:T(8,128)S(1)}, u32[]{:S(2)}, u32[]{:S(2)}) collective-permute-start(f32[128,128]{1,0:T(8,128)} %copy-done.12), channel_id=1, source_target_pairs={{0,8},{8,0},{16,24},{24,16},{1,9},{9,1},{17,25},{25,17},{2,10},{10... | collective-permute-start | bytes 196616 | tf_op jit(solution)/shard_map/ppermute | solution.py:346
  22.3 2.1 %collective-permute-start.1 = (f32[128,128]{1,0:T(8,128)S(1)}, f32[128,128]{1,0:T(8,128)S(1)}, u32[]{:S(2)}, u32[]{:S(2)}) collective-permute-start(f32[128,128]{1,0:T(8,128)S(1)} %get-tuple-element.13), channel_id=1, source_target_pairs={{8,16},{16,8},{9,17},{17,9},{10,18},{18,10},{11,19},{19,11},{12,20... | collective-permute-start | bytes 196616 | tf_op jit(solution)/shard_map/ppermute | solution.py:345
  24.4 0.3 collective-permute-done.swapped
  24.7 3.5 %collective-permute-done.1.next_swapped = f32[128,128]{1,0:T(8,128)S(1)} collective-permute-done((f32[128,128]{1,0:T(8,128)S(1)}, f32[128,128]{1,0:T(8,128)S(1)}, u32[]{:S(2)}, u32[]{:S(2)}) %collective-permute-start.1) | collective-permute-done | bytes 65568 | tf_op jit(solution)/shard_map/ppermute | solution.py:345
  28.2 0.7 %corners.1 = (f32[32,128]{1,0:T(8,128)S(1)}, f32[32,128]{1,0:T(8,128)S(1)}) custom-call(f32[128,128]{1,0:T(8,128)S(1)} %collective-permute-done.swapped, f32[128,128]{1,0:T(8,128)S(1)} %collective-permute-done.1.next_swapped, f32[112,128]{1,0:T(8,128)S(1)} %get-tuple-element.14.edges, s32[6]{0:T(128)S(1)} %stack.31.where), custom_call_target="tpu_custom_call" | custom-call | flops 1000000 | bytes 4000000 | tf_op jit(solution)/shard_map/corners/pallas_call | solution.py:348
  28.9 1.9 %collective-permute-start.2 = (f32[32,128]{1,0:T(8,128)S(1)}, f32[32,128]{1,0:T(8,128)S(1)}, u32[]{:S(2)}, u32[]{:S(2)}) collective-permute-start(f32[32,128]{1,0:T(8,128)S(1)} %get-tuple-element.15), channel_id=1, source_target_pairs={{0,1},{1,0},{2,3},{3,2},{4,5},{5,4},{6,7},{7,6},{8,9},{9,8},{10,11... | collective-permute-start | bytes 49160 | tf_op jit(solution)/shard_map/ppermute | solution.py:359
  30.8 0.0 collective-permute-start.3
  30.8 0.8 %collective-permute-done.2.beside = f32[32,128]{1,0:T(8,128)S(1)} collective-permute-done((f32[32,128]{1,0:T(8,128)S(1)}, f32[32,128]{1,0:T(8,128)S(1)}, u32[]{:S(2)}, u32[]{:S(2)}) %collective-permute-start.2) | collective-permute-done | bytes 16416 | tf_op jit(solution)/shard_map/ppermute | solution.py:359
  31.6 4.1 %collective-permute-done.3.next_beside = f32[32,128]{1,0:T(8,128)S(1)} collective-permute-done((f32[32,128]{1,0:T(8,128)S(1)}, f32[32,128]{1,0:T(8,128)S(1)}, u32[]{:S(2)}, u32[]{:S(2)}) %collective-permute-start.3) | collective-permute-done | bytes 16416 | tf_op jit(solution)/shard_map/ppermute | solution.py:358
  35.7 0.0 all-to-all-done.1.got
  35.7 0.0 copy-done.10
  35.7 0.0 copy-done.11
  35.7 3.1 %second_step.1 = f32[25,32,128]{2,1,0:T(8,128)} custom-call(f32[128,128]{1,0:T(8,128)S(1)} %collective-permute-done.swapped, f32[128,128]{1,0:T(8,128)S(1)} %collective-permute-done.1.next_swapped, f32[32,128]{1,0:T(8,128)S(1)} %collective-permute-done.2.beside, f32[32,128]{1,0:T(8,128)S(1)} %collective-permute-done.3.next_beside, ...), custom_call_target="tpu_custom_call", output_to_operand_aliasing={{}: (9, {})} | custom-call | tf_op jit(solution)/shard_map/second_step/pallas_call | solution.py:360
Async XLA Ops:
  0.0 8.2 %all-to-all-start = ((f32[1,1,8,128]{3,1,0,2:T(1,128)}), f32[1,1,8,128]{3,1,0,2:T(1,128)S(1)}, u32[]{:S(2)}, u32[]{:S(2)}) async-start(f32[1,1,8,128]{3,1,0,2:T(1,128)} %bitcast.13), calls=%async_computation | async-start | bytes 8192 | tf_op jit(solution)/shard_map/all_to_all | solution.py:297
  5.4 1.4 %copy-start = (f32[4,25,32,128]{3,2,1,0:T(8,128)S(1)}, f32[4,25,32,128]{3,2,1,0:T(8,128)}, u32[]{:S(2)}) copy-start(f32[4,25,32,128]{3,2,1,0:T(8,128)} %side.5) | copy-start | bytes 4915204
  6.8 1.0 %copy-start.4 = (s32[25,32,128]{2,1,0:T(8,128)S(1)}, s32[25,32,128]{2,1,0:T(8,128)}, u32[]{:S(2)}) copy-start(s32[25,32,128]{2,1,0:T(8,128)} %mask.3) | copy-start | bytes 1228804
  7.8 0.7 %copy-start.8 = (s32[1,1,8,128]{3,2,1,0:T(8,128)S(1)}, s32[1,1,8,128]{3,2,1,0:T(8,128)}, u32[]{:S(2)}) copy-start(s32[1,1,8,128]{3,2,1,0:T(8,128)} %param.16) | copy-start | bytes 12292
  7.8 0.7 %copy-start.9 = (s32[1,1,8]{2,1,0:T(1,128)S(1)}, s32[1,1,8]{2,1,0:T(1,128)}, u32[]{:S(2)}) copy-start(s32[1,1,8]{2,1,0:T(1,128)} %param.17) | copy-start | bytes 100
  7.9 2.4 %copy-start.1 = (f32[4,25,32,128]{3,2,1,0:T(8,128)S(1)}, f32[4,25,32,128]{3,2,1,0:T(8,128)}, u32[]{:S(2)}) copy-start(f32[4,25,32,128]{3,2,1,0:T(8,128)} %side.5) | copy-start | bytes 4915204
  7.9 2.4 %copy-start.2 = (f32[2,25,32,128]{3,2,1,0:T(8,128)S(1)}, f32[2,25,32,128]{3,2,1,0:T(8,128)}, u32[]{:S(2)}) copy-start(f32[2,25,32,128]{3,2,1,0:T(8,128)} %vert.3) | copy-start | bytes 2457604
  7.9 2.4 %copy-start.3 = (f32[25,32,128]{2,1,0:T(8,128)S(1)}, f32[25,32,128]{2,1,0:T(8,128)}, u32[]{:S(2)}) copy-start(f32[25,32,128]{2,1,0:T(8,128)} %centre.3) | copy-start | bytes 1228804
  7.9 2.4 %copy-start.5 = (s32[25,32,128]{2,1,0:T(8,128)S(1)}, s32[25,32,128]{2,1,0:T(8,128)}, u32[]{:S(2)}) copy-start(s32[25,32,128]{2,1,0:T(8,128)} %mask.3) | copy-start | bytes 1228804
  10.3 1.0 %copy-start.6 = (f32[25,32,128]{2,1,0:T(8,128)S(1)}, f32[25,32,128]{2,1,0:T(8,128)}, u32[]{:S(2)}) copy-start(f32[25,32,128]{2,1,0:T(8,128)} %adjoint.1) | copy-start | bytes 1228804
  11.3 24.4 %copy-start.10 = (s32[8]{0:T(128)S(1)}, s32[8]{0:T(128)}, u32[]{:S(2)}) copy-start(s32[8]{0:T(128)} %partner.1) | copy-start | bytes 100
  11.3 24.4 %copy-start.11 = (s32[8]{0:T(128)S(1)}, s32[8]{0:T(128)}, u32[]{:S(2)}) copy-start(s32[8]{0:T(128)} %flip.1) | copy-start | bytes 100
  14.0 0.7 %copy-start.7 = (f32[8,80,128]{2,1,0:T(8,128)}, f32[8,80,128]{2,1,0:T(8,128)S(1)}, u32[]{:S(2)}) copy-start(f32[8,80,128]{2,1,0:T(8,128)S(1)} %get-tuple-element.17) | copy-start | bytes 983044
  14.8 0.6 %copy-start.12 = (f32[128,128]{1,0:T(8,128)}, f32[128,128]{1,0:T(8,128)S(1)}, u32[]{:S(2)}) copy-start(f32[128,128]{1,0:T(8,128)S(1)} %get-tuple-element.12) | copy-start | bytes 196612
  15.4 20.3 %all-to-all-start.1 = ((f32[8,80,128]{2,1,0:T(8,128)}), f32[8,80,128]{2,1,0:T(8,128)S(1)}, u32[]{:S(2)}, u32[]{:S(2)}) async-start(f32[8,80,128]{2,1,0:T(8,128)} %copy-done.7), calls=%async_computation.1 | async-start | bytes 655360 | tf_op jit(solution)/shard_map/all_to_all | solution.py:344
  21.1 3.6 %collective-permute-start = (f32[128,128]{1,0:T(8,128)}, f32[128,128]{1,0:T(8,128)S(1)}, u32[]{:S(2)}, u32[]{:S(2)}) collective-permute-start(f32[128,128]{1,0:T(8,128)} %copy-done.12), channel_id=1, source_target_pairs={{0,8},{8,0},{16,24},{24,16},{1,9},{9,1},{17,25},{25,17},{2,10},{10... | collective-permute-start | bytes 196616 | tf_op jit(solution)/shard_map/ppermute | solution.py:346
  22.3 5.9 %collective-permute-start.1 = (f32[128,128]{1,0:T(8,128)S(1)}, f32[128,128]{1,0:T(8,128)S(1)}, u32[]{:S(2)}, u32[]{:S(2)}) collective-permute-start(f32[128,128]{1,0:T(8,128)S(1)} %get-tuple-element.13), channel_id=1, source_target_pairs={{8,16},{16,8},{9,17},{17,9},{10,18},{18,10},{11,19},{19,11},{12,20... | collective-permute-start | bytes 196616 | tf_op jit(solution)/shard_map/ppermute | solution.py:345
  28.9 2.7 %collective-permute-start.2 = (f32[32,128]{1,0:T(8,128)S(1)}, f32[32,128]{1,0:T(8,128)S(1)}, u32[]{:S(2)}, u32[]{:S(2)}) collective-permute-start(f32[32,128]{1,0:T(8,128)S(1)} %get-tuple-element.15), channel_id=1, source_target_pairs={{0,1},{1,0},{2,3},{3,2},{4,5},{5,4},{6,7},{7,6},{8,9},{9,8},{10,11... | collective-permute-start | bytes 49160 | tf_op jit(solution)/shard_map/ppermute | solution.py:359
  30.8 5.0 %collective-permute-start.3 = (f32[32,128]{1,0:T(8,128)S(1)}, f32[32,128]{1,0:T(8,128)S(1)}, u32[]{:S(2)}, u32[]{:S(2)}) collective-permute-start(f32[32,128]{1,0:T(8,128)S(1)} %get-tuple-element.16), channel_id=1, source_target_pairs={{1,2},{2,1},{3,4},{4,3},{5,6},{6,5},{7,0},{0,7},{9,10},{10,9},{11,... | collective-permute-start | bytes 49160 | tf_op jit(solution)/shard_map/ppermute | solution.py:358

commit v3 on v2

--- a/solution.py
+++ b/solution.py
@@ -78,7 +78,9 @@
     return eastward, westward
 
 
-def forcing_kernel(sources, misfit, cell, count, forcing, hot, valued):
+def forcing_kernel(sources, misfit, cell, count, adjoint_far, start, hot, valued, forcing, adjoint, arrived):
+    load = pltpu.make_async_copy(adjoint_far, adjoint, arrived)
+    load.start()
     group = min(GROUP, sources)
     lane = iota((1, CAP), 1)
     for first in range(0, sources, group):
@@ -102,6 +104,9 @@
             forcing[...] = part
         else:
             forcing[...] += part
+    load.wait()
+    for k in range(LEVELS):
+        start[k] = adjoint[k] + forcing[k * ROWS : (k + 1) * ROWS, :]
 
 
 def to_lanes(column, offset):
@@ -139,12 +144,10 @@
     return pltpu.make_async_copy(source.at[levels], target.at[levels], semaphores.at[i])
 
 
-def first_kernel(forcing, where, scales, adjoint, side, centre, vert, mask, part_far, swap, next_swap, edges, slots, held, part, up, down, base, sent):
+def first_kernel(held, where, scales, side, centre, vert, mask, part_far, swap, next_swap, edges, slots, part, up, down, base, sent, posted):
     for i in range(4):
         for ref in (up, down):
             ref[i * PAD + 24 : (i + 1) * PAD, :] = jnp.zeros((8, COLS), jnp.float32)
-    for k in range(LEVELS):
-        held[k] = adjoint[k] + forcing[k * ROWS : (k + 1) * ROWS, :]
     lane = iota((ROWS, COLS), 1)
     packed = [jnp.zeros((ROWS, COLS), jnp.float32)] * 2
     for k in range(LEVELS):
@@ -165,8 +168,9 @@
     own_east, own_west = ends(up[3 * PAD : 4 * PAD, :])
     base[CORNER : CORNER + 1, :] = to_lanes(own_east, OFFSET[0]) + to_lanes(own_west, OFFSET[1])
     base[CORNER + 1 : SLOT, :] = jnp.zeros((SLOT - CORNER - 1, COLS), jnp.float32)
-    for s in range(slots.shape[0]):
-        slots[s] = base[...]
+    spread = [pltpu.make_async_copy(base, slots.at[s], posted.at[s]) for s in range(slots.shape[0])]
+    for copy in spread:
+        copy.start()
     upward = where[4] == 0
     swap[...] = jnp.where(upward, up[...], down[...])
     next_swap[...] = jnp.where(upward, down[...], up[...])
@@ -178,6 +182,8 @@
     edges[48 + PAD : EDGES, :] = up[0:PAD, :]
     for i in range(LEVELS // CHUNK):
         chunk(part, part_far, sent, i).wait()
+    for copy in spread:
+        copy.wait()
 
 
 def corner_kernel(swapped, next_swapped, edges, where, swap, next_swap):
@@ -312,35 +318,38 @@
         cost_estimate=ahead,
         name="edge_scales",
     )(side_coeff, land_mask)
-    forcing = pl.pallas_call(
+    start = pl.pallas_call(
         functools.partial(forcing_kernel, sources),
-        out_shape=jax.ShapeDtypeStruct((LEVELS * ROWS, COLS), f32),
-        in_specs=[VMEM, VMEM, SMEM],
+        out_shape=tile,
+        in_specs=[VMEM, VMEM, SMEM, FAR],
         out_specs=VMEM,
         scratch_shapes=[
             pltpu.VMEM((LEVELS * ROWS, group * CAP), jnp.bfloat16),
             pltpu.VMEM((3 * COLS, group * CAP), jnp.bfloat16),
+            pltpu.VMEM((LEVELS * ROWS, COLS), f32),
+            field,
+            pltpu.SemaphoreType.DMA,
         ],
         compiler_params=pltpu.CompilerParams(vmem_limit_bytes=(8 if small else 24) * MIB),
         cost_estimate=pl.CostEstimate(flops=10**8, bytes_accessed=8 * 10**6, transcendentals=0),
         name="forcing",
-    )(received.reshape(sources, CAP), obs_cell.reshape(sources, CAP), obs_count.reshape(1, sources))
+    )(received.reshape(sources, CAP), obs_cell.reshape(sources, CAP), obs_count.reshape(1, sources), pltpu.with_memory_space_constraint(adjoint_in, pltpu.HBM))
     part, swap, next_swap, edges, slots = pl.pallas_call(
         first_kernel,
-        out_shape=(tile, lines, lines, jax.ShapeDtypeStruct((EDGES, COLS), f32), jax.ShapeDtypeStruct((sources, SLOT, COLS), f32)),
-        in_specs=[VMEM, SMEM] + [VMEM] * 6,
-        out_specs=(FAR,) + (VMEM,) * 4,
+        out_shape=(tile, lines, lines, jax.ShapeDtypeStruct((EDGES, COLS), f32), pltpu.HBM((sources, SLOT, COLS), f32)),
+        in_specs=[VMEM, SMEM] + [VMEM] * 5,
+        out_specs=(FAR,) + (VMEM,) * 3 + (FAR,),
         scratch_shapes=[
-            field,
             field,
             pltpu.VMEM((LINES, COLS), f32),
             pltpu.VMEM((LINES, COLS), f32),
             pltpu.VMEM((SLOT, COLS), f32),
             chunks,
+            pltpu.SemaphoreType.DMA((sources,)),
         ],
         compiler_params=pltpu.CompilerParams(vmem_limit_bytes=(8 if small else 24) * MIB),
         name="first_step",
-    )(forcing, where, scales, adjoint_in, side_coeff, centre, vert_coeff, land_mask)
+    )(start, where, scales, side_coeff, centre, vert_coeff, land_mask)
     got = lax.all_to_all(slots, "col", split_axis=0, concat_axis=0, tiled=True)
     next_swapped = lax.ppermute(next_swap, "tile", swaps(1, tiles - 1))
     swapped = lax.ppermute(swap, "tile", swaps(0, tiles))

time: 39.2 us -> 38.3 us (0.977)
  local copies, waits for them, and re-layouts: 5.2 us -> 3.48 us
  Pallas kernels: 8.4 us -> 9.17 us
    unnamed x26 -> x22, local copies, waits for them, and re-layouts: 5.12 us -> 3.4 us
    pallas_call x1, Pallas kernels: 1.71 us -> 2.31 us  [body(): pl.pallas_call(functools.partial(forcing_kernel, sources), out_shape=tile...]
where the time goes in v3:
time: 38.3 us; the launch traced here: 37.8 us
  starting transfers between devices  16.3 us (43%)
  Pallas kernels  9.17 us (24%)
  waiting for transfers between devices  8.76 us (23%)
  local copies, waits for them, and re-layouts  3.48 us (9%)
    all_to_all x1, starting transfers between devices, body(): got = lax.all_to_all(slots, 'col', split_axis=0, concat_axis=0, tiled=True)  5.74 us
    all_to_all x1, starting transfers between devices, body(): lax.all_to_all(obs_misfit, 'col', split_axis=2, concat_axis=1, tiled=True)  5.41 us
    ppermute x1, waiting for transfers between devices, body(): lax.ppermute(next_beside, 'col', swaps(1, sources - 1) + round_trip)  4.12 us
    ppermute x1, waiting for transfers between devices, body(): next_swapped = lax.ppermute(next_swap, 'tile', swaps(1, tiles - 1))  3.48 us
    unnamed x22, local copies, waits for them, and re-layouts  3.4 us
    pallas_call x1, Pallas kernels, body(): pl.pallas_call(second_kernel, out_shape=tile, in_specs=[VMEM] * 6 + [SMEM...  3.05 us
    pallas_call x1, Pallas kernels, body(): pl.pallas_call(first_kernel, out_shape=(tile, lines, lines, jax.ShapeDtyp...  2.9 us
    pallas_call x1, Pallas kernels, body(): pl.pallas_call(functools.partial(forcing_kernel, sources), out_shape=tile...  2.31 us
  transfers between devices with their start and end apart: 6, of which 4 were waited for; matrix products, arithmetic and copies ran while one was open for 0% of the time, Pallas kernels for 2%

profile of v3, /device:TPU:29, one launch (start us, length us, event | category | flops | bytes accessed | tf_op | source)
XLA Modules:
  0.0 37.8 jit_solution(14658050088860991764)
XLA Ops:
  0.0 5.4 %all-to-all-start = ((f32[1,1,8,128]{3,1,0,2:T(1,128)}), f32[1,1,8,128]{3,1,0,2:T(1,128)S(1)}, u32[]{:S(2)}, u32[]{:S(2)}) async-start(f32[1,1,8,128]{3,1,0,2:T(1,128)} %bitcast.13), calls=%async_computation | async-start | bytes 8192 | tf_op jit(solution)/shard_map/all_to_all | solution.py:303
  5.4 0.0 copy-start
  5.4 1.4 %copy-done = f32[4,25,32,128]{3,2,1,0:T(8,128)S(1)} copy-done((f32[4,25,32,128]{3,2,1,0:T(8,128)S(1)}, f32[4,25,32,128]{3,2,1,0:T(8,128)}, u32[]{:S(2)}) %copy-start) | copy-done | bytes 1638424
  6.8 0.0 copy-start.4
  6.8 1.0 %copy-done.4 = s32[25,32,128]{2,1,0:T(8,128)S(1)} copy-done((s32[25,32,128]{2,1,0:T(8,128)S(1)}, s32[25,32,128]{2,1,0:T(8,128)}, u32[]{:S(2)}) %copy-start.4) | copy-done | bytes 409624
  7.8 0.0 copy-start.6
  7.8 0.0 copy-start.9
  7.9 0.0 copy-start.1
  7.9 0.0 copy-start.2
  7.9 0.0 copy-start.3
  7.9 0.0 copy-start.5
  7.9 0.2 edge_scales.1.scales
  8.1 0.1 stack.31.where
  8.2 0.0 all-to-all-done
  8.2 0.3 copy-done.6
  8.5 0.0 copy-done.9
  8.5 2.3 %forcing.1.held = f32[25,32,128]{2,1,0:T(8,128)S(1)} custom-call(f32[8,128]{1,0:T(8,128)S(1)} %bitcast.10, s32[8,128]{1,0:T(8,128)S(1)} %bitcast.11, s32[1,8]{1,0:T(1,128)S(1)} %bitcast.12, f32[25,32,128]{2,1,0:T(8,128)} %adjoint_far.1), custom_call_target="tpu_custom_call" | custom-call | flops 100000000 | bytes 8000000 | tf_op jit(solution)/shard_map/forcing/pallas_call | solution.py:321
  10.9 0.0 copy-done.1
  10.9 0.0 copy-done.2
  10.9 0.0 copy-done.3
  10.9 0.0 copy-done.5
  10.9 0.0 copy-start.7
  10.9 0.0 copy-start.8
  10.9 2.9 %first_step.1 = (f32[25,32,128]{2,1,0:T(8,128)}, f32[128,128]{1,0:T(8,128)S(1)}, f32[128,128]{1,0:T(8,128)S(1)}, f32[112,128]{1,0:T(8,128)S(1)}, f32[8,80,128]{2,1,0:T(8,128)}) custom-call(f32[25,32,128]{2,1,0:T(8,128)S(1)} %forcing.1.held, s32[6]{0:T(128)S(1)} %stack.31.where, f32[80,128]{1,0:T(8,128)S(1)} %edge_scales.1.scales, ...), custom_call_target="tpu_custom_call" | custom-call | tf_op jit(solution)/shard_map/first_step/pallas_call | solution.py:337
  13.8 0.0 copy-start.10
  13.8 0.6 %copy-done.10 = f32[128,128]{1,0:T(8,128)} copy-done((f32[128,128]{1,0:T(8,128)}, f32[128,128]{1,0:T(8,128)S(1)}, u32[]{:S(2)}) %copy-start.10) | copy-done | bytes 65560
  14.4 5.7 %all-to-all-start.1 = ((f32[8,80,128]{2,1,0:T(8,128)}), f32[8,80,128]{2,1,0:T(8,128)S(1)}, u32[]{:S(2)}, u32[]{:S(2)}) async-start(f32[8,80,128]{2,1,0:T(8,128)} %get-tuple-element.17), calls=%async_computation.1 | async-start | bytes 655360 | tf_op jit(solution)/shard_map/all_to_all | solution.py:353
  20.2 1.2 %collective-permute-start = (f32[128,128]{1,0:T(8,128)}, f32[128,128]{1,0:T(8,128)S(1)}, u32[]{:S(2)}, u32[]{:S(2)}) collective-permute-start(f32[128,128]{1,0:T(8,128)} %copy-done.10), channel_id=1, source_target_pairs={{0,8},{8,0},{16,24},{24,16},{1,9},{9,1},{17,25},{25,17},{2,10},{10... | collective-permute-start | bytes 196616 | tf_op jit(solution)/shard_map/ppermute | solution.py:355
  21.4 2.1 %collective-permute-start.1 = (f32[128,128]{1,0:T(8,128)S(1)}, f32[128,128]{1,0:T(8,128)S(1)}, u32[]{:S(2)}, u32[]{:S(2)}) collective-permute-start(f32[128,128]{1,0:T(8,128)S(1)} %get-tuple-element.13), channel_id=1, source_target_pairs={{8,16},{16,8},{9,17},{17,9},{10,18},{18,10},{11,19},{19,11},{12,20... | collective-permute-start | bytes 196616 | tf_op jit(solution)/shard_map/ppermute | solution.py:354
  23.5 0.3 collective-permute-done.swapped
  23.8 3.5 %collective-permute-done.1.next_swapped = f32[128,128]{1,0:T(8,128)S(1)} collective-permute-done((f32[128,128]{1,0:T(8,128)S(1)}, f32[128,128]{1,0:T(8,128)S(1)}, u32[]{:S(2)}, u32[]{:S(2)}) %collective-permute-start.1) | collective-permute-done | bytes 65568 | tf_op jit(solution)/shard_map/ppermute | solution.py:354
  27.3 0.7 %corners.1 = (f32[32,128]{1,0:T(8,128)S(1)}, f32[32,128]{1,0:T(8,128)S(1)}) custom-call(f32[128,128]{1,0:T(8,128)S(1)} %collective-permute-done.swapped, f32[128,128]{1,0:T(8,128)S(1)} %collective-permute-done.1.next_swapped, f32[112,128]{1,0:T(8,128)S(1)} %get-tuple-element.14.edges, s32[6]{0:T(128)S(1)} %stack.31.where), custom_call_target="tpu_custom_call" | custom-call | flops 1000000 | bytes 4000000 | tf_op jit(solution)/shard_map/corners/pallas_call | solution.py:357
  28.0 1.9 %collective-permute-start.2 = (f32[32,128]{1,0:T(8,128)S(1)}, f32[32,128]{1,0:T(8,128)S(1)}, u32[]{:S(2)}, u32[]{:S(2)}) collective-permute-start(f32[32,128]{1,0:T(8,128)S(1)} %get-tuple-element.15), channel_id=1, source_target_pairs={{0,1},{1,0},{2,3},{3,2},{4,5},{5,4},{6,7},{7,6},{8,9},{9,8},{10,11... | collective-permute-start | bytes 49160 | tf_op jit(solution)/shard_map/ppermute | solution.py:368
  29.8 0.0 collective-permute-start.3
  29.8 0.8 %collective-permute-done.2.beside = f32[32,128]{1,0:T(8,128)S(1)} collective-permute-done((f32[32,128]{1,0:T(8,128)S(1)}, f32[32,128]{1,0:T(8,128)S(1)}, u32[]{:S(2)}, u32[]{:S(2)}) %collective-permute-start.2) | collective-permute-done | bytes 16416 | tf_op jit(solution)/shard_map/ppermute | solution.py:368
  30.7 4.1 %collective-permute-done.3.next_beside = f32[32,128]{1,0:T(8,128)S(1)} collective-permute-done((f32[32,128]{1,0:T(8,128)S(1)}, f32[32,128]{1,0:T(8,128)S(1)}, u32[]{:S(2)}, u32[]{:S(2)}) %collective-permute-start.3) | collective-permute-done | bytes 16416 | tf_op jit(solution)/shard_map/ppermute | solution.py:367
  34.8 0.0 all-to-all-done.1.got
  34.8 0.0 copy-done.7
  34.8 0.0 copy-done.8
  34.8 3.1 %second_step.1 = f32[25,32,128]{2,1,0:T(8,128)} custom-call(f32[128,128]{1,0:T(8,128)S(1)} %collective-permute-done.swapped, f32[128,128]{1,0:T(8,128)S(1)} %collective-permute-done.1.next_swapped, f32[32,128]{1,0:T(8,128)S(1)} %collective-permute-done.2.beside, f32[32,128]{1,0:T(8,128)S(1)} %collective-permute-done.3.next_beside, ...), custom_call_target="tpu_custom_call", output_to_operand_aliasing={{}: (9, {})} | custom-call | tf_op jit(solution)/shard_map/second_step/pallas_call | solution.py:369
Async XLA Ops:
  0.0 8.2 %all-to-all-start = ((f32[1,1,8,128]{3,1,0,2:T(1,128)}), f32[1,1,8,128]{3,1,0,2:T(1,128)S(1)}, u32[]{:S(2)}, u32[]{:S(2)}) async-start(f32[1,1,8,128]{3,1,0,2:T(1,128)} %bitcast.13), calls=%async_computation | async-start | bytes 8192 | tf_op jit(solution)/shard_map/all_to_all | solution.py:303
  5.4 1.4 %copy-start = (f32[4,25,32,128]{3,2,1,0:T(8,128)S(1)}, f32[4,25,32,128]{3,2,1,0:T(8,128)}, u32[]{:S(2)}) copy-start(f32[4,25,32,128]{3,2,1,0:T(8,128)} %side.5) | copy-start | bytes 4915204
  6.8 1.0 %copy-start.4 = (s32[25,32,128]{2,1,0:T(8,128)S(1)}, s32[25,32,128]{2,1,0:T(8,128)}, u32[]{:S(2)}) copy-start(s32[25,32,128]{2,1,0:T(8,128)} %mask.3) | copy-start | bytes 1228804
  7.8 0.7 %copy-start.6 = (s32[1,1,8,128]{3,2,1,0:T(8,128)S(1)}, s32[1,1,8,128]{3,2,1,0:T(8,128)}, u32[]{:S(2)}) copy-start(s32[1,1,8,128]{3,2,1,0:T(8,128)} %param.16) | copy-start | bytes 12292
  7.8 0.7 %copy-start.9 = (s32[1,1,8]{2,1,0:T(1,128)S(1)}, s32[1,1,8]{2,1,0:T(1,128)}, u32[]{:S(2)}) copy-start(s32[1,1,8]{2,1,0:T(1,128)} %param.17) | copy-start | bytes 100
  7.9 3.0 %copy-start.1 = (f32[4,25,32,128]{3,2,1,0:T(8,128)S(1)}, f32[4,25,32,128]{3,2,1,0:T(8,128)}, u32[]{:S(2)}) copy-start(f32[4,25,32,128]{3,2,1,0:T(8,128)} %side.5) | copy-start | bytes 4915204
  7.9 3.0 %copy-start.2 = (f32[2,25,32,128]{3,2,1,0:T(8,128)S(1)}, f32[2,25,32,128]{3,2,1,0:T(8,128)}, u32[]{:S(2)}) copy-start(f32[2,25,32,128]{3,2,1,0:T(8,128)} %vert.3) | copy-start | bytes 2457604
  7.9 3.0 %copy-start.3 = (f32[25,32,128]{2,1,0:T(8,128)S(1)}, f32[25,32,128]{2,1,0:T(8,128)}, u32[]{:S(2)}) copy-start(f32[25,32,128]{2,1,0:T(8,128)} %centre.3) | copy-start | bytes 1228804
  7.9 3.0 %copy-start.5 = (s32[25,32,128]{2,1,0:T(8,128)S(1)}, s32[25,32,128]{2,1,0:T(8,128)}, u32[]{:S(2)}) copy-start(s32[25,32,128]{2,1,0:T(8,128)} %mask.3) | copy-start | bytes 1228804
  10.9 23.9 %copy-start.7 = (s32[8]{0:T(128)S(1)}, s32[8]{0:T(128)}, u32[]{:S(2)}) copy-start(s32[8]{0:T(128)} %partner.1) | copy-start | bytes 100
  10.9 23.9 %copy-start.8 = (s32[8]{0:T(128)S(1)}, s32[8]{0:T(128)}, u32[]{:S(2)}) copy-start(s32[8]{0:T(128)} %flip.1) | copy-start | bytes 100
  13.8 0.6 %copy-start.10 = (f32[128,128]{1,0:T(8,128)}, f32[128,128]{1,0:T(8,128)S(1)}, u32[]{:S(2)}) copy-start(f32[128,128]{1,0:T(8,128)S(1)} %get-tuple-element.12) | copy-start | bytes 196612
  14.4 20.3 %all-to-all-start.1 = ((f32[8,80,128]{2,1,0:T(8,128)}), f32[8,80,128]{2,1,0:T(8,128)S(1)}, u32[]{:S(2)}, u32[]{:S(2)}) async-start(f32[8,80,128]{2,1,0:T(8,128)} %get-tuple-element.17), calls=%async_computation.1 | async-start | bytes 655360 | tf_op jit(solution)/shard_map/all_to_all | solution.py:353
  20.2 3.6 %collective-permute-start = (f32[128,128]{1,0:T(8,128)}, f32[128,128]{1,0:T(8,128)S(1)}, u32[]{:S(2)}, u32[]{:S(2)}) collective-permute-start(f32[128,128]{1,0:T(8,128)} %copy-done.10), channel_id=1, source_target_pairs={{0,8},{8,0},{16,24},{24,16},{1,9},{9,1},{17,25},{25,17},{2,10},{10... | collective-permute-start | bytes 196616 | tf_op jit(solution)/shard_map/ppermute | solution.py:355
  21.4 5.9 %collective-permute-start.1 = (f32[128,128]{1,0:T(8,128)S(1)}, f32[128,128]{1,0:T(8,128)S(1)}, u32[]{:S(2)}, u32[]{:S(2)}) collective-permute-start(f32[128,128]{1,0:T(8,128)S(1)} %get-tuple-element.13), channel_id=1, source_target_pairs={{8,16},{16,8},{9,17},{17,9},{10,18},{18,10},{11,19},{19,11},{12,20... | collective-permute-start | bytes 196616 | tf_op jit(solution)/shard_map/ppermute | solution.py:354
  28.0 2.7 %collective-permute-start.2 = (f32[32,128]{1,0:T(8,128)S(1)}, f32[32,128]{1,0:T(8,128)S(1)}, u32[]{:S(2)}, u32[]{:S(2)}) collective-permute-start(f32[32,128]{1,0:T(8,128)S(1)} %get-tuple-element.15), channel_id=1, source_target_pairs={{0,1},{1,0},{2,3},{3,2},{4,5},{5,4},{6,7},{7,6},{8,9},{9,8},{10,11... | collective-permute-start | bytes 49160 | tf_op jit(solution)/shard_map/ppermute | solution.py:368
  29.8 5.0 %collective-permute-start.3 = (f32[32,128]{1,0:T(8,128)S(1)}, f32[32,128]{1,0:T(8,128)S(1)}, u32[]{:S(2)}, u32[]{:S(2)}) collective-permute-start(f32[32,128]{1,0:T(8,128)S(1)} %get-tuple-element.16), channel_id=1, source_target_pairs={{1,2},{2,1},{3,4},{4,3},{5,6},{6,5},{7,0},{0,7},{9,10},{10,9},{11,... | collective-permute-start | bytes 49160 | tf_op jit(solution)/shard_map/ppermute | solution.py:367

commit v4 on v3

--- a/solution.py
+++ b/solution.py
@@ -78,7 +78,7 @@
     return eastward, westward
 
 
-def forcing_kernel(sources, misfit, cell, count, adjoint_far, start, hot, valued, forcing, adjoint, arrived):
+def forcing_kernel(sources, misfit, cell, count, adjoint_far, start, hot, valued, adjoint, arrived):
     load = pltpu.make_async_copy(adjoint_far, adjoint, arrived)
     load.start()
     group = min(GROUP, sources)
@@ -101,12 +101,10 @@
         part = lax.dot_general(hot[...], valued[...], (((1,), (1,)), ((), ())), preferred_element_type=jnp.float32)
         part = part[:, 0:COLS] + part[:, COLS : 2 * COLS] + part[:, 2 * COLS : 3 * COLS]
         if first == 0:
-            forcing[...] = part
-        else:
-            forcing[...] += part
-    load.wait()
-    for k in range(LEVELS):
-        start[k] = adjoint[k] + forcing[k * ROWS : (k + 1) * ROWS, :]
+            load.wait()
+        held = adjoint if first == 0 else start
+        for k in range(LEVELS):
+            start[k] = held[k] + part[k * ROWS : (k + 1) * ROWS, :]
 
 
 def to_lanes(column, offset):
@@ -144,7 +142,7 @@
     return pltpu.make_async_copy(source.at[levels], target.at[levels], semaphores.at[i])
 
 
-def first_kernel(held, where, scales, side, centre, vert, mask, part_far, swap, next_swap, edges, slots, part, up, down, base, sent, posted):
+def first_kernel(held, where, scales, side, centre, vert, mask, part_far, swap, next_swap, edges, slots, part, up, down, base, picked, next_picked, sent, posted):
     for i in range(4):
         for ref in (up, down):
             ref[i * PAD + 24 : (i + 1) * PAD, :] = jnp.zeros((8, COLS), jnp.float32)
@@ -172,8 +170,12 @@
     for copy in spread:
         copy.start()
     upward = where[4] == 0
-    swap[...] = jnp.where(upward, up[...], down[...])
-    next_swap[...] = jnp.where(upward, down[...], up[...])
+    picked[...] = jnp.where(upward, up[...], down[...])
+    next_picked[...] = jnp.where(upward, down[...], up[...])
+    spread.append(pltpu.make_async_copy(picked, swap, posted.at[slots.shape[0]]))
+    spread.append(pltpu.make_async_copy(next_picked, next_swap, posted.at[slots.shape[0] + 1]))
+    for copy in spread[-2:]:
+        copy.start()
     for i, p in enumerate(packed):
         edges[8 * i : 8 * i + 8, :], edges[24 + 8 * i : 32 + 8 * i, :] = tight(p)
     edges[16:24, :] = scales[0:8, :]
@@ -205,7 +207,9 @@
         ref[24:EDGE, :] = jnp.where(iota((EDGE - 24, COLS), 0) == 0, corners, 0.0)
 
 
-def second_kernel(swapped, next_swapped, beside, next_beside, edges, got, partner, flip, where, part_far, side, centre, vert, out, held, part, result, lines, near_sides, far_sides, west_side, east_side, loaded, sent):
+def second_kernel(swapped, next_swapped, beside, next_beside, edges, got_far, partner, flip, where, part_far, side, centre, vert, out, held, part, result, lines, near_sides, far_sides, west_side, east_side, got, loaded, sent, gathered):
+    gather = pltpu.make_async_copy(got_far, got, gathered)
+    gather.start()
     for i in range(LEVELS // CHUNK):
         chunk(part_far, part, loaded, i).start()
     sources = got.shape[0]
@@ -231,6 +235,7 @@
         return jnp.where(flip[source] == 1, jnp.take_along_axis(rows, back, axis=1), rows)
 
     level_lane = iota((PAD, COLS), 1)
+    gather.wait()
     source = comes_from(column)
     earlier = comes_from(source)
     before = jnp.where(source == 0, sources - 1, source - 1)
@@ -303,7 +308,7 @@
     received = lax.all_to_all(obs_misfit, "col", split_axis=2, concat_axis=1, tiled=True)
     f32 = jnp.float32
     tile = jax.ShapeDtypeStruct((LEVELS, ROWS, COLS), f32)
-    lines = jax.ShapeDtypeStruct((LINES, COLS), f32)
+    lines = pltpu.HBM((LINES, COLS), f32)
     field = pltpu.VMEM((LEVELS, ROWS, COLS), f32)
     chunks = pltpu.SemaphoreType.DMA((LEVELS // CHUNK,))
     group = min(GROUP, sources)
@@ -326,7 +331,6 @@
         scratch_shapes=[
             pltpu.VMEM((LEVELS * ROWS, group * CAP), jnp.bfloat16),
             pltpu.VMEM((3 * COLS, group * CAP), jnp.bfloat16),
-            pltpu.VMEM((LEVELS * ROWS, COLS), f32),
             field,
             pltpu.SemaphoreType.DMA,
         ],
@@ -338,14 +342,16 @@
         first_kernel,
         out_shape=(tile, lines, lines, jax.ShapeDtypeStruct((EDGES, COLS), f32), pltpu.HBM((sources, SLOT, COLS), f32)),
         in_specs=[VMEM, SMEM] + [VMEM] * 5,
-        out_specs=(FAR,) + (VMEM,) * 3 + (FAR,),
+        out_specs=(FAR, FAR, FAR, VMEM, FAR),
         scratch_shapes=[
             field,
             pltpu.VMEM((LINES, COLS), f32),
             pltpu.VMEM((LINES, COLS), f32),
             pltpu.VMEM((SLOT, COLS), f32),
+            pltpu.VMEM((LINES, COLS), f32),
+            pltpu.VMEM((LINES, COLS), f32),
             chunks,
-            pltpu.SemaphoreType.DMA((sources,)),
+            pltpu.SemaphoreType.DMA((sources + 2,)),
         ],
         compiler_params=pltpu.CompilerParams(vmem_limit_bytes=(8 if small else 24) * MIB),
         name="first_step",
@@ -369,7 +375,7 @@
     return pl.pallas_call(
         second_kernel,
         out_shape=tile,
-        in_specs=[VMEM] * 6 + [SMEM] * 3 + [FAR] + [VMEM] * 3,
+        in_specs=[VMEM] * 5 + [FAR] + [SMEM] * 3 + [FAR] + [VMEM] * 3,
         out_specs=FAR,
         input_output_aliases={9: 0},
         scratch_shapes=[
@@ -381,10 +387,12 @@
             pltpu.VMEM((ROWS, COLS), f32),
             pltpu.VMEM((EDGE, COLS), f32),
             pltpu.VMEM((EDGE, COLS), f32),
+            pltpu.VMEM((sources, SLOT, COLS), f32),
             chunks,
             chunks,
+            pltpu.SemaphoreType.DMA,
         ],
-        compiler_params=pltpu.CompilerParams(vmem_limit_bytes=8 * MIB),
+        compiler_params=pltpu.CompilerParams(vmem_limit_bytes=(8 if small else 24) * MIB),
         name="second_step",
     )(
         swapped,

time: 38.3 us -> 37.9 us (0.990)
  local copies, waits for them, and re-layouts: 3.48 us -> 2.87 us
    unnamed x22 -> x20, local copies, waits for them, and re-layouts: 3.4 us -> 2.79 us
where the time goes in v4:
time: 37.9 us; the launch traced here: 37.5 us
  starting transfers between devices  16.3 us (43%)
  Pallas kernels  9.22 us (24%)
  waiting for transfers between devices  8.97 us (24%)
  local copies, waits for them, and re-layouts  2.87 us (8%)
    all_to_all x1, starting transfers between devices, body(): got = lax.all_to_all(slots, 'col', split_axis=0, concat_axis=0, tiled=True)  5.75 us
    all_to_all x1, starting transfers between devices, body(): lax.all_to_all(obs_misfit, 'col', split_axis=2, concat_axis=1, tiled=True)  5.41 us
    ppermute x1, waiting for transfers between devices, body(): lax.ppermute(next_beside, 'col', swaps(1, sources - 1) + round_trip)  4.12 us
    ppermute x1, waiting for transfers between devices, body(): next_swapped = lax.ppermute(next_swap, 'tile', swaps(1, tiles - 1))  3.69 us
    pallas_call x1, Pallas kernels, body(): pl.pallas_call(second_kernel, out_shape=tile, in_specs=[VMEM] * 5 + [FAR]...  3.06 us
    pallas_call x1, Pallas kernels, body(): pl.pallas_call(first_kernel, out_shape=(tile, lines, lines, jax.ShapeDtyp...  2.95 us
    unnamed x20, local copies, waits for them, and re-layouts  2.79 us
    pallas_call x1, Pallas kernels, body(): pl.pallas_call(functools.partial(forcing_kernel, sources), out_shape=tile...  2.31 us
  transfers between devices with their start and end apart: 6, of which 4 were waited for; matrix products, arithmetic and copies ran while one was open for 0% of the time, Pallas kernels for 2%

profile of v4, /device:TPU:29, one launch (start us, length us, event | category | flops | bytes accessed | tf_op | source)
XLA Modules:
  0.0 37.5 jit_solution(8793756620830843509)
XLA Ops:
  0.0 5.4 %all-to-all-start = ((f32[1,1,8,128]{3,1,0,2:T(1,128)}), f32[1,1,8,128]{3,1,0,2:T(1,128)S(1)}, u32[]{:S(2)}, u32[]{:S(2)}) async-start(f32[1,1,8,128]{3,1,0,2:T(1,128)} %bitcast.13), calls=%async_computation | async-start | bytes 8192 | tf_op jit(solution)/shard_map/all_to_all | solution.py:308
  5.4 0.0 copy-start
  5.4 1.4 %copy-done = f32[4,25,32,128]{3,2,1,0:T(8,128)S(1)} copy-done((f32[4,25,32,128]{3,2,1,0:T(8,128)S(1)}, f32[4,25,32,128]{3,2,1,0:T(8,128)}, u32[]{:S(2)}) %copy-start) | copy-done | bytes 1638424
  6.8 0.0 copy-start.4
  6.8 1.0 %copy-done.4 = s32[25,32,128]{2,1,0:T(8,128)S(1)} copy-done((s32[25,32,128]{2,1,0:T(8,128)S(1)}, s32[25,32,128]{2,1,0:T(8,128)}, u32[]{:S(2)}) %copy-start.4) | copy-done | bytes 409624
  7.8 0.0 copy-start.6
  7.8 0.0 copy-start.9
  7.9 0.0 copy-start.1
  7.9 0.0 copy-start.2
  7.9 0.0 copy-start.3
  7.9 0.0 copy-start.5
  7.9 0.2 edge_scales.1.scales
  8.1 0.1 stack.31.where
  8.2 0.0 all-to-all-done
  8.2 0.3 copy-done.6
  8.5 0.0 copy-done.9
  8.5 2.3 %forcing.1.held = f32[25,32,128]{2,1,0:T(8,128)S(1)} custom-call(f32[8,128]{1,0:T(8,128)S(1)} %bitcast.10, s32[8,128]{1,0:T(8,128)S(1)} %bitcast.11, s32[1,8]{1,0:T(1,128)S(1)} %bitcast.12, f32[25,32,128]{2,1,0:T(8,128)} %adjoint_far.1), custom_call_target="tpu_custom_call" | custom-call | flops 100000000 | bytes 8000000 | tf_op jit(solution)/shard_map/forcing/pallas_call | solution.py:326
  10.9 0.0 copy-done.1
  10.9 0.0 copy-done.2
  10.9 0.0 copy-done.3
  10.9 0.0 copy-done.5
  10.9 0.0 copy-start.7
  10.9 0.0 copy-start.8
  10.9 2.9 %first_step.1 = (f32[25,32,128]{2,1,0:T(8,128)}, f32[128,128]{1,0:T(8,128)}, f32[128,128]{1,0:T(8,128)}, f32[112,128]{1,0:T(8,128)S(1)}, f32[8,80,128]{2,1,0:T(8,128)}) custom-call(f32[25,32,128]{2,1,0:T(8,128)S(1)} %forcing.1.held, s32[6]{0:T(128)S(1)} %stack.31.where, f32[80,128]{1,0:T(8,128)S(1)} %edge_scales.1.scales, f32[4,25,32,128]{3,2,1,0:T(8,128)S(1)} %copy-done.1, ...), custom_call_target="tpu_custom_call" | custom-call | tf_op jit(solution)/shard_map/first_step/pallas_call | solution.py:341
  13.9 5.7 %all-to-all-start.1 = ((f32[8,80,128]{2,1,0:T(8,128)}), f32[8,80,128]{2,1,0:T(8,128)S(1)}, u32[]{:S(2)}, u32[]{:S(2)}) async-start(f32[8,80,128]{2,1,0:T(8,128)} %get-tuple-element.17), calls=%async_computation.1 | async-start | bytes 655360 | tf_op jit(solution)/shard_map/all_to_all | solution.py:359
  19.6 1.2 %collective-permute-start = (f32[128,128]{1,0:T(8,128)}, f32[128,128]{1,0:T(8,128)S(1)}, u32[]{:S(2)}, u32[]{:S(2)}) collective-permute-start(f32[128,128]{1,0:T(8,128)} %get-tuple-element.12), channel_id=1, source_target_pairs={{0,8},{8,0},{16,24},{24,16},{1,9},{9,1},{17,25},{25,17},{2,10},{10... | collective-permute-start | bytes 196616 | tf_op jit(solution)/shard_map/ppermute | solution.py:361
  20.8 2.1 %collective-permute-start.1 = (f32[128,128]{1,0:T(8,128)}, f32[128,128]{1,0:T(8,128)S(1)}, u32[]{:S(2)}, u32[]{:S(2)}) collective-permute-start(f32[128,128]{1,0:T(8,128)} %get-tuple-element.13), channel_id=1, source_target_pairs={{8,16},{16,8},{9,17},{17,9},{10,18},{18,10},{11,19},{19,11},{12,20... | collective-permute-start | bytes 196616 | tf_op jit(solution)/shard_map/ppermute | solution.py:360
  22.9 0.3 collective-permute-done.swapped
  23.2 3.7 %collective-permute-done.1.next_swapped = f32[128,128]{1,0:T(8,128)S(1)} collective-permute-done((f32[128,128]{1,0:T(8,128)}, f32[128,128]{1,0:T(8,128)S(1)}, u32[]{:S(2)}, u32[]{:S(2)}) %collective-permute-start.1) | collective-permute-done | bytes 65568 | tf_op jit(solution)/shard_map/ppermute | solution.py:360
  26.9 0.7 %corners.1 = (f32[32,128]{1,0:T(8,128)S(1)}, f32[32,128]{1,0:T(8,128)S(1)}) custom-call(f32[128,128]{1,0:T(8,128)S(1)} %collective-permute-done.swapped, f32[128,128]{1,0:T(8,128)S(1)} %collective-permute-done.1.next_swapped, f32[112,128]{1,0:T(8,128)S(1)} %get-tuple-element.14.edges, s32[6]{0:T(128)S(1)} %stack.31.where), custom_call_target="tpu_custom_call" | custom-call | flops 1000000 | bytes 4000000 | tf_op jit(solution)/shard_map/corners/pallas_call | solution.py:363
  27.6 1.9 %collective-permute-start.2 = (f32[32,128]{1,0:T(8,128)S(1)}, f32[32,128]{1,0:T(8,128)S(1)}, u32[]{:S(2)}, u32[]{:S(2)}) collective-permute-start(f32[32,128]{1,0:T(8,128)S(1)} %get-tuple-element.15), channel_id=1, source_target_pairs={{0,1},{1,0},{2,3},{3,2},{4,5},{5,4},{6,7},{7,6},{8,9},{9,8},{10,11... | collective-permute-start | bytes 49160 | tf_op jit(solution)/shard_map/ppermute | solution.py:374
  29.5 0.0 collective-permute-start.3
  29.5 0.8 %collective-permute-done.2.beside = f32[32,128]{1,0:T(8,128)S(1)} collective-permute-done((f32[32,128]{1,0:T(8,128)S(1)}, f32[32,128]{1,0:T(8,128)S(1)}, u32[]{:S(2)}, u32[]{:S(2)}) %collective-permute-start.2) | collective-permute-done | bytes 16416 | tf_op jit(solution)/shard_map/ppermute | solution.py:374
  30.3 4.1 %collective-permute-done.3.next_beside = f32[32,128]{1,0:T(8,128)S(1)} collective-permute-done((f32[32,128]{1,0:T(8,128)S(1)}, f32[32,128]{1,0:T(8,128)S(1)}, u32[]{:S(2)}, u32[]{:S(2)}) %collective-permute-start.3) | collective-permute-done | bytes 16416 | tf_op jit(solution)/shard_map/ppermute | solution.py:373
  34.4 0.0 all-to-all-done.1.got_far
  34.4 0.0 copy-done.7
  34.4 0.0 copy-done.8
  34.4 3.1 %second_step.1 = f32[25,32,128]{2,1,0:T(8,128)} custom-call(f32[128,128]{1,0:T(8,128)S(1)} %collective-permute-done.swapped, f32[128,128]{1,0:T(8,128)S(1)} %collective-permute-done.1.next_swapped, f32[32,128]{1,0:T(8,128)S(1)} %collective-permute-done.2.beside, f32[32,128]{1,0:T(8,128)S(1)} %collective-permute-done.3.next_beside, ...), custom_call_target="tpu_custom_call", output_to_operand_aliasing={{}: (9, {})} | custom-call | tf_op jit(solution)/shard_map/second_step/pallas_call | solution.py:375
Async XLA Ops:
  0.0 8.2 %all-to-all-start = ((f32[1,1,8,128]{3,1,0,2:T(1,128)}), f32[1,1,8,128]{3,1,0,2:T(1,128)S(1)}, u32[]{:S(2)}, u32[]{:S(2)}) async-start(f32[1,1,8,128]{3,1,0,2:T(1,128)} %bitcast.13), calls=%async_computation | async-start | bytes 8192 | tf_op jit(solution)/shard_map/all_to_all | solution.py:308
  5.4 1.4 %copy-start = (f32[4,25,32,128]{3,2,1,0:T(8,128)S(1)}, f32[4,25,32,128]{3,2,1,0:T(8,128)}, u32[]{:S(2)}) copy-start(f32[4,25,32,128]{3,2,1,0:T(8,128)} %side.5) | copy-start | bytes 4915204
  6.8 1.0 %copy-start.4 = (s32[25,32,128]{2,1,0:T(8,128)S(1)}, s32[25,32,128]{2,1,0:T(8,128)}, u32[]{:S(2)}) copy-start(s32[25,32,128]{2,1,0:T(8,128)} %mask.3) | copy-start | bytes 1228804
  7.8 0.7 %copy-start.6 = (s32[1,1,8,128]{3,2,1,0:T(8,128)S(1)}, s32[1,1,8,128]{3,2,1,0:T(8,128)}, u32[]{:S(2)}) copy-start(s32[1,1,8,128]{3,2,1,0:T(8,128)} %param.16) | copy-start | bytes 12292
  7.8 0.7 %copy-start.9 = (s32[1,1,8]{2,1,0:T(1,128)S(1)}, s32[1,1,8]{2,1,0:T(1,128)}, u32[]{:S(2)}) copy-start(s32[1,1,8]{2,1,0:T(1,128)} %param.17) | copy-start | bytes 100
  7.9 3.0 %copy-start.1 = (f32[4,25,32,128]{3,2,1,0:T(8,128)S(1)}, f32[4,25,32,128]{3,2,1,0:T(8,128)}, u32[]{:S(2)}) copy-start(f32[4,25,32,128]{3,2,1,0:T(8,128)} %side.5) | copy-start | bytes 4915204
  7.9 3.0 %copy-start.2 = (f32[2,25,32,128]{3,2,1,0:T(8,128)S(1)}, f32[2,25,32,128]{3,2,1,0:T(8,128)}, u32[]{:S(2)}) copy-start(f32[2,25,32,128]{3,2,1,0:T(8,128)} %vert.3) | copy-start | bytes 2457604
  7.9 3.0 %copy-start.3 = (f32[25,32,128]{2,1,0:T(8,128)S(1)}, f32[25,32,128]{2,1,0:T(8,128)}, u32[]{:S(2)}) copy-start(f32[25,32,128]{2,1,0:T(8,128)} %centre.3) | copy-start | bytes 1228804
  7.9 3.0 %copy-start.5 = (s32[25,32,128]{2,1,0:T(8,128)S(1)}, s32[25,32,128]{2,1,0:T(8,128)}, u32[]{:S(2)}) copy-start(s32[25,32,128]{2,1,0:T(8,128)} %mask.3) | copy-start | bytes 1228804
  10.9 23.5 %copy-start.7 = (s32[8]{0:T(128)S(1)}, s32[8]{0:T(128)}, u32[]{:S(2)}) copy-start(s32[8]{0:T(128)} %partner.1) | copy-start | bytes 100
  10.9 23.5 %copy-start.8 = (s32[8]{0:T(128)S(1)}, s32[8]{0:T(128)}, u32[]{:S(2)}) copy-start(s32[8]{0:T(128)} %flip.1) | copy-start | bytes 100
  13.9 20.6 %all-to-all-start.1 = ((f32[8,80,128]{2,1,0:T(8,128)}), f32[8,80,128]{2,1,0:T(8,128)S(1)}, u32[]{:S(2)}, u32[]{:S(2)}) async-start(f32[8,80,128]{2,1,0:T(8,128)} %get-tuple-element.17), calls=%async_computation.1 | async-start | bytes 655360 | tf_op jit(solution)/shard_map/all_to_all | solution.py:359
  19.6 3.6 %collective-permute-start = (f32[128,128]{1,0:T(8,128)}, f32[128,128]{1,0:T(8,128)S(1)}, u32[]{:S(2)}, u32[]{:S(2)}) collective-permute-start(f32[128,128]{1,0:T(8,128)} %get-tuple-element.12), channel_id=1, source_target_pairs={{0,8},{8,0},{16,24},{24,16},{1,9},{9,1},{17,25},{25,17},{2,10},{10... | collective-permute-start | bytes 196616 | tf_op jit(solution)/shard_map/ppermute | solution.py:361
  20.8 6.1 %collective-permute-start.1 = (f32[128,128]{1,0:T(8,128)}, f32[128,128]{1,0:T(8,128)S(1)}, u32[]{:S(2)}, u32[]{:S(2)}) collective-permute-start(f32[128,128]{1,0:T(8,128)} %get-tuple-element.13), channel_id=1, source_target_pairs={{8,16},{16,8},{9,17},{17,9},{10,18},{18,10},{11,19},{19,11},{12,20... | collective-permute-start | bytes 196616 | tf_op jit(solution)/shard_map/ppermute | solution.py:360
  27.6 2.7 %collective-permute-start.2 = (f32[32,128]{1,0:T(8,128)S(1)}, f32[32,128]{1,0:T(8,128)S(1)}, u32[]{:S(2)}, u32[]{:S(2)}) collective-permute-start(f32[32,128]{1,0:T(8,128)S(1)} %get-tuple-element.15), channel_id=1, source_target_pairs={{0,1},{1,0},{2,3},{3,2},{4,5},{5,4},{6,7},{7,6},{8,9},{9,8},{10,11... | collective-permute-start | bytes 49160 | tf_op jit(solution)/shard_map/ppermute | solution.py:374
  29.5 5.0 %collective-permute-start.3 = (f32[32,128]{1,0:T(8,128)S(1)}, f32[32,128]{1,0:T(8,128)S(1)}, u32[]{:S(2)}, u32[]{:S(2)}) collective-permute-start(f32[32,128]{1,0:T(8,128)S(1)} %get-tuple-element.16), channel_id=1, source_target_pairs={{1,2},{2,1},{3,4},{4,3},{5,6},{6,5},{7,0},{0,7},{9,10},{10,9},{11,... | collective-permute-start | bytes 49160 | tf_op jit(solution)/shard_map/ppermute | solution.py:373

commit v5 on v4

--- a/solution.py
+++ b/solution.py
@@ -14,7 +14,6 @@
 GROUP = 8
 CHUNK = 5
 PAD = 32
-LINES = 4 * PAD
 CORNER = 3 * LEVELS
 SLOT = 80
 EDGE = 32
@@ -89,17 +88,16 @@
             cells = cell[first + s : first + s + 1, :]
             v = jnp.where(lane < count[0, first + s], misfit[first + s : first + s + 1, :], 0.0)
             high = v.astype(jnp.bfloat16).astype(jnp.float32)
-            middle = (v - high).astype(jnp.bfloat16).astype(jnp.float32)
-            low = v - high - middle
+            low = v - high
             column = iota((COLS, CAP), 0) == (cells & (COLS - 1))
-            for i, part in enumerate((high, middle, low)):
+            for i, part in enumerate((high, low)):
                 valued[i * COLS : (i + 1) * COLS, at] = jnp.where(column, part, 0.0).astype(jnp.bfloat16)
             place = cells >> 7
             for k in range(LEVELS):
                 match = (iota((ROWS, CAP), 0) + k * ROWS) == place
                 hot[k * ROWS : (k + 1) * ROWS, at] = jnp.where(match, 1.0, 0.0).astype(jnp.bfloat16)
         part = lax.dot_general(hot[...], valued[...], (((1,), (1,)), ((), ())), preferred_element_type=jnp.float32)
-        part = part[:, 0:COLS] + part[:, COLS : 2 * COLS] + part[:, 2 * COLS : 3 * COLS]
+        part = part[:, 0:COLS] + part[:, COLS : 2 * COLS]
         if first == 0:
             load.wait()
         held = adjoint if first == 0 else start
@@ -128,13 +126,10 @@
     return block[:, COLS - 1 : COLS], block[:, 0:1]
 
 
-def from_tiles(swapped, next_swapped, where, start):
-    rows = slice(start, start + PAD)
+def from_tiles(swapped, next_swapped, where, rows):
     upward = where[4] == 0
-    return (
-        jnp.where(upward, next_swapped[rows, :], swapped[rows, :]),
-        jnp.where(upward, swapped[rows, :], next_swapped[rows, :]),
-    )
+    first, second = swapped[rows, :], next_swapped[rows, :]
+    return jnp.where(upward, second, first), jnp.where(upward, first, second)
 
 
 def chunk(source, target, semaphores, i):
@@ -142,31 +137,29 @@
     return pltpu.make_async_copy(source.at[levels], target.at[levels], semaphores.at[i])
 
 
-def first_kernel(held, where, scales, side, centre, vert, mask, part_far, swap, next_swap, edges, slots, part, up, down, base, picked, next_picked, sent, posted):
-    for i in range(4):
-        for ref in (up, down):
-            ref[i * PAD + 24 : (i + 1) * PAD, :] = jnp.zeros((8, COLS), jnp.float32)
+def first_kernel(held, where, scales, side, centre, vert, mask, part_far, swap, next_swap, edges, slots, part, up, down, tips, picked, next_picked, sent, posted):
+    for ref in (up, down):
+        ref[CORNER + 1 : SLOT, :] = jnp.zeros((SLOT - CORNER - 1, COLS), jnp.float32)
+    for i in range(2):
+        tips[i * PAD + 24 : (i + 1) * PAD, :] = jnp.zeros((8, COLS), jnp.float32)
     lane = iota((ROWS, COLS), 1)
     packed = [jnp.zeros((ROWS, COLS), jnp.float32)] * 2
     for k in range(LEVELS):
         r, east, west, north, south = terms(k, held, centre, side, vert)
         part[k] = jnp.where(mask[k] == 0, LAND, r)
         sides = outer(lane, east, west)
-        for ref, leaving, at in ((up, north[0:1], ROWS - 1), (down, south[ROWS - 1 : ROWS], 0)):
+        for i, (ref, leaving, at) in enumerate(((up, north[0:1], ROWS - 1), (down, south[ROWS - 1 : ROWS], 0))):
             ref[k : k + 1, :] = leaving
-            ref[PAD + k : PAD + k + 1, :] = r[at : at + 1]
-            ref[3 * PAD + k : 3 * PAD + k + 1, :] = sides[at : at + 1]
+            ref[LEVELS + k : LEVELS + k + 1, :] = r[at : at + 1]
+            tips[i * PAD + k : i * PAD + k + 1, :] = sides[at : at + 1]
         packed = [p + turn(x, 2 * k + 1) for p, x in zip(packed, (sides, outer(lane, r, r)))]
         if (k + 1) % CHUNK == 0:
             chunk(part, part_far, sent, k // CHUNK).start()
-    up[2 * PAD : 3 * PAD, :] = scales[16 : 16 + PAD, :]
-    down[2 * PAD : 3 * PAD, :] = scales[16 + PAD : 16 + 2 * PAD, :]
-    for i in range(3):
-        base[i * LEVELS : (i + 1) * LEVELS, :] = up[i * PAD : i * PAD + LEVELS, :]
-    own_east, own_west = ends(up[3 * PAD : 4 * PAD, :])
-    base[CORNER : CORNER + 1, :] = to_lanes(own_east, OFFSET[0]) + to_lanes(own_west, OFFSET[1])
-    base[CORNER + 1 : SLOT, :] = jnp.zeros((SLOT - CORNER - 1, COLS), jnp.float32)
-    spread = [pltpu.make_async_copy(base, slots.at[s], posted.at[s]) for s in range(slots.shape[0])]
+    for i, ref in enumerate((up, down)):
+        ref[2 * LEVELS : 3 * LEVELS, :] = scales[16 + i * PAD : 16 + i * PAD + LEVELS, :]
+        east, west = ends(tips[i * PAD : (i + 1) * PAD, :])
+        ref[CORNER : CORNER + 1, :] = to_lanes(east, OFFSET[0]) + to_lanes(west, OFFSET[1])
+    spread = [pltpu.make_async_copy(up, slots.at[s], posted.at[s]) for s in range(slots.shape[0])]
     for copy in spread:
         copy.start()
     upward = where[4] == 0
@@ -189,15 +182,13 @@
 
 
 def corner_kernel(swapped, next_swapped, edges, where, swap, next_swap):
-    low, high = from_tiles(swapped, next_swapped, where, 0)
-    low_sides, high_sides = from_tiles(swapped, next_swapped, where, 3 * PAD)
+    low, high = from_tiles(swapped, next_swapped, where, slice(0, PAD))
+    low_tips, high_tips = from_tiles(swapped, next_swapped, where, slice(CORNER, CORNER + 1))
     low_last, low_first = ends(low)
     high_last, high_first = ends(high)
-    low_east, low_west = ends(low_sides)
-    high_east, high_west = ends(high_sides)
-    corners = (
-        to_lanes(low_east, OFFSET[0]) + to_lanes(low_west, OFFSET[1]) + to_lanes(high_west, OFFSET[2]) + to_lanes(high_east, OFFSET[3])
-    )
+    eastern = iota((1, COLS), 1) < OFFSET[1]
+    corners = low_tips + turn(jnp.where(eastern, high_tips, 0.0), OFFSET[3] - OFFSET[0])
+    corners = corners + turn(jnp.where(eastern, 0.0, high_tips), OFFSET[2] - OFFSET[1])
     eastward = spot_rows(to_lanes(low_last, OFFSET[0]), to_lanes(high_last, OFFSET[3]))
     westward = spot_rows(to_lanes(low_first, OFFSET[0]), to_lanes(high_first, OFFSET[3]))
     to_east = where[5] == 0
@@ -213,9 +204,12 @@
     for i in range(LEVELS // CHUNK):
         chunk(part_far, part, loaded, i).start()
     sources = got.shape[0]
-    below_near, above_near = from_tiles(swapped, next_swapped, where, 0)
-    below_part, above_part = from_tiles(swapped, next_swapped, where, PAD)
-    below_scale, above_scale = from_tiles(swapped, next_swapped, where, 2 * PAD)
+    below_near, above_near = from_tiles(swapped, next_swapped, where, slice(0, PAD))
+    below_part, above_part = from_tiles(swapped, next_swapped, where, slice(LEVELS, LEVELS + PAD))
+    below_scale, above_scale = (
+        turn(rows, SLOT - PAD - 2 * LEVELS, 0)
+        for rows in from_tiles(swapped, next_swapped, where, slice(SLOT - PAD, SLOT))
+    )
     sum_low = below_part + edges[48 : 48 + PAD, :]
     sum_high = above_part + edges[48 + PAD : EDGES, :]
     even_column = where[5] == 0
@@ -308,7 +302,7 @@
     received = lax.all_to_all(obs_misfit, "col", split_axis=2, concat_axis=1, tiled=True)
     f32 = jnp.float32
     tile = jax.ShapeDtypeStruct((LEVELS, ROWS, COLS), f32)
-    lines = pltpu.HBM((LINES, COLS), f32)
+    lines = pltpu.HBM((SLOT, COLS), f32)
     field = pltpu.VMEM((LEVELS, ROWS, COLS), f32)
     chunks = pltpu.SemaphoreType.DMA((LEVELS // CHUNK,))
     group = min(GROUP, sources)
@@ -330,7 +324,7 @@
         out_specs=VMEM,
         scratch_shapes=[
             pltpu.VMEM((LEVELS * ROWS, group * CAP), jnp.bfloat16),
-            pltpu.VMEM((3 * COLS, group * CAP), jnp.bfloat16),
+            pltpu.VMEM((2 * COLS, group * CAP), jnp.bfloat16),
             field,
             pltpu.SemaphoreType.DMA,
         ],
@@ -345,11 +339,11 @@
         out_specs=(FAR, FAR, FAR, VMEM, FAR),
         scratch_shapes=[
             field,
-            pltpu.VMEM((LINES, COLS), f32),
-            pltpu.VMEM((LINES, COLS), f32),
             pltpu.VMEM((SLOT, COLS), f32),
-            pltpu.VMEM((LINES, COLS), f32),
-            pltpu.VMEM((LINES, COLS), f32),
+            pltpu.VMEM((SLOT, COLS), f32),
+            pltpu.VMEM((2 * PAD, COLS), f32),
+            pltpu.VMEM((SLOT, COLS), f32),
+            pltpu.VMEM((SLOT, COLS), f32),
             chunks,
             pltpu.SemaphoreType.DMA((sources + 2,)),
         ],

time: 37.9 us -> 37.2 us (0.982)
  Pallas kernels: 9.22 us -> 8.8 us
    pallas_call x1, Pallas kernels: 2.31 us -> 1.82 us  [body(): pl.pallas_call(functools.partial(forcing_kernel, sources), out_shape=tile...]
  transfers between devices with their start and end apart: 6 -> 6, of which waited for: 4 -> 3; matrix products, arithmetic and copies ran while one was open for 0% -> 0% of each run, Pallas kernels for 2% -> 2%
where the time goes in v5:
time: 37.2 us; the launch traced here: 36.8 us
  starting transfers between devices  16.3 us (44%)
  Pallas kernels  8.8 us (24%)
  waiting for transfers between devices  8.71 us (23%)
  local copies, waits for them, and re-layouts  2.87 us (8%)
    all_to_all x1, starting transfers between devices, body(): got = lax.all_to_all(slots, 'col', split_axis=0, concat_axis=0, tiled=True)  5.75 us
    all_to_all x1, starting transfers between devices, body(): lax.all_to_all(obs_misfit, 'col', split_axis=2, concat_axis=1, tiled=True)  5.41 us
    ppermute x1, waiting for transfers between devices, body(): lax.ppermute(next_beside, 'col', swaps(1, sources - 1) + round_trip)  4.12 us
    ppermute x1, waiting for transfers between devices, body(): next_swapped = lax.ppermute(next_swap, 'tile', swaps(1, tiles - 1))  3.7 us
    pallas_call x1, Pallas kernels, body(): pl.pallas_call(second_kernel, out_shape=tile, in_specs=[VMEM] * 5 + [FAR]...  3.06 us
    pallas_call x1, Pallas kernels, body(): pl.pallas_call(first_kernel, out_shape=(tile, lines, lines, jax.ShapeDtyp...  3.03 us
    unnamed x20, local copies, waits for them, and re-layouts  2.79 us
    ppermute x1, starting transfers between devices, body(): next_swapped = lax.ppermute(next_swap, 'tile', swaps(1, tiles - 1))  2.09 us
  transfers between devices with their start and end apart: 6, of which 3 were waited for; matrix products, arithmetic and copies ran while one was open for 0% of the time, Pallas kernels for 2%

profile of v5, /device:TPU:29, one launch (start us, length us, event | category | flops | bytes accessed | tf_op | source)
XLA Modules:
  0.0 36.8 jit_solution(9735759999360470276)
XLA Ops:
  0.0 5.4 %all-to-all-start = ((f32[1,1,8,128]{3,1,0,2:T(1,128)}), f32[1,1,8,128]{3,1,0,2:T(1,128)S(1)}, u32[]{:S(2)}, u32[]{:S(2)}) async-start(f32[1,1,8,128]{3,1,0,2:T(1,128)} %bitcast.13), calls=%async_computation | async-start | bytes 8192 | tf_op jit(solution)/shard_map/all_to_all | solution.py:302
  5.4 0.0 copy-start
  5.4 1.4 %copy-done = f32[4,25,32,128]{3,2,1,0:T(8,128)S(1)} copy-done((f32[4,25,32,128]{3,2,1,0:T(8,128)S(1)}, f32[4,25,32,128]{3,2,1,0:T(8,128)}, u32[]{:S(2)}) %copy-start) | copy-done | bytes 1638424
  6.8 0.0 copy-start.4
  6.8 1.0 %copy-done.4 = s32[25,32,128]{2,1,0:T(8,128)S(1)} copy-done((s32[25,32,128]{2,1,0:T(8,128)S(1)}, s32[25,32,128]{2,1,0:T(8,128)}, u32[]{:S(2)}) %copy-start.4) | copy-done | bytes 409624
  7.8 0.0 copy-start.6
  7.8 0.0 copy-start.9
  7.9 0.0 copy-start.1
  7.9 0.0 copy-start.2
  7.9 0.0 copy-start.3
  7.9 0.0 copy-start.5
  7.9 0.2 edge_scales.1.scales
  8.1 0.1 stack.31.where
  8.2 0.0 all-to-all-done
  8.2 0.3 copy-done.6
  8.5 0.0 copy-done.9
  8.5 1.8 %forcing.1.held = f32[25,32,128]{2,1,0:T(8,128)S(1)} custom-call(f32[8,128]{1,0:T(8,128)S(1)} %bitcast.10, s32[8,128]{1,0:T(8,128)S(1)} %bitcast.11, s32[1,8]{1,0:T(1,128)S(1)} %bitcast.12, f32[25,32,128]{2,1,0:T(8,128)} %adjoint_far.1), custom_call_target="tpu_custom_call" | custom-call | flops 100000000 | bytes 8000000 | tf_op jit(solution)/shard_map/forcing/pallas_call | solution.py:320
  10.4 0.0 copy-done.1
  10.4 0.0 copy-done.2
  10.4 0.0 copy-done.3
  10.4 0.0 copy-done.5
  10.4 0.0 copy-start.7
  10.4 0.0 copy-start.8
  10.4 3.0 %first_step.1 = (f32[25,32,128]{2,1,0:T(8,128)}, f32[80,128]{1,0:T(8,128)}, f32[80,128]{1,0:T(8,128)}, f32[112,128]{1,0:T(8,128)S(1)}, f32[8,80,128]{2,1,0:T(8,128)}) custom-call(f32[25,32,128]{2,1,0:T(8,128)S(1)} %forcing.1.held, s32[6]{0:T(128)S(1)} %stack.31.where, f32[80,128]{1,0:T(8,128)S(1)} %edge_scales.1.scales, f32[4,25,32,128]{3,2,1,0:T(8,128)S(1)} %copy-done.1, ...), custom_call_target="tpu_custom_call" | custom-call | tf_op jit(solution)/shard_map/first_step/pallas_call | solution.py:335
  13.5 5.7 %all-to-all-start.1 = ((f32[8,80,128]{2,1,0:T(8,128)}), f32[8,80,128]{2,1,0:T(8,128)S(1)}, u32[]{:S(2)}, u32[]{:S(2)}) async-start(f32[8,80,128]{2,1,0:T(8,128)} %get-tuple-element.17), calls=%async_computation.1 | async-start | bytes 655360 | tf_op jit(solution)/shard_map/all_to_all | solution.py:353
  19.2 1.2 %collective-permute-start = (f32[80,128]{1,0:T(8,128)}, f32[80,128]{1,0:T(8,128)S(1)}, u32[]{:S(2)}, u32[]{:S(2)}) collective-permute-start(f32[80,128]{1,0:T(8,128)} %get-tuple-element.12), channel_id=1, source_target_pairs={{0,8},{8,0},{16,24},{24,16},{1,9},{9,1},{17,25},{25,17},{2,10},{10... | collective-permute-start | bytes 122888 | tf_op jit(solution)/shard_map/ppermute | solution.py:355
  20.4 2.1 %collective-permute-start.1 = (f32[80,128]{1,0:T(8,128)}, f32[80,128]{1,0:T(8,128)S(1)}, u32[]{:S(2)}, u32[]{:S(2)}) collective-permute-start(f32[80,128]{1,0:T(8,128)} %get-tuple-element.13), channel_id=1, source_target_pairs={{8,16},{16,8},{9,17},{17,9},{10,18},{18,10},{11,19},{19,11},{12,20... | collective-permute-start | bytes 122888 | tf_op jit(solution)/shard_map/ppermute | solution.py:354
  22.5 0.0 collective-permute-done.swapped
  22.6 3.7 %collective-permute-done.1.next_swapped = f32[80,128]{1,0:T(8,128)S(1)} collective-permute-done((f32[80,128]{1,0:T(8,128)}, f32[80,128]{1,0:T(8,128)S(1)}, u32[]{:S(2)}, u32[]{:S(2)}) %collective-permute-start.1) | collective-permute-done | bytes 40992 | tf_op jit(solution)/shard_map/ppermute | solution.py:354
  26.3 0.6 %corners.1 = (f32[32,128]{1,0:T(8,128)S(1)}, f32[32,128]{1,0:T(8,128)S(1)}) custom-call(f32[80,128]{1,0:T(8,128)S(1)} %collective-permute-done.swapped, f32[80,128]{1,0:T(8,128)S(1)} %collective-permute-done.1.next_swapped, f32[112,128]{1,0:T(8,128)S(1)} %get-tuple-element.14.edges, s32[6]{0:T(128)S(1)} %stack.31.where), custom_call_target="tpu_custom_call" | custom-call | flops 1000000 | bytes 4000000 | tf_op jit(solution)/shard_map/corners/pallas_call | solution.py:357
  26.9 1.9 %collective-permute-start.2 = (f32[32,128]{1,0:T(8,128)S(1)}, f32[32,128]{1,0:T(8,128)S(1)}, u32[]{:S(2)}, u32[]{:S(2)}) collective-permute-start(f32[32,128]{1,0:T(8,128)S(1)} %get-tuple-element.15), channel_id=1, source_target_pairs={{0,1},{1,0},{2,3},{3,2},{4,5},{5,4},{6,7},{7,6},{8,9},{9,8},{10,11... | collective-permute-start | bytes 49160 | tf_op jit(solution)/shard_map/ppermute | solution.py:368
  28.8 0.0 collective-permute-start.3
  28.8 0.8 %collective-permute-done.2.beside = f32[32,128]{1,0:T(8,128)S(1)} collective-permute-done((f32[32,128]{1,0:T(8,128)S(1)}, f32[32,128]{1,0:T(8,128)S(1)}, u32[]{:S(2)}, u32[]{:S(2)}) %collective-permute-start.2) | collective-permute-done | bytes 16416 | tf_op jit(solution)/shard_map/ppermute | solution.py:368
  29.6 4.1 %collective-permute-done.3.next_beside = f32[32,128]{1,0:T(8,128)S(1)} collective-permute-done((f32[32,128]{1,0:T(8,128)S(1)}, f32[32,128]{1,0:T(8,128)S(1)}, u32[]{:S(2)}, u32[]{:S(2)}) %collective-permute-start.3) | collective-permute-done | bytes 16416 | tf_op jit(solution)/shard_map/ppermute | solution.py:367
  33.7 0.0 all-to-all-done.1.got_far
  33.7 0.0 copy-done.7
  33.7 0.0 copy-done.8
  33.7 3.1 %second_step.1 = f32[25,32,128]{2,1,0:T(8,128)} custom-call(f32[80,128]{1,0:T(8,128)S(1)} %collective-permute-done.swapped, f32[80,128]{1,0:T(8,128)S(1)} %collective-permute-done.1.next_swapped, f32[32,128]{1,0:T(8,128)S(1)} %collective-permute-done.2.beside, f32[32,128]{1,0:T(8,128)S(1)} %collective-permute-done.3.next_beside, ...), custom_call_target="tpu_custom_call", output_to_operand_aliasing={{}: (9, {})} | custom-call | tf_op jit(solution)/shard_map/second_step/pallas_call | solution.py:369
Async XLA Ops:
  0.0 8.2 %all-to-all-start = ((f32[1,1,8,128]{3,1,0,2:T(1,128)}), f32[1,1,8,128]{3,1,0,2:T(1,128)S(1)}, u32[]{:S(2)}, u32[]{:S(2)}) async-start(f32[1,1,8,128]{3,1,0,2:T(1,128)} %bitcast.13), calls=%async_computation | async-start | bytes 8192 | tf_op jit(solution)/shard_map/all_to_all | solution.py:302
  5.4 1.4 %copy-start = (f32[4,25,32,128]{3,2,1,0:T(8,128)S(1)}, f32[4,25,32,128]{3,2,1,0:T(8,128)}, u32[]{:S(2)}) copy-start(f32[4,25,32,128]{3,2,1,0:T(8,128)} %side.5) | copy-start | bytes 4915204
  6.8 1.0 %copy-start.4 = (s32[25,32,128]{2,1,0:T(8,128)S(1)}, s32[25,32,128]{2,1,0:T(8,128)}, u32[]{:S(2)}) copy-start(s32[25,32,128]{2,1,0:T(8,128)} %mask.3) | copy-start | bytes 1228804
  7.8 0.7 %copy-start.6 = (s32[1,1,8,128]{3,2,1,0:T(8,128)S(1)}, s32[1,1,8,128]{3,2,1,0:T(8,128)}, u32[]{:S(2)}) copy-start(s32[1,1,8,128]{3,2,1,0:T(8,128)} %param.16) | copy-start | bytes 12292
  7.8 0.7 %copy-start.9 = (s32[1,1,8]{2,1,0:T(1,128)S(1)}, s32[1,1,8]{2,1,0:T(1,128)}, u32[]{:S(2)}) copy-start(s32[1,1,8]{2,1,0:T(1,128)} %param.17) | copy-start | bytes 100
  7.9 2.5 %copy-start.1 = (f32[4,25,32,128]{3,2,1,0:T(8,128)S(1)}, f32[4,25,32,128]{3,2,1,0:T(8,128)}, u32[]{:S(2)}) copy-start(f32[4,25,32,128]{3,2,1,0:T(8,128)} %side.5) | copy-start | bytes 4915204
  7.9 2.5 %copy-start.2 = (f32[2,25,32,128]{3,2,1,0:T(8,128)S(1)}, f32[2,25,32,128]{3,2,1,0:T(8,128)}, u32[]{:S(2)}) copy-start(f32[2,25,32,128]{3,2,1,0:T(8,128)} %vert.3) | copy-start | bytes 2457604
  7.9 2.5 %copy-start.3 = (f32[25,32,128]{2,1,0:T(8,128)S(1)}, f32[25,32,128]{2,1,0:T(8,128)}, u32[]{:S(2)}) copy-start(f32[25,32,128]{2,1,0:T(8,128)} %centre.3) | copy-start | bytes 1228804
  7.9 2.5 %copy-start.5 = (s32[25,32,128]{2,1,0:T(8,128)S(1)}, s32[25,32,128]{2,1,0:T(8,128)}, u32[]{:S(2)}) copy-start(s32[25,32,128]{2,1,0:T(8,128)} %mask.3) | copy-start | bytes 1228804
  10.4 23.3 %copy-start.7 = (s32[8]{0:T(128)S(1)}, s32[8]{0:T(128)}, u32[]{:S(2)}) copy-start(s32[8]{0:T(128)} %partner.1) | copy-start | bytes 100
  10.4 23.3 %copy-start.8 = (s32[8]{0:T(128)S(1)}, s32[8]{0:T(128)}, u32[]{:S(2)}) copy-start(s32[8]{0:T(128)} %flip.1) | copy-start | bytes 100
  13.5 20.3 %all-to-all-start.1 = ((f32[8,80,128]{2,1,0:T(8,128)}), f32[8,80,128]{2,1,0:T(8,128)S(1)}, u32[]{:S(2)}, u32[]{:S(2)}) async-start(f32[8,80,128]{2,1,0:T(8,128)} %get-tuple-element.17), calls=%async_computation.1 | async-start | bytes 655360 | tf_op jit(solution)/shard_map/all_to_all | solution.py:353
  19.2 3.4 %collective-permute-start = (f32[80,128]{1,0:T(8,128)}, f32[80,128]{1,0:T(8,128)S(1)}, u32[]{:S(2)}, u32[]{:S(2)}) collective-permute-start(f32[80,128]{1,0:T(8,128)} %get-tuple-element.12), channel_id=1, source_target_pairs={{0,8},{8,0},{16,24},{24,16},{1,9},{9,1},{17,25},{25,17},{2,10},{10... | collective-permute-start | bytes 122888 | tf_op jit(solution)/shard_map/ppermute | solution.py:355
  20.4 5.8 %collective-permute-start.1 = (f32[80,128]{1,0:T(8,128)}, f32[80,128]{1,0:T(8,128)S(1)}, u32[]{:S(2)}, u32[]{:S(2)}) collective-permute-start(f32[80,128]{1,0:T(8,128)} %get-tuple-element.13), channel_id=1, source_target_pairs={{8,16},{16,8},{9,17},{17,9},{10,18},{18,10},{11,19},{19,11},{12,20... | collective-permute-start | bytes 122888 | tf_op jit(solution)/shard_map/ppermute | solution.py:354
  26.9 2.7 %collective-permute-start.2 = (f32[32,128]{1,0:T(8,128)S(1)}, f32[32,128]{1,0:T(8,128)S(1)}, u32[]{:S(2)}, u32[]{:S(2)}) collective-permute-start(f32[32,128]{1,0:T(8,128)S(1)} %get-tuple-element.15), channel_id=1, source_target_pairs={{0,1},{1,0},{2,3},{3,2},{4,5},{5,4},{6,7},{7,6},{8,9},{9,8},{10,11... | collective-permute-start | bytes 49160 | tf_op jit(solution)/shard_map/ppermute | solution.py:368
  28.8 5.0 %collective-permute-start.3 = (f32[32,128]{1,0:T(8,128)S(1)}, f32[32,128]{1,0:T(8,128)S(1)}, u32[]{:S(2)}, u32[]{:S(2)}) collective-permute-start(f32[32,128]{1,0:T(8,128)S(1)} %get-tuple-element.16), channel_id=1, source_target_pairs={{1,2},{2,1},{3,4},{4,3},{5,6},{6,5},{7,0},{0,7},{9,10},{10,9},{11,... | collective-permute-start | bytes 49160 | tf_op jit(solution)/shard_map/ppermute | solution.py:367

commit v6 on v5

--- a/solution.py
+++ b/solution.py
@@ -77,7 +77,7 @@
     return eastward, westward
 
 
-def forcing_kernel(sources, misfit, cell, count, adjoint_far, start, hot, valued, adjoint, arrived):
+def forced(sources, misfit, cell, count, adjoint_far, start, hot, valued, adjoint, arrived):
     load = pltpu.make_async_copy(adjoint_far, adjoint, arrived)
     load.start()
     group = min(GROUP, sources)
@@ -137,7 +137,8 @@
     return pltpu.make_async_copy(source.at[levels], target.at[levels], semaphores.at[i])
 
 
-def first_kernel(held, where, scales, side, centre, vert, mask, part_far, swap, next_swap, edges, slots, part, up, down, tips, picked, next_picked, sent, posted):
+def first_kernel(sources, misfit, cell, count, adjoint_far, where, scales, side, centre, vert, mask, part_far, swap, next_swap, edges, slots, hot, valued, adjoint, held, part, up, down, tips, picked, next_picked, sent, posted, arrived):
+    forced(sources, misfit, cell, count, adjoint_far, held, hot, valued, adjoint, arrived)
     for ref in (up, down):
         ref[CORNER + 1 : SLOT, :] = jnp.zeros((SLOT - CORNER - 1, COLS), jnp.float32)
     for i in range(2):
@@ -198,9 +199,7 @@
         ref[24:EDGE, :] = jnp.where(iota((EDGE - 24, COLS), 0) == 0, corners, 0.0)
 
 
-def second_kernel(swapped, next_swapped, beside, next_beside, edges, got_far, partner, flip, where, part_far, side, centre, vert, out, held, part, result, lines, near_sides, far_sides, west_side, east_side, got, loaded, sent, gathered):
-    gather = pltpu.make_async_copy(got_far, got, gathered)
-    gather.start()
+def second_kernel(swapped, next_swapped, beside, next_beside, edges, got, partner, flip, where, part_far, side, centre, vert, out, held, part, result, lines, near_sides, far_sides, west_side, east_side, loaded, sent):
     for i in range(LEVELS // CHUNK):
         chunk(part_far, part, loaded, i).start()
     sources = got.shape[0]
@@ -229,7 +228,6 @@
         return jnp.where(flip[source] == 1, jnp.take_along_axis(rows, back, axis=1), rows)
 
     level_lane = iota((PAD, COLS), 1)
-    gather.wait()
     source = comes_from(column)
     earlier = comes_from(source)
     before = jnp.where(source == 0, sources - 1, source - 1)
@@ -317,27 +315,16 @@
         cost_estimate=ahead,
         name="edge_scales",
     )(side_coeff, land_mask)
-    start = pl.pallas_call(
-        functools.partial(forcing_kernel, sources),
-        out_shape=tile,
-        in_specs=[VMEM, VMEM, SMEM, FAR],
-        out_specs=VMEM,
+    part, swap, next_swap, edges, slots = pl.pallas_call(
+        functools.partial(first_kernel, sources),
+        out_shape=(tile, lines, lines, jax.ShapeDtypeStruct((EDGES, COLS), f32), pltpu.HBM((sources, SLOT, COLS), f32)),
+        in_specs=[VMEM, VMEM, SMEM, FAR, SMEM] + [VMEM] * 5,
+        out_specs=(FAR, FAR, FAR, VMEM, FAR),
         scratch_shapes=[
             pltpu.VMEM((LEVELS * ROWS, group * CAP), jnp.bfloat16),
             pltpu.VMEM((2 * COLS, group * CAP), jnp.bfloat16),
             field,
-            pltpu.SemaphoreType.DMA,
-        ],
-        compiler_params=pltpu.CompilerParams(vmem_limit_bytes=(8 if small else 24) * MIB),
-        cost_estimate=pl.CostEstimate(flops=10**8, bytes_accessed=8 * 10**6, transcendentals=0),
-        name="forcing",
-    )(received.reshape(sources, CAP), obs_cell.reshape(sources, CAP), obs_count.reshape(1, sources), pltpu.with_memory_space_constraint(adjoint_in, pltpu.HBM))
-    part, swap, next_swap, edges, slots = pl.pallas_call(
-        first_kernel,
-        out_shape=(tile, lines, lines, jax.ShapeDtypeStruct((EDGES, COLS), f32), pltpu.HBM((sources, SLOT, COLS), f32)),
-        in_specs=[VMEM, SMEM] + [VMEM] * 5,
-        out_specs=(FAR, FAR, FAR, VMEM, FAR),
-        scratch_shapes=[
+            field,
             field,
             pltpu.VMEM((SLOT, COLS), f32),
             pltpu.VMEM((SLOT, COLS), f32),
@@ -346,10 +333,22 @@
             pltpu.VMEM((SLOT, COLS), f32),
             chunks,
             pltpu.SemaphoreType.DMA((sources + 2,)),
+            pltpu.SemaphoreType.DMA,
         ],
-        compiler_params=pltpu.CompilerParams(vmem_limit_bytes=(8 if small else 24) * MIB),
+        compiler_params=pltpu.CompilerParams(vmem_limit_bytes=(10 if small else 24) * MIB),
         name="first_step",
-    )(start, where, scales, side_coeff, centre, vert_coeff, land_mask)
+    )(
+        received.reshape(sources, CAP),
+        obs_cell.reshape(sources, CAP),
+        obs_count.reshape(1, sources),
+        pltpu.with_memory_space_constraint(adjoint_in, pltpu.HBM),
+        where,
+        scales,
+        side_coeff,
+        centre,
+        vert_coeff,
+        land_mask,
+    )
     got = lax.all_to_all(slots, "col", split_axis=0, concat_axis=0, tiled=True)
     next_swapped = lax.ppermute(next_swap, "tile", swaps(1, tiles - 1))
     swapped = lax.ppermute(swap, "tile", swaps(0, tiles))
@@ -369,7 +368,7 @@
     return pl.pallas_call(
         second_kernel,
         out_shape=tile,
-        in_specs=[VMEM] * 5 + [FAR] + [SMEM] * 3 + [FAR] + [VMEM] * 3,
+        in_specs=[VMEM] * 6 + [SMEM] * 3 + [FAR] + [VMEM] * 3,
         out_specs=FAR,
         input_output_aliases={9: 0},
         scratch_shapes=[
@@ -381,10 +380,8 @@
             pltpu.VMEM((ROWS, COLS), f32),
             pltpu.VMEM((EDGE, COLS), f32),
             pltpu.VMEM((EDGE, COLS), f32),
-            pltpu.VMEM((sources, SLOT, COLS), f32),
             chunks,
             chunks,
-            pltpu.SemaphoreType.DMA,
         ],
         compiler_params=pltpu.CompilerParams(vmem_limit_bytes=(8 if small else 24) * MIB),
         name="second_step",

time: 37.2 us -> 37.1 us (level)
  local copies, waits for them, and re-layouts: 2.87 us -> 4.03 us
  Pallas kernels: 8.8 us -> 8.16 us
  starting transfers between devices: 16.3 us -> 15.7 us
    unnamed x20, local copies, waits for them, and re-layouts: 2.79 us -> 3.95 us
    pallas_call x3 -> x2, Pallas kernels: 7.91 us -> 7.27 us  [the longest x1 4.28 us: body(): pl.pallas_call(functools.partial(first_kernel, sources), out_shape=(tile,...]
    all_to_all x1, starting transfers between devices: 5.75 us -> 5.11 us  [body(): got = lax.all_to_all(slots, 'col', split_axis=0, concat_axis=0, tiled=True)]
where the time goes in v6:
time: 37.1 us; the launch traced here: 36.6 us
  starting transfers between devices  15.7 us (42%)
  waiting for transfers between devices  8.71 us (23%)
  Pallas kernels  8.16 us (22%)
  local copies, waits for them, and re-layouts  4.03 us (11%)
    all_to_all x1, starting transfers between devices, body(): lax.all_to_all(obs_misfit, 'col', split_axis=2, concat_axis=1, tiled=True)  5.41 us
    all_to_all x1, starting transfers between devices, body(): got = lax.all_to_all(slots, 'col', split_axis=0, concat_axis=0, tiled=True)  5.11 us
    pallas_call x1, Pallas kernels, body(): pl.pallas_call(functools.partial(first_kernel, sources), out_shape=(tile,...  4.28 us
    ppermute x1, waiting for transfers between devices, body(): lax.ppermute(next_beside, 'col', swaps(1, sources - 1) + round_trip)  4.12 us
    unnamed x20, local copies, waits for them, and re-layouts  3.95 us
    ppermute x1, waiting for transfers between devices, body(): next_swapped = lax.ppermute(next_swap, 'tile', swaps(1, tiles - 1))  3.7 us
    pallas_call x1, Pallas kernels, body(): pl.pallas_call(second_kernel, out_shape=tile, in_specs=[VMEM] * 6 + [SMEM...  2.99 us
    ppermute x1, starting transfers between devices, body(): next_swapped = lax.ppermute(next_swap, 'tile', swaps(1, tiles - 1))  2.09 us
  transfers between devices with their start and end apart: 6, of which 3 were waited for; matrix products, arithmetic and copies ran while one was open for 0% of the time, Pallas kernels for 2%

profile of v6, /device:TPU:29, one launch (start us, length us, event | category | flops | bytes accessed | tf_op | source)
XLA Modules:
  0.0 36.6 jit_solution(6324254239420981272)
XLA Ops:
  0.0 5.4 %all-to-all-start = ((f32[1,1,8,128]{3,1,0,2:T(1,128)}), f32[1,1,8,128]{3,1,0,2:T(1,128)S(1)}, u32[]{:S(2)}, u32[]{:S(2)}) async-start(f32[1,1,8,128]{3,1,0,2:T(1,128)} %bitcast.13), calls=%async_computation | async-start | bytes 8192 | tf_op jit(solution)/shard_map/all_to_all | solution.py:300
  5.4 0.0 copy-start
  5.4 1.4 %copy-done = f32[4,25,32,128]{3,2,1,0:T(8,128)S(1)} copy-done((f32[4,25,32,128]{3,2,1,0:T(8,128)S(1)}, f32[4,25,32,128]{3,2,1,0:T(8,128)}, u32[]{:S(2)}) %copy-start) | copy-done | bytes 1638424
  6.8 0.0 copy-start.4
  6.8 1.0 %copy-done.4 = s32[25,32,128]{2,1,0:T(8,128)S(1)} copy-done((s32[25,32,128]{2,1,0:T(8,128)S(1)}, s32[25,32,128]{2,1,0:T(8,128)}, u32[]{:S(2)}) %copy-start.4) | copy-done | bytes 409624
  7.8 0.0 copy-start.1
  7.8 0.0 copy-start.2
  7.9 0.0 copy-start.3
  7.9 0.0 copy-start.5
  7.9 0.0 copy-start.6
  7.9 0.0 copy-start.7
  7.9 0.2 edge_scales.1.scales
  8.1 0.1 stack.31.where
  8.2 0.0 all-to-all-done
  8.2 1.1 %copy-done.1 = f32[4,25,32,128]{3,2,1,0:T(8,128)S(1)} copy-done((f32[4,25,32,128]{3,2,1,0:T(8,128)S(1)}, f32[4,25,32,128]{3,2,1,0:T(8,128)}, u32[]{:S(2)}) %copy-start.1) | copy-done | bytes 1638424
  9.3 0.2 copy-done.2
  9.5 0.1 copy-done.3
  9.6 0.1 copy-done.5
  9.7 0.0 copy-done.6
  9.7 0.0 copy-done.7
  9.7 0.0 copy-start.8
  9.7 0.0 copy-start.9
  9.7 4.3 %first_step.1 = (f32[25,32,128]{2,1,0:T(8,128)}, f32[80,128]{1,0:T(8,128)}, f32[80,128]{1,0:T(8,128)}, f32[112,128]{1,0:T(8,128)S(1)}, f32[8,80,128]{2,1,0:T(8,128)}) custom-call(f32[8,128]{1,0:T(8,128)S(1)} %bitcast.10, s32[8,128]{1,0:T(8,128)S(1)} %bitcast.11, s32[1,8]{1,0:T(1,128)S(1)} %bitcast.12, f32[25,32,128]{2,1,0:T(8,128)} %adjoint_far.1, ...), custom_call_target="tpu_custom_call" | custom-call | tf_op jit(solution)/shard_map/first_step/pallas_call | solution.py:318
  14.0 5.1 %all-to-all-start.1 = ((f32[8,80,128]{2,1,0:T(8,128)}), f32[8,80,128]{2,1,0:T(8,128)S(1)}, u32[]{:S(2)}, u32[]{:S(2)}) async-start(f32[8,80,128]{2,1,0:T(8,128)} %get-tuple-element.17), calls=%async_computation.1 | async-start | bytes 655360 | tf_op jit(solution)/shard_map/all_to_all | solution.py:352
  19.1 1.2 %collective-permute-start = (f32[80,128]{1,0:T(8,128)}, f32[80,128]{1,0:T(8,128)S(1)}, u32[]{:S(2)}, u32[]{:S(2)}) collective-permute-start(f32[80,128]{1,0:T(8,128)} %get-tuple-element.12), channel_id=1, source_target_pairs={{0,8},{8,0},{16,24},{24,16},{1,9},{9,1},{17,25},{25,17},{2,10},{10... | collective-permute-start | bytes 122888 | tf_op jit(solution)/shard_map/ppermute | solution.py:354
  20.3 2.1 %collective-permute-start.1 = (f32[80,128]{1,0:T(8,128)}, f32[80,128]{1,0:T(8,128)S(1)}, u32[]{:S(2)}, u32[]{:S(2)}) collective-permute-start(f32[80,128]{1,0:T(8,128)} %get-tuple-element.13), channel_id=1, source_target_pairs={{8,16},{16,8},{9,17},{17,9},{10,18},{18,10},{11,19},{19,11},{12,20... | collective-permute-start | bytes 122888 | tf_op jit(solution)/shard_map/ppermute | solution.py:353
  22.4 0.0 collective-permute-done.swapped
  22.5 3.7 %collective-permute-done.1.next_swapped = f32[80,128]{1,0:T(8,128)S(1)} collective-permute-done((f32[80,128]{1,0:T(8,128)}, f32[80,128]{1,0:T(8,128)S(1)}, u32[]{:S(2)}, u32[]{:S(2)}) %collective-permute-start.1) | collective-permute-done | bytes 40992 | tf_op jit(solution)/shard_map/ppermute | solution.py:353
  26.2 0.6 %corners.1 = (f32[32,128]{1,0:T(8,128)S(1)}, f32[32,128]{1,0:T(8,128)S(1)}) custom-call(f32[80,128]{1,0:T(8,128)S(1)} %collective-permute-done.swapped, f32[80,128]{1,0:T(8,128)S(1)} %collective-permute-done.1.next_swapped, f32[112,128]{1,0:T(8,128)S(1)} %get-tuple-element.14.edges, s32[6]{0:T(128)S(1)} %stack.31.where), custom_call_target="tpu_custom_call" | custom-call | flops 1000000 | bytes 4000000 | tf_op jit(solution)/shard_map/corners/pallas_call | solution.py:356
  26.8 1.9 %collective-permute-start.2 = (f32[32,128]{1,0:T(8,128)S(1)}, f32[32,128]{1,0:T(8,128)S(1)}, u32[]{:S(2)}, u32[]{:S(2)}) collective-permute-start(f32[32,128]{1,0:T(8,128)S(1)} %get-tuple-element.15), channel_id=1, source_target_pairs={{0,1},{1,0},{2,3},{3,2},{4,5},{5,4},{6,7},{7,6},{8,9},{9,8},{10,11... | collective-permute-start | bytes 49160 | tf_op jit(solution)/shard_map/ppermute | solution.py:367
  28.7 0.0 collective-permute-start.3
  28.7 0.8 %collective-permute-done.2.beside = f32[32,128]{1,0:T(8,128)S(1)} collective-permute-done((f32[32,128]{1,0:T(8,128)S(1)}, f32[32,128]{1,0:T(8,128)S(1)}, u32[]{:S(2)}, u32[]{:S(2)}) %collective-permute-start.2) | collective-permute-done | bytes 16416 | tf_op jit(solution)/shard_map/ppermute | solution.py:367
  29.5 4.1 %collective-permute-done.3.next_beside = f32[32,128]{1,0:T(8,128)S(1)} collective-permute-done((f32[32,128]{1,0:T(8,128)S(1)}, f32[32,128]{1,0:T(8,128)S(1)}, u32[]{:S(2)}, u32[]{:S(2)}) %collective-permute-start.3) | collective-permute-done | bytes 16416 | tf_op jit(solution)/shard_map/ppermute | solution.py:366
  33.6 0.0 all-to-all-done.1.got
  33.6 0.0 copy-done.8
  33.7 0.0 copy-done.9
  33.7 3.0 %second_step.1 = f32[25,32,128]{2,1,0:T(8,128)} custom-call(f32[80,128]{1,0:T(8,128)S(1)} %collective-permute-done.swapped, f32[80,128]{1,0:T(8,128)S(1)} %collective-permute-done.1.next_swapped, f32[32,128]{1,0:T(8,128)S(1)} %collective-permute-done.2.beside, f32[32,128]{1,0:T(8,128)S(1)} %collective-permute-done.3.next_beside, ...), custom_call_target="tpu_custom_call", output_to_operand_aliasing={{}: (9, {})} | custom-call | tf_op jit(solution)/shard_map/second_step/pallas_call | solution.py:368
Async XLA Ops:
  0.0 8.2 %all-to-all-start = ((f32[1,1,8,128]{3,1,0,2:T(1,128)}), f32[1,1,8,128]{3,1,0,2:T(1,128)S(1)}, u32[]{:S(2)}, u32[]{:S(2)}) async-start(f32[1,1,8,128]{3,1,0,2:T(1,128)} %bitcast.13), calls=%async_computation | async-start | bytes 8192 | tf_op jit(solution)/shard_map/all_to_all | solution.py:300
  5.4 1.4 %copy-start = (f32[4,25,32,128]{3,2,1,0:T(8,128)S(1)}, f32[4,25,32,128]{3,2,1,0:T(8,128)}, u32[]{:S(2)}) copy-start(f32[4,25,32,128]{3,2,1,0:T(8,128)} %side.5) | copy-start | bytes 4915204
  6.8 1.0 %copy-start.4 = (s32[25,32,128]{2,1,0:T(8,128)S(1)}, s32[25,32,128]{2,1,0:T(8,128)}, u32[]{:S(2)}) copy-start(s32[25,32,128]{2,1,0:T(8,128)} %mask.3) | copy-start | bytes 1228804
  7.8 1.4 %copy-start.1 = (f32[4,25,32,128]{3,2,1,0:T(8,128)S(1)}, f32[4,25,32,128]{3,2,1,0:T(8,128)}, u32[]{:S(2)}) copy-start(f32[4,25,32,128]{3,2,1,0:T(8,128)} %side.5) | copy-start | bytes 4915204
  7.8 1.6 %copy-start.2 = (f32[2,25,32,128]{3,2,1,0:T(8,128)S(1)}, f32[2,25,32,128]{3,2,1,0:T(8,128)}, u32[]{:S(2)}) copy-start(f32[2,25,32,128]{3,2,1,0:T(8,128)} %vert.3) | copy-start | bytes 2457604
  7.9 1.7 %copy-start.3 = (f32[25,32,128]{2,1,0:T(8,128)S(1)}, f32[25,32,128]{2,1,0:T(8,128)}, u32[]{:S(2)}) copy-start(f32[25,32,128]{2,1,0:T(8,128)} %centre.3) | copy-start | bytes 1228804
  7.9 1.9 %copy-start.5 = (s32[25,32,128]{2,1,0:T(8,128)S(1)}, s32[25,32,128]{2,1,0:T(8,128)}, u32[]{:S(2)}) copy-start(s32[25,32,128]{2,1,0:T(8,128)} %mask.3) | copy-start | bytes 1228804
  7.9 1.9 %copy-start.6 = (s32[1,1,8,128]{3,2,1,0:T(8,128)S(1)}, s32[1,1,8,128]{3,2,1,0:T(8,128)}, u32[]{:S(2)}) copy-start(s32[1,1,8,128]{3,2,1,0:T(8,128)} %param.16) | copy-start | bytes 12292
  7.9 1.8 %copy-start.7 = (s32[1,1,8]{2,1,0:T(1,128)S(1)}, s32[1,1,8]{2,1,0:T(1,128)}, u32[]{:S(2)}) copy-start(s32[1,1,8]{2,1,0:T(1,128)} %param.17) | copy-start | bytes 100
  9.7 23.9 %copy-start.8 = (s32[8]{0:T(128)S(1)}, s32[8]{0:T(128)}, u32[]{:S(2)}) copy-start(s32[8]{0:T(128)} %partner.1) | copy-start | bytes 100
  9.7 23.9 %copy-start.9 = (s32[8]{0:T(128)S(1)}, s32[8]{0:T(128)}, u32[]{:S(2)}) copy-start(s32[8]{0:T(128)} %flip.1) | copy-start | bytes 100
  14.0 19.6 %all-to-all-start.1 = ((f32[8,80,128]{2,1,0:T(8,128)}), f32[8,80,128]{2,1,0:T(8,128)S(1)}, u32[]{:S(2)}, u32[]{:S(2)}) async-start(f32[8,80,128]{2,1,0:T(8,128)} %get-tuple-element.17), calls=%async_computation.1 | async-start | bytes 655360 | tf_op jit(solution)/shard_map/all_to_all | solution.py:352
  19.1 3.4 %collective-permute-start = (f32[80,128]{1,0:T(8,128)}, f32[80,128]{1,0:T(8,128)S(1)}, u32[]{:S(2)}, u32[]{:S(2)}) collective-permute-start(f32[80,128]{1,0:T(8,128)} %get-tuple-element.12), channel_id=1, source_target_pairs={{0,8},{8,0},{16,24},{24,16},{1,9},{9,1},{17,25},{25,17},{2,10},{10... | collective-permute-start | bytes 122888 | tf_op jit(solution)/shard_map/ppermute | solution.py:354
  20.3 5.8 %collective-permute-start.1 = (f32[80,128]{1,0:T(8,128)}, f32[80,128]{1,0:T(8,128)S(1)}, u32[]{:S(2)}, u32[]{:S(2)}) collective-permute-start(f32[80,128]{1,0:T(8,128)} %get-tuple-element.13), channel_id=1, source_target_pairs={{8,16},{16,8},{9,17},{17,9},{10,18},{18,10},{11,19},{19,11},{12,20... | collective-permute-start | bytes 122888 | tf_op jit(solution)/shard_map/ppermute | solution.py:353
  26.8 2.7 %collective-permute-start.2 = (f32[32,128]{1,0:T(8,128)S(1)}, f32[32,128]{1,0:T(8,128)S(1)}, u32[]{:S(2)}, u32[]{:S(2)}) collective-permute-start(f32[32,128]{1,0:T(8,128)S(1)} %get-tuple-element.15), channel_id=1, source_target_pairs={{0,1},{1,0},{2,3},{3,2},{4,5},{5,4},{6,7},{7,6},{8,9},{9,8},{10,11... | collective-permute-start | bytes 49160 | tf_op jit(solution)/shard_map/ppermute | solution.py:367
  28.7 5.0 %collective-permute-start.3 = (f32[32,128]{1,0:T(8,128)S(1)}, f32[32,128]{1,0:T(8,128)S(1)}, u32[]{:S(2)}, u32[]{:S(2)}) collective-permute-start(f32[32,128]{1,0:T(8,128)S(1)} %get-tuple-element.16), channel_id=1, source_target_pairs={{1,2},{2,1},{3,4},{4,3},{5,6},{6,5},{7,0},{0,7},{9,10},{10,9},{11,... | collective-permute-start | bytes 49160 | tf_op jit(solution)/shard_map/ppermute | solution.py:366

commit v7 on v6

--- a/solution.py
+++ b/solution.py
@@ -137,7 +137,7 @@
     return pltpu.make_async_copy(source.at[levels], target.at[levels], semaphores.at[i])
 
 
-def first_kernel(sources, misfit, cell, count, adjoint_far, where, scales, side, centre, vert, mask, part_far, swap, next_swap, edges, slots, hot, valued, adjoint, held, part, up, down, tips, picked, next_picked, sent, posted, arrived):
+def first_kernel(sources, misfit, cell, count, adjoint_far, where, scales, side, centre, vert, mask, part, swap, next_swap, edges, slots, hot, valued, adjoint, held, up, down, tips, picked, next_picked, posted, arrived):
     forced(sources, misfit, cell, count, adjoint_far, held, hot, valued, adjoint, arrived)
     for ref in (up, down):
         ref[CORNER + 1 : SLOT, :] = jnp.zeros((SLOT - CORNER - 1, COLS), jnp.float32)
@@ -154,8 +154,6 @@
             ref[LEVELS + k : LEVELS + k + 1, :] = r[at : at + 1]
             tips[i * PAD + k : i * PAD + k + 1, :] = sides[at : at + 1]
         packed = [p + turn(x, 2 * k + 1) for p, x in zip(packed, (sides, outer(lane, r, r)))]
-        if (k + 1) % CHUNK == 0:
-            chunk(part, part_far, sent, k // CHUNK).start()
     for i, ref in enumerate((up, down)):
         ref[2 * LEVELS : 3 * LEVELS, :] = scales[16 + i * PAD : 16 + i * PAD + LEVELS, :]
         east, west = ends(tips[i * PAD : (i + 1) * PAD, :])
@@ -176,8 +174,6 @@
     edges[40:48, :] = scales[8:16, :]
     edges[48 : 48 + PAD, :] = down[0:PAD, :]
     edges[48 + PAD : EDGES, :] = up[0:PAD, :]
-    for i in range(LEVELS // CHUNK):
-        chunk(part, part_far, sent, i).wait()
     for copy in spread:
         copy.wait()
 
@@ -199,9 +195,9 @@
         ref[24:EDGE, :] = jnp.where(iota((EDGE - 24, COLS), 0) == 0, corners, 0.0)
 
 
-def second_kernel(swapped, next_swapped, beside, next_beside, edges, got, partner, flip, where, part_far, side, centre, vert, out, held, part, result, lines, near_sides, far_sides, west_side, east_side, loaded, sent):
-    for i in range(LEVELS // CHUNK):
-        chunk(part_far, part, loaded, i).start()
+def second_kernel(swapped, next_swapped, beside, next_beside, edges, got_far, partner, flip, where, part, side, centre, vert, out, held, result, lines, near_sides, far_sides, west_side, east_side, got, gathered, sent):
+    gather = pltpu.make_async_copy(got_far, got, gathered)
+    gather.start()
     sources = got.shape[0]
     below_near, above_near = from_tiles(swapped, next_swapped, where, slice(0, PAD))
     below_part, above_part = from_tiles(swapped, next_swapped, where, slice(LEVELS, LEVELS + PAD))
@@ -227,6 +223,25 @@
         back = COLS - 1 - iota((PAD, COLS), 1)
         return jnp.where(flip[source] == 1, jnp.take_along_axis(rows, back, axis=1), rows)
 
+    lines[0:PAD, :] = jnp.where(at_top, 0.0, above_near)
+    lines[3 * PAD : 4 * PAD, :] = below_near
+
+    def spread_sides(ref, from_west, from_east):
+        even = (iota((8, COLS), 1) & 1) == 0
+        for g, offset in enumerate(OFFSET):
+            ref[8 * g : 8 * g + 8, :] = jnp.where(even, turn(from_west, -offset), turn(from_east, -offset - 1))
+
+    spread_sides(near_sides, west_side[0:8, :], east_side[0:8, :])
+    row, lane = iota((ROWS, COLS), 0), iota((ROWS, COLS), 1)
+
+    def joined(k, r, sides, first, last):
+        r = r + jnp.where((lane == 0) | (lane == COLS - 1), turn(sides[...], -2 * k), 0.0)
+        r = r + jnp.where(row == 0, first, 0.0) + jnp.where(row == ROWS - 1, last, 0.0)
+        return jnp.where(part[k] == LAND, 0.0, r)
+
+    for k in range(LEVELS):
+        held[k] = joined(k, part[k], near_sides, lines[3 * PAD + k : 3 * PAD + k + 1, :], lines[k : k + 1, :])
+    gather.wait()
     level_lane = iota((PAD, COLS), 1)
     source = comes_from(column)
     earlier = comes_from(source)
@@ -244,36 +259,21 @@
     cross_east = to_rows(got[after, CORNER : CORNER + 1, :], OFFSET[1])
     sum_fold = sum_fold + jnp.where(level_lane == 0, cross_west, 0.0) + jnp.where(level_lane == COLS - 1, cross_east, 0.0)
     fold_second = turned(turn(got[source, SLOT - PAD : SLOT, :], SLOT - PAD - 2 * LEVELS, 0) * sum_fold, source)
-    lines[0:PAD, :] = jnp.where(at_top, fold_first, above_near)
+    fold_first = jnp.where(at_top, fold_first, 0.0)
+    for k in range(LEVELS):
+        last = part[k, ROWS - 1 : ROWS, :]
+        held[k, ROWS - 1 : ROWS, :] += jnp.where(last == LAND, 0.0, fold_first[k : k + 1, :])
     lines[PAD : 2 * PAD, :] = below_scale * sum_low
     lines[2 * PAD : 3 * PAD, :] = jnp.where(at_top, fold_second, above_scale * sum_high)
-    lines[3 * PAD : 4 * PAD, :] = below_near
     from_left = comes_from(left)
     from_right = comes_from(right)
     fold_left = turned(got[from_left, 0:PAD, :], from_left)[:, COLS - 1 : COLS]
     fold_right = turned(got[from_right, 0:PAD, :], from_right)[:, 0:1]
     fold_left = jnp.where(at_top, to_lanes(fold_left, OFFSET[3]), 0.0)
     fold_right = jnp.where(at_top, to_lanes(fold_right, OFFSET[3]), 0.0)
-    near_left = west_side[0:8, :]
-    near_right = east_side[0:8, :]
     next_left = west_side[16:24, :] * (west_side[8:16, :] + edges[24:32, :] + spot_rows(0.0, fold_left))
     next_right = east_side[16:24, :] * (east_side[8:16, :] + edges[0:8, :] + spot_rows(0.0, fold_right))
-    even = (iota((8, COLS), 1) & 1) == 0
-    for ref, from_west, from_east in ((near_sides, near_left, near_right), (far_sides, next_left, next_right)):
-        for g, offset in enumerate(OFFSET):
-            ref[8 * g : 8 * g + 8, :] = jnp.where(even, turn(from_west, -offset), turn(from_east, -offset - 1))
-
-    row, lane = iota((ROWS, COLS), 0), iota((ROWS, COLS), 1)
-
-    def joined(k, r, sides, first, last):
-        r = r + jnp.where((lane == 0) | (lane == COLS - 1), turn(sides[...], -2 * k), 0.0)
-        r = r + jnp.where(row == 0, first, 0.0) + jnp.where(row == ROWS - 1, last, 0.0)
-        return jnp.where(part[k] == LAND, 0.0, r)
-
-    for k in range(LEVELS):
-        if k % CHUNK == 0:
-            chunk(part_far, part, loaded, k // CHUNK).wait()
-        held[k] = joined(k, part[k], near_sides, lines[3 * PAD + k : 3 * PAD + k + 1, :], lines[k : k + 1, :])
+    spread_sides(far_sides, next_left, next_right)
     for k in range(LEVELS):
         r = terms(k, held, centre, side, vert)[0]
         result[k] = joined(k, r, far_sides, lines[PAD + k : PAD + k + 1, :], lines[2 * PAD + k : 2 * PAD + k + 1, :])
@@ -319,11 +319,10 @@
         functools.partial(first_kernel, sources),
         out_shape=(tile, lines, lines, jax.ShapeDtypeStruct((EDGES, COLS), f32), pltpu.HBM((sources, SLOT, COLS), f32)),
         in_specs=[VMEM, VMEM, SMEM, FAR, SMEM] + [VMEM] * 5,
-        out_specs=(FAR, FAR, FAR, VMEM, FAR),
+        out_specs=(VMEM, FAR, FAR, VMEM, FAR),
         scratch_shapes=[
             pltpu.VMEM((LEVELS * ROWS, group * CAP), jnp.bfloat16),
             pltpu.VMEM((2 * COLS, group * CAP), jnp.bfloat16),
-            field,
             field,
             field,
             pltpu.VMEM((SLOT, COLS), f32),
@@ -331,7 +330,6 @@
             pltpu.VMEM((2 * PAD, COLS), f32),
             pltpu.VMEM((SLOT, COLS), f32),
             pltpu.VMEM((SLOT, COLS), f32),
-            chunks,
             pltpu.SemaphoreType.DMA((sources + 2,)),
             pltpu.SemaphoreType.DMA,
         ],
@@ -368,11 +366,9 @@
     return pl.pallas_call(
         second_kernel,
         out_shape=tile,
-        in_specs=[VMEM] * 6 + [SMEM] * 3 + [FAR] + [VMEM] * 3,
+        in_specs=[VMEM] * 5 + [FAR] + [SMEM] * 3 + [VMEM] * 4,
         out_specs=FAR,
-        input_output_aliases={9: 0},
         scratch_shapes=[
-            field,
             field,
             field,
             pltpu.VMEM((4 * PAD, COLS), f32),
@@ -380,7 +376,8 @@
             pltpu.VMEM((ROWS, COLS), f32),
             pltpu.VMEM((EDGE, COLS), f32),
             pltpu.VMEM((EDGE, COLS), f32),
-            chunks,
+            pltpu.VMEM((sources, SLOT, COLS), f32),
+            pltpu.SemaphoreType.DMA,
             chunks,
         ],
         compiler_params=pltpu.CompilerParams(vmem_limit_bytes=(8 if small else 24) * MIB),
@@ -391,7 +388,7 @@
         beside,
         next_beside,
         edges,
-        got,
+        pltpu.with_memory_space_constraint(got, pltpu.HBM),
         fold_partner,
         fold_flip,
         where,

time: 37.1 us -> 38.2 us (1.030)
  local copies, waits for them, and re-layouts: 4.03 us -> 4.92 us
    unnamed x20, local copies, waits for them, and re-layouts: 3.95 us -> 4.84 us
  transfers between devices with their start and end apart: 6 -> 6, of which waited for: 3 -> 4; matrix products, arithmetic and copies ran while one was open for 0% -> 0% of each run, Pallas kernels for 2% -> 2%
where the time goes in v7:
time: 38.2 us; the launch traced here: 37.7 us
  starting transfers between devices  15.9 us (42%)
  waiting for transfers between devices  8.71 us (23%)
  Pallas kernels  8.13 us (21%)
  local copies, waits for them, and re-layouts  4.92 us (13%)
    all_to_all x1, starting transfers between devices, body(): lax.all_to_all(obs_misfit, 'col', split_axis=2, concat_axis=1, tiled=True)  5.41 us
    all_to_all x1, starting transfers between devices, body(): got = lax.all_to_all(slots, 'col', split_axis=0, concat_axis=0, tiled=True)  5.33 us
    unnamed x20, local copies, waits for them, and re-layouts  4.84 us
    pallas_call x1, Pallas kernels, body(): pl.pallas_call(functools.partial(first_kernel, sources), out_shape=(tile,...  4.22 us
    ppermute x1, waiting for transfers between devices, body(): lax.ppermute(next_beside, 'col', swaps(1, sources - 1) + round_trip)  4.12 us
    ppermute x1, waiting for transfers between devices, body(): next_swapped = lax.ppermute(next_swap, 'tile', swaps(1, tiles - 1))  3.59 us
    pallas_call x1, Pallas kernels, body(): pl.pallas_call(second_kernel, out_shape=tile, in_specs=[VMEM] * 5 + [FAR]...  3.03 us
    ppermute x1, starting transfers between devices, body(): next_swapped = lax.ppermute(next_swap, 'tile', swaps(1, tiles - 1))  2.09 us
  transfers between devices with their start and end apart: 6, of which 4 were waited for; matrix products, arithmetic and copies ran while one was open for 0% of the time, Pallas kernels for 2%

profile of v7, /device:TPU:29, one launch (start us, length us, event | category | flops | bytes accessed | tf_op | source)
XLA Modules:
  0.0 37.7 jit_solution(1324034783657150481)
XLA Ops:
  0.0 5.4 %all-to-all-start = ((f32[1,1,8,128]{3,1,0,2:T(1,128)}), f32[1,1,8,128]{3,1,0,2:T(1,128)S(1)}, u32[]{:S(2)}, u32[]{:S(2)}) async-start(f32[1,1,8,128]{3,1,0,2:T(1,128)} %bitcast.13), calls=%async_computation | async-start | bytes 8192 | tf_op jit(solution)/shard_map/all_to_all | solution.py:300
  5.4 0.0 copy-start
  5.4 1.4 %copy-done = f32[4,25,32,128]{3,2,1,0:T(8,128)S(1)} copy-done((f32[4,25,32,128]{3,2,1,0:T(8,128)S(1)}, f32[4,25,32,128]{3,2,1,0:T(8,128)}, u32[]{:S(2)}) %copy-start) | copy-done | bytes 1638424
  6.8 0.0 copy-start.4
  6.8 1.0 %copy-done.4 = s32[25,32,128]{2,1,0:T(8,128)S(1)} copy-done((s32[25,32,128]{2,1,0:T(8,128)S(1)}, s32[25,32,128]{2,1,0:T(8,128)}, u32[]{:S(2)}) %copy-start.4) | copy-done | bytes 409624
  7.8 0.0 copy-start.1
  7.8 0.0 copy-start.2
  7.9 0.0 copy-start.3
  7.9 0.0 copy-start.6
  7.9 0.0 copy-start.7
  7.9 0.2 edge_scales.1.scales
  8.1 0.1 stack.31.where
  8.2 0.0 all-to-all-done
  8.2 1.1 %copy-done.1 = f32[4,25,32,128]{3,2,1,0:T(8,128)S(1)} copy-done((f32[4,25,32,128]{3,2,1,0:T(8,128)S(1)}, f32[4,25,32,128]{3,2,1,0:T(8,128)}, u32[]{:S(2)}) %copy-start.1) | copy-done | bytes 1638424
  9.3 0.2 copy-done.2
  9.5 0.1 copy-done.3
  9.6 0.0 copy-done.6
  9.6 0.0 copy-done.7
  9.6 0.0 copy-start.5
  9.6 1.0 %copy-done.5 = s32[25,32,128]{2,1,0:T(8,128)S(1)} copy-done((s32[25,32,128]{2,1,0:T(8,128)S(1)}, s32[25,32,128]{2,1,0:T(8,128)}, u32[]{:S(2)}) %copy-start.5) | copy-done | bytes 409624
  10.6 0.0 copy-start.8
  10.6 0.0 copy-start.9
  10.6 4.2 %first_step.1 = (f32[25,32,128]{2,1,0:T(8,128)S(1)}, f32[80,128]{1,0:T(8,128)}, f32[80,128]{1,0:T(8,128)}, f32[112,128]{1,0:T(8,128)S(1)}, f32[8,80,128]{2,1,0:T(8,128)}) custom-call(f32[8,128]{1,0:T(8,128)S(1)} %bitcast.10, s32[8,128]{1,0:T(8,128)S(1)} %bitcast.11, s32[1,8]{1,0:T(1,128)S(1)} %bitcast.12, f32[25,32,128]{2,1,0:T(8,128)} %adjoint_far.1, ...), custom_call_target="tpu_custom_call" | custom-call | tf_op jit(solution)/shard_map/first_step/pallas_call | solution.py:318
  14.8 5.3 %all-to-all-start.1 = ((f32[8,80,128]{2,1,0:T(8,128)}), f32[8,80,128]{2,1,0:T(8,128)}, u32[]{:S(2)}, u32[]{:S(2)}) async-start(f32[8,80,128]{2,1,0:T(8,128)} %get-tuple-element.17), calls=%async_computation.1 | async-start | bytes 655360 | tf_op jit(solution)/shard_map/all_to_all | solution.py:350
  20.2 1.2 %collective-permute-start = (f32[80,128]{1,0:T(8,128)}, f32[80,128]{1,0:T(8,128)S(1)}, u32[]{:S(2)}, u32[]{:S(2)}) collective-permute-start(f32[80,128]{1,0:T(8,128)} %get-tuple-element.12), channel_id=1, source_target_pairs={{0,8},{8,0},{16,24},{24,16},{1,9},{9,1},{17,25},{25,17},{2,10},{10... | collective-permute-start | bytes 122888 | tf_op jit(solution)/shard_map/ppermute | solution.py:352
  21.4 2.1 %collective-permute-start.1 = (f32[80,128]{1,0:T(8,128)}, f32[80,128]{1,0:T(8,128)S(1)}, u32[]{:S(2)}, u32[]{:S(2)}) collective-permute-start(f32[80,128]{1,0:T(8,128)} %get-tuple-element.13), channel_id=1, source_target_pairs={{8,16},{16,8},{9,17},{17,9},{10,18},{18,10},{11,19},{19,11},{12,20... | collective-permute-start | bytes 122888 | tf_op jit(solution)/shard_map/ppermute | solution.py:351
  23.5 0.2 collective-permute-done.swapped
  23.6 3.6 %collective-permute-done.1.next_swapped = f32[80,128]{1,0:T(8,128)S(1)} collective-permute-done((f32[80,128]{1,0:T(8,128)}, f32[80,128]{1,0:T(8,128)S(1)}, u32[]{:S(2)}, u32[]{:S(2)}) %collective-permute-start.1) | collective-permute-done | bytes 40992 | tf_op jit(solution)/shard_map/ppermute | solution.py:351
  27.2 0.6 %corners.1 = (f32[32,128]{1,0:T(8,128)S(1)}, f32[32,128]{1,0:T(8,128)S(1)}) custom-call(f32[80,128]{1,0:T(8,128)S(1)} %collective-permute-done.swapped, f32[80,128]{1,0:T(8,128)S(1)} %collective-permute-done.1.next_swapped, f32[112,128]{1,0:T(8,128)S(1)} %get-tuple-element.14.edges, s32[6]{0:T(128)S(1)} %stack.31.where), custom_call_target="tpu_custom_call" | custom-call | flops 1000000 | bytes 4000000 | tf_op jit(solution)/shard_map/corners/pallas_call | solution.py:354
  27.9 1.9 %collective-permute-start.2 = (f32[32,128]{1,0:T(8,128)S(1)}, f32[32,128]{1,0:T(8,128)S(1)}, u32[]{:S(2)}, u32[]{:S(2)}) collective-permute-start(f32[32,128]{1,0:T(8,128)S(1)} %get-tuple-element.15), channel_id=1, source_target_pairs={{0,1},{1,0},{2,3},{3,2},{4,5},{5,4},{6,7},{7,6},{8,9},{9,8},{10,11... | collective-permute-start | bytes 49160 | tf_op jit(solution)/shard_map/ppermute | solution.py:365
  29.7 0.0 collective-permute-start.3
  29.7 0.8 %collective-permute-done.2.beside = f32[32,128]{1,0:T(8,128)S(1)} collective-permute-done((f32[32,128]{1,0:T(8,128)S(1)}, f32[32,128]{1,0:T(8,128)S(1)}, u32[]{:S(2)}, u32[]{:S(2)}) %collective-permute-start.2) | collective-permute-done | bytes 16416 | tf_op jit(solution)/shard_map/ppermute | solution.py:365
  30.6 4.1 %collective-permute-done.3.next_beside = f32[32,128]{1,0:T(8,128)S(1)} collective-permute-done((f32[32,128]{1,0:T(8,128)S(1)}, f32[32,128]{1,0:T(8,128)S(1)}, u32[]{:S(2)}, u32[]{:S(2)}) %collective-permute-start.3) | collective-permute-done | bytes 16416 | tf_op jit(solution)/shard_map/ppermute | solution.py:364
  34.7 0.0 all-to-all-done.1.got_far
  34.7 0.0 copy-done.8
  34.7 0.0 copy-done.9
  34.7 3.0 %second_step.1 = f32[25,32,128]{2,1,0:T(8,128)} custom-call(f32[80,128]{1,0:T(8,128)S(1)} %collective-permute-done.swapped, f32[80,128]{1,0:T(8,128)S(1)} %collective-permute-done.1.next_swapped, f32[32,128]{1,0:T(8,128)S(1)} %collective-permute-done.2.beside, f32[32,128]{1,0:T(8,128)S(1)} %collective-permute-done.3.next_beside, ...), custom_call_target="tpu_custom_call" | custom-call | tf_op jit(solution)/shard_map/second_step/pallas_call | solution.py:366
Async XLA Ops:
  0.0 8.2 %all-to-all-start = ((f32[1,1,8,128]{3,1,0,2:T(1,128)}), f32[1,1,8,128]{3,1,0,2:T(1,128)S(1)}, u32[]{:S(2)}, u32[]{:S(2)}) async-start(f32[1,1,8,128]{3,1,0,2:T(1,128)} %bitcast.13), calls=%async_computation | async-start | bytes 8192 | tf_op jit(solution)/shard_map/all_to_all | solution.py:300
  5.4 1.4 %copy-start = (f32[4,25,32,128]{3,2,1,0:T(8,128)S(1)}, f32[4,25,32,128]{3,2,1,0:T(8,128)}, u32[]{:S(2)}) copy-start(f32[4,25,32,128]{3,2,1,0:T(8,128)} %side.5) | copy-start | bytes 4915204
  6.8 1.0 %copy-start.4 = (s32[25,32,128]{2,1,0:T(8,128)S(1)}, s32[25,32,128]{2,1,0:T(8,128)}, u32[]{:S(2)}) copy-start(s32[25,32,128]{2,1,0:T(8,128)} %mask.3) | copy-start | bytes 1228804
  7.8 1.4 %copy-start.1 = (f32[4,25,32,128]{3,2,1,0:T(8,128)S(1)}, f32[4,25,32,128]{3,2,1,0:T(8,128)}, u32[]{:S(2)}) copy-start(f32[4,25,32,128]{3,2,1,0:T(8,128)} %side.5) | copy-start | bytes 4915204
  7.8 1.6 %copy-start.2 = (f32[2,25,32,128]{3,2,1,0:T(8,128)S(1)}, f32[2,25,32,128]{3,2,1,0:T(8,128)}, u32[]{:S(2)}) copy-start(f32[2,25,32,128]{3,2,1,0:T(8,128)} %vert.3) | copy-start | bytes 2457604
  7.9 1.7 %copy-start.3 = (f32[25,32,128]{2,1,0:T(8,128)S(1)}, f32[25,32,128]{2,1,0:T(8,128)}, u32[]{:S(2)}) copy-start(f32[25,32,128]{2,1,0:T(8,128)} %centre.3) | copy-start | bytes 1228804
  7.9 1.7 %copy-start.6 = (s32[1,1,8,128]{3,2,1,0:T(8,128)S(1)}, s32[1,1,8,128]{3,2,1,0:T(8,128)}, u32[]{:S(2)}) copy-start(s32[1,1,8,128]{3,2,1,0:T(8,128)} %param.16) | copy-start | bytes 12292
  7.9 1.7 %copy-start.7 = (s32[1,1,8]{2,1,0:T(1,128)S(1)}, s32[1,1,8]{2,1,0:T(1,128)}, u32[]{:S(2)}) copy-start(s32[1,1,8]{2,1,0:T(1,128)} %param.17) | copy-start | bytes 100
  9.6 1.0 %copy-start.5 = (s32[25,32,128]{2,1,0:T(8,128)S(1)}, s32[25,32,128]{2,1,0:T(8,128)}, u32[]{:S(2)}) copy-start(s32[25,32,128]{2,1,0:T(8,128)} %mask.3) | copy-start | bytes 1228804
  10.6 24.1 %copy-start.8 = (s32[8]{0:T(128)S(1)}, s32[8]{0:T(128)}, u32[]{:S(2)}) copy-start(s32[8]{0:T(128)} %partner.1) | copy-start | bytes 100
  10.6 24.1 %copy-start.9 = (s32[8]{0:T(128)S(1)}, s32[8]{0:T(128)}, u32[]{:S(2)}) copy-start(s32[8]{0:T(128)} %flip.1) | copy-start | bytes 100
  14.8 19.9 %all-to-all-start.1 = ((f32[8,80,128]{2,1,0:T(8,128)}), f32[8,80,128]{2,1,0:T(8,128)}, u32[]{:S(2)}, u32[]{:S(2)}) async-start(f32[8,80,128]{2,1,0:T(8,128)} %get-tuple-element.17), calls=%async_computation.1 | async-start | bytes 655360 | tf_op jit(solution)/shard_map/all_to_all | solution.py:350
  20.2 3.5 %collective-permute-start = (f32[80,128]{1,0:T(8,128)}, f32[80,128]{1,0:T(8,128)S(1)}, u32[]{:S(2)}, u32[]{:S(2)}) collective-permute-start(f32[80,128]{1,0:T(8,128)} %get-tuple-element.12), channel_id=1, source_target_pairs={{0,8},{8,0},{16,24},{24,16},{1,9},{9,1},{17,25},{25,17},{2,10},{10... | collective-permute-start | bytes 122888 | tf_op jit(solution)/shard_map/ppermute | solution.py:352
  21.4 5.8 %collective-permute-start.1 = (f32[80,128]{1,0:T(8,128)}, f32[80,128]{1,0:T(8,128)S(1)}, u32[]{:S(2)}, u32[]{:S(2)}) collective-permute-start(f32[80,128]{1,0:T(8,128)} %get-tuple-element.13), channel_id=1, source_target_pairs={{8,16},{16,8},{9,17},{17,9},{10,18},{18,10},{11,19},{19,11},{12,20... | collective-permute-start | bytes 122888 | tf_op jit(solution)/shard_map/ppermute | solution.py:351
  27.9 2.7 %collective-permute-start.2 = (f32[32,128]{1,0:T(8,128)S(1)}, f32[32,128]{1,0:T(8,128)S(1)}, u32[]{:S(2)}, u32[]{:S(2)}) collective-permute-start(f32[32,128]{1,0:T(8,128)S(1)} %get-tuple-element.15), channel_id=1, source_target_pairs={{0,1},{1,0},{2,3},{3,2},{4,5},{5,4},{6,7},{7,6},{8,9},{9,8},{10,11... | collective-permute-start | bytes 49160 | tf_op jit(solution)/shard_map/ppermute | solution.py:365
  29.7 5.0 %collective-permute-start.3 = (f32[32,128]{1,0:T(8,128)S(1)}, f32[32,128]{1,0:T(8,128)S(1)}, u32[]{:S(2)}, u32[]{:S(2)}) collective-permute-start(f32[32,128]{1,0:T(8,128)S(1)} %get-tuple-element.16), channel_id=1, source_target_pairs={{1,2},{2,1},{3,4},{4,3},{5,6},{6,5},{7,0},{0,7},{9,10},{10,9},{11,... | collective-permute-start | bytes 49160 | tf_op jit(solution)/shard_map/ppermute | solution.py:364

commit v8 on v6

--- a/solution.py
+++ b/solution.py
@@ -137,8 +137,11 @@
     return pltpu.make_async_copy(source.at[levels], target.at[levels], semaphores.at[i])
 
 
-def first_kernel(sources, misfit, cell, count, adjoint_far, where, scales, side, centre, vert, mask, part_far, swap, next_swap, edges, slots, hot, valued, adjoint, held, part, up, down, tips, picked, next_picked, sent, posted, arrived):
+def first_kernel(sources, misfit, cell, count, adjoint_far, where, scales, side, centre_far, vert, mask, part, swap, next_swap, edges, slots, hot, valued, adjoint, held, centre, up, down, tips, picked, next_picked, near, posted, arrived):
+    load = pltpu.make_async_copy(centre_far, centre, near)
+    load.start()
     forced(sources, misfit, cell, count, adjoint_far, held, hot, valued, adjoint, arrived)
+    load.wait()
     for ref in (up, down):
         ref[CORNER + 1 : SLOT, :] = jnp.zeros((SLOT - CORNER - 1, COLS), jnp.float32)
     for i in range(2):
@@ -154,8 +157,6 @@
             ref[LEVELS + k : LEVELS + k + 1, :] = r[at : at + 1]
             tips[i * PAD + k : i * PAD + k + 1, :] = sides[at : at + 1]
         packed = [p + turn(x, 2 * k + 1) for p, x in zip(packed, (sides, outer(lane, r, r)))]
-        if (k + 1) % CHUNK == 0:
-            chunk(part, part_far, sent, k // CHUNK).start()
     for i, ref in enumerate((up, down)):
         ref[2 * LEVELS : 3 * LEVELS, :] = scales[16 + i * PAD : 16 + i * PAD + LEVELS, :]
         east, west = ends(tips[i * PAD : (i + 1) * PAD, :])
@@ -176,8 +177,6 @@
     edges[40:48, :] = scales[8:16, :]
     edges[48 : 48 + PAD, :] = down[0:PAD, :]
     edges[48 + PAD : EDGES, :] = up[0:PAD, :]
-    for i in range(LEVELS // CHUNK):
-        chunk(part, part_far, sent, i).wait()
     for copy in spread:
         copy.wait()
 
@@ -199,9 +198,9 @@
         ref[24:EDGE, :] = jnp.where(iota((EDGE - 24, COLS), 0) == 0, corners, 0.0)
 
 
-def second_kernel(swapped, next_swapped, beside, next_beside, edges, got, partner, flip, where, part_far, side, centre, vert, out, held, part, result, lines, near_sides, far_sides, west_side, east_side, loaded, sent):
-    for i in range(LEVELS // CHUNK):
-        chunk(part_far, part, loaded, i).start()
+def second_kernel(swapped, next_swapped, beside, next_beside, edges, got, partner, flip, where, part, side, centre_far, vert, out, held, centre, result, lines, near_sides, far_sides, west_side, east_side, near, sent):
+    load = pltpu.make_async_copy(centre_far, centre, near)
+    load.start()
     sources = got.shape[0]
     below_near, above_near = from_tiles(swapped, next_swapped, where, slice(0, PAD))
     below_part, above_part = from_tiles(swapped, next_swapped, where, slice(LEVELS, LEVELS + PAD))
@@ -271,9 +270,8 @@
         return jnp.where(part[k] == LAND, 0.0, r)
 
     for k in range(LEVELS):
-        if k % CHUNK == 0:
-            chunk(part_far, part, loaded, k // CHUNK).wait()
         held[k] = joined(k, part[k], near_sides, lines[3 * PAD + k : 3 * PAD + k + 1, :], lines[k : k + 1, :])
+    load.wait()
     for k in range(LEVELS):
         r = terms(k, held, centre, side, vert)[0]
         result[k] = joined(k, r, far_sides, lines[PAD + k : PAD + k + 1, :], lines[2 * PAD + k : 2 * PAD + k + 1, :])
@@ -318,8 +316,8 @@
     part, swap, next_swap, edges, slots = pl.pallas_call(
         functools.partial(first_kernel, sources),
         out_shape=(tile, lines, lines, jax.ShapeDtypeStruct((EDGES, COLS), f32), pltpu.HBM((sources, SLOT, COLS), f32)),
-        in_specs=[VMEM, VMEM, SMEM, FAR, SMEM] + [VMEM] * 5,
-        out_specs=(FAR, FAR, FAR, VMEM, FAR),
+        in_specs=[VMEM, VMEM, SMEM, FAR, SMEM, VMEM, VMEM, FAR, VMEM, VMEM],
+        out_specs=(VMEM, FAR, FAR, VMEM, FAR),
         scratch_shapes=[
             pltpu.VMEM((LEVELS * ROWS, group * CAP), jnp.bfloat16),
             pltpu.VMEM((2 * COLS, group * CAP), jnp.bfloat16),
@@ -331,7 +329,7 @@
             pltpu.VMEM((2 * PAD, COLS), f32),
             pltpu.VMEM((SLOT, COLS), f32),
             pltpu.VMEM((SLOT, COLS), f32),
-            chunks,
+            pltpu.SemaphoreType.DMA,
             pltpu.SemaphoreType.DMA((sources + 2,)),
             pltpu.SemaphoreType.DMA,
         ],
@@ -345,7 +343,7 @@
         where,
         scales,
         side_coeff,
-        centre,
+        pltpu.with_memory_space_constraint(centre, pltpu.HBM),
         vert_coeff,
         land_mask,
     )
@@ -368,9 +366,8 @@
     return pl.pallas_call(
         second_kernel,
         out_shape=tile,
-        in_specs=[VMEM] * 6 + [SMEM] * 3 + [FAR] + [VMEM] * 3,
+        in_specs=[VMEM] * 6 + [SMEM] * 3 + [VMEM, VMEM, FAR, VMEM],
         out_specs=FAR,
-        input_output_aliases={9: 0},
         scratch_shapes=[
             field,
             field,
@@ -380,7 +377,7 @@
             pltpu.VMEM((ROWS, COLS), f32),
             pltpu.VMEM((EDGE, COLS), f32),
             pltpu.VMEM((EDGE, COLS), f32),
-            chunks,
+            pltpu.SemaphoreType.DMA,
             chunks,
         ],
         compiler_params=pltpu.CompilerParams(vmem_limit_bytes=(8 if small else 24) * MIB),
@@ -397,7 +394,7 @@
         where,
         part,
         side_coeff,
-        centre,
+        pltpu.with_memory_space_constraint(centre, pltpu.HBM),
         vert_coeff,
     )
 

time: 37.1 us -> 37.8 us (1.019)
  local copies, waits for them, and re-layouts: 4.03 us -> 4.83 us
    unnamed x20 -> x18, local copies, waits for them, and re-layouts: 3.95 us -> 4.74 us
where the time goes in v8:
time: 37.8 us; the launch traced here: 37.3 us
  starting transfers between devices  15.7 us (42%)
  waiting for transfers between devices  8.71 us (23%)
  Pallas kernels  8.08 us (21%)
  local copies, waits for them, and re-layouts  4.83 us (13%)
    all_to_all x1, starting transfers between devices, body(): lax.all_to_all(obs_misfit, 'col', split_axis=2, concat_axis=1, tiled=True)  5.41 us
    all_to_all x1, starting transfers between devices, body(): got = lax.all_to_all(slots, 'col', split_axis=0, concat_axis=0, tiled=True)  5.11 us
    unnamed x18, local copies, waits for them, and re-layouts  4.74 us
    pallas_call x1, Pallas kernels, body(): pl.pallas_call(functools.partial(first_kernel, sources), out_shape=(tile,...  4.25 us
    ppermute x1, waiting for transfers between devices, body(): lax.ppermute(next_beside, 'col', swaps(1, sources - 1) + round_trip)  4.12 us
    ppermute x1, waiting for transfers between devices, body(): next_swapped = lax.ppermute(next_swap, 'tile', swaps(1, tiles - 1))  3.7 us
    pallas_call x1, Pallas kernels, body(): pl.pallas_call(second_kernel, out_shape=tile, in_specs=[VMEM] * 6 + [SMEM...  2.94 us
    ppermute x1, starting transfers between devices, body(): next_swapped = lax.ppermute(next_swap, 'tile', swaps(1, tiles - 1))  2.09 us
  transfers between devices with their start and end apart: 6, of which 3 were waited for; matrix products, arithmetic and copies ran while one was open for 0% of the time, Pallas kernels for 2%

profile of v8, /device:TPU:29, one launch (start us, length us, event | category | flops | bytes accessed | tf_op | source)
XLA Modules:
  0.0 37.3 jit_solution(8612228237847139326)
XLA Ops:
  0.0 5.4 %all-to-all-start = ((f32[1,1,8,128]{3,1,0,2:T(1,128)}), f32[1,1,8,128]{3,1,0,2:T(1,128)S(1)}, u32[]{:S(2)}, u32[]{:S(2)}) async-start(f32[1,1,8,128]{3,1,0,2:T(1,128)} %bitcast.13), calls=%async_computation | async-start | bytes 8192 | tf_op jit(solution)/shard_map/all_to_all | solution.py:298
  5.4 0.0 copy-start
  5.4 1.4 %copy-done = f32[4,25,32,128]{3,2,1,0:T(8,128)S(1)} copy-done((f32[4,25,32,128]{3,2,1,0:T(8,128)S(1)}, f32[4,25,32,128]{3,2,1,0:T(8,128)}, u32[]{:S(2)}) %copy-start) | copy-done | bytes 1638424
  6.8 0.0 copy-start.3
  6.8 1.0 %copy-done.3 = s32[25,32,128]{2,1,0:T(8,128)S(1)} copy-done((s32[25,32,128]{2,1,0:T(8,128)S(1)}, s32[25,32,128]{2,1,0:T(8,128)}, u32[]{:S(2)}) %copy-start.3) | copy-done | bytes 409624
  7.8 0.0 copy-start.1
  7.8 0.0 copy-start.2
  7.9 0.0 copy-start.5
  7.9 0.0 copy-start.6
  7.9 0.2 edge_scales.1.scales
  8.1 0.1 stack.31.where
  8.2 0.0 all-to-all-done
  8.2 1.1 %copy-done.1 = f32[4,25,32,128]{3,2,1,0:T(8,128)S(1)} copy-done((f32[4,25,32,128]{3,2,1,0:T(8,128)S(1)}, f32[4,25,32,128]{3,2,1,0:T(8,128)}, u32[]{:S(2)}) %copy-start.1) | copy-done | bytes 1638424
  9.3 0.2 copy-done.2
  9.5 0.0 copy-done.5
  9.5 0.0 copy-done.6
  9.5 0.0 copy-start.4
  9.5 1.0 %copy-done.4 = s32[25,32,128]{2,1,0:T(8,128)S(1)} copy-done((s32[25,32,128]{2,1,0:T(8,128)S(1)}, s32[25,32,128]{2,1,0:T(8,128)}, u32[]{:S(2)}) %copy-start.4) | copy-done | bytes 409624
  10.5 0.0 copy-start.7
  10.5 0.0 copy-start.8
  10.5 4.3 %first_step.1 = (f32[25,32,128]{2,1,0:T(8,128)S(1)}, f32[80,128]{1,0:T(8,128)}, f32[80,128]{1,0:T(8,128)}, f32[112,128]{1,0:T(8,128)S(1)}, f32[8,80,128]{2,1,0:T(8,128)}) custom-call(f32[8,128]{1,0:T(8,128)S(1)} %bitcast.10, s32[8,128]{1,0:T(8,128)S(1)} %bitcast.11, s32[1,8]{1,0:T(1,128)S(1)} %bitcast.12, f32[25,32,128]{2,1,0:T(8,128)} %adjoint_far.1, ...), custom_call_target="tpu_custom_call" | custom-call | tf_op jit(solution)/shard_map/first_step/pallas_call | solution.py:316
  14.8 5.1 %all-to-all-start.1 = ((f32[8,80,128]{2,1,0:T(8,128)}), f32[8,80,128]{2,1,0:T(8,128)S(1)}, u32[]{:S(2)}, u32[]{:S(2)}) async-start(f32[8,80,128]{2,1,0:T(8,128)} %get-tuple-element.17), calls=%async_computation.1 | async-start | bytes 655360 | tf_op jit(solution)/shard_map/all_to_all | solution.py:350
  19.9 1.2 %collective-permute-start = (f32[80,128]{1,0:T(8,128)}, f32[80,128]{1,0:T(8,128)S(1)}, u32[]{:S(2)}, u32[]{:S(2)}) collective-permute-start(f32[80,128]{1,0:T(8,128)} %get-tuple-element.12), channel_id=1, source_target_pairs={{0,8},{8,0},{16,24},{24,16},{1,9},{9,1},{17,25},{25,17},{2,10},{10... | collective-permute-start | bytes 122888 | tf_op jit(solution)/shard_map/ppermute | solution.py:352
  21.1 2.1 %collective-permute-start.1 = (f32[80,128]{1,0:T(8,128)}, f32[80,128]{1,0:T(8,128)S(1)}, u32[]{:S(2)}, u32[]{:S(2)}) collective-permute-start(f32[80,128]{1,0:T(8,128)} %get-tuple-element.13), channel_id=1, source_target_pairs={{8,16},{16,8},{9,17},{17,9},{10,18},{18,10},{11,19},{19,11},{12,20... | collective-permute-start | bytes 122888 | tf_op jit(solution)/shard_map/ppermute | solution.py:351
  23.2 0.0 collective-permute-done.swapped
  23.2 3.7 %collective-permute-done.1.next_swapped = f32[80,128]{1,0:T(8,128)S(1)} collective-permute-done((f32[80,128]{1,0:T(8,128)}, f32[80,128]{1,0:T(8,128)S(1)}, u32[]{:S(2)}, u32[]{:S(2)}) %collective-permute-start.1) | collective-permute-done | bytes 40992 | tf_op jit(solution)/shard_map/ppermute | solution.py:351
  26.9 0.6 %corners.1 = (f32[32,128]{1,0:T(8,128)S(1)}, f32[32,128]{1,0:T(8,128)S(1)}) custom-call(f32[80,128]{1,0:T(8,128)S(1)} %collective-permute-done.swapped, f32[80,128]{1,0:T(8,128)S(1)} %collective-permute-done.1.next_swapped, f32[112,128]{1,0:T(8,128)S(1)} %get-tuple-element.14.edges, s32[6]{0:T(128)S(1)} %stack.31.where), custom_call_target="tpu_custom_call" | custom-call | flops 1000000 | bytes 4000000 | tf_op jit(solution)/shard_map/corners/pallas_call | solution.py:354
  27.6 1.9 %collective-permute-start.2 = (f32[32,128]{1,0:T(8,128)S(1)}, f32[32,128]{1,0:T(8,128)S(1)}, u32[]{:S(2)}, u32[]{:S(2)}) collective-permute-start(f32[32,128]{1,0:T(8,128)S(1)} %get-tuple-element.15), channel_id=1, source_target_pairs={{0,1},{1,0},{2,3},{3,2},{4,5},{5,4},{6,7},{7,6},{8,9},{9,8},{10,11... | collective-permute-start | bytes 49160 | tf_op jit(solution)/shard_map/ppermute | solution.py:365
  29.4 0.0 collective-permute-start.3
  29.4 0.8 %collective-permute-done.2.beside = f32[32,128]{1,0:T(8,128)S(1)} collective-permute-done((f32[32,128]{1,0:T(8,128)S(1)}, f32[32,128]{1,0:T(8,128)S(1)}, u32[]{:S(2)}, u32[]{:S(2)}) %collective-permute-start.2) | collective-permute-done | bytes 16416 | tf_op jit(solution)/shard_map/ppermute | solution.py:365
  30.3 4.1 %collective-permute-done.3.next_beside = f32[32,128]{1,0:T(8,128)S(1)} collective-permute-done((f32[32,128]{1,0:T(8,128)S(1)}, f32[32,128]{1,0:T(8,128)S(1)}, u32[]{:S(2)}, u32[]{:S(2)}) %collective-permute-start.3) | collective-permute-done | bytes 16416 | tf_op jit(solution)/shard_map/ppermute | solution.py:364
  34.4 0.0 all-to-all-done.1.got
  34.4 0.0 copy-done.7
  34.4 0.0 copy-done.8
  34.4 2.9 %second_step.1 = f32[25,32,128]{2,1,0:T(8,128)} custom-call(f32[80,128]{1,0:T(8,128)S(1)} %collective-permute-done.swapped, f32[80,128]{1,0:T(8,128)S(1)} %collective-permute-done.1.next_swapped, f32[32,128]{1,0:T(8,128)S(1)} %collective-permute-done.2.beside, f32[32,128]{1,0:T(8,128)S(1)} %collective-permute-done.3.next_beside, ...), custom_call_target="tpu_custom_call" | custom-call | tf_op jit(solution)/shard_map/second_step/pallas_call | solution.py:366
Async XLA Ops:
  0.0 8.2 %all-to-all-start = ((f32[1,1,8,128]{3,1,0,2:T(1,128)}), f32[1,1,8,128]{3,1,0,2:T(1,128)S(1)}, u32[]{:S(2)}, u32[]{:S(2)}) async-start(f32[1,1,8,128]{3,1,0,2:T(1,128)} %bitcast.13), calls=%async_computation | async-start | bytes 8192 | tf_op jit(solution)/shard_map/all_to_all | solution.py:298
  5.4 1.4 %copy-start = (f32[4,25,32,128]{3,2,1,0:T(8,128)S(1)}, f32[4,25,32,128]{3,2,1,0:T(8,128)}, u32[]{:S(2)}) copy-start(f32[4,25,32,128]{3,2,1,0:T(8,128)} %side.5) | copy-start | bytes 4915204
  6.8 1.0 %copy-start.3 = (s32[25,32,128]{2,1,0:T(8,128)S(1)}, s32[25,32,128]{2,1,0:T(8,128)}, u32[]{:S(2)}) copy-start(s32[25,32,128]{2,1,0:T(8,128)} %mask.3) | copy-start | bytes 1228804
  7.8 1.4 %copy-start.1 = (f32[4,25,32,128]{3,2,1,0:T(8,128)S(1)}, f32[4,25,32,128]{3,2,1,0:T(8,128)}, u32[]{:S(2)}) copy-start(f32[4,25,32,128]{3,2,1,0:T(8,128)} %side.5) | copy-start | bytes 4915204
  7.8 1.6 %copy-start.2 = (f32[2,25,32,128]{3,2,1,0:T(8,128)S(1)}, f32[2,25,32,128]{3,2,1,0:T(8,128)}, u32[]{:S(2)}) copy-start(f32[2,25,32,128]{3,2,1,0:T(8,128)} %vert.3) | copy-start | bytes 2457604
  7.9 1.6 %copy-start.5 = (s32[1,1,8,128]{3,2,1,0:T(8,128)S(1)}, s32[1,1,8,128]{3,2,1,0:T(8,128)}, u32[]{:S(2)}) copy-start(s32[1,1,8,128]{3,2,1,0:T(8,128)} %param.16) | copy-start | bytes 12292
  7.9 1.6 %copy-start.6 = (s32[1,1,8]{2,1,0:T(1,128)S(1)}, s32[1,1,8]{2,1,0:T(1,128)}, u32[]{:S(2)}) copy-start(s32[1,1,8]{2,1,0:T(1,128)} %param.17) | copy-start | bytes 100
  9.5 1.0 %copy-start.4 = (s32[25,32,128]{2,1,0:T(8,128)S(1)}, s32[25,32,128]{2,1,0:T(8,128)}, u32[]{:S(2)}) copy-start(s32[25,32,128]{2,1,0:T(8,128)} %mask.3) | copy-start | bytes 1228804
  10.5 23.9 %copy-start.7 = (s32[8]{0:T(128)S(1)}, s32[8]{0:T(128)}, u32[]{:S(2)}) copy-start(s32[8]{0:T(128)} %partner.1) | copy-start | bytes 100
  10.5 23.9 %copy-start.8 = (s32[8]{0:T(128)S(1)}, s32[8]{0:T(128)}, u32[]{:S(2)}) copy-start(s32[8]{0:T(128)} %flip.1) | copy-start | bytes 100
  14.8 19.6 %all-to-all-start.1 = ((f32[8,80,128]{2,1,0:T(8,128)}), f32[8,80,128]{2,1,0:T(8,128)S(1)}, u32[]{:S(2)}, u32[]{:S(2)}) async-start(f32[8,80,128]{2,1,0:T(8,128)} %get-tuple-element.17), calls=%async_computation.1 | async-start | bytes 655360 | tf_op jit(solution)/shard_map/all_to_all | solution.py:350
  19.9 3.4 %collective-permute-start = (f32[80,128]{1,0:T(8,128)}, f32[80,128]{1,0:T(8,128)S(1)}, u32[]{:S(2)}, u32[]{:S(2)}) collective-permute-start(f32[80,128]{1,0:T(8,128)} %get-tuple-element.12), channel_id=1, source_target_pairs={{0,8},{8,0},{16,24},{24,16},{1,9},{9,1},{17,25},{25,17},{2,10},{10... | collective-permute-start | bytes 122888 | tf_op jit(solution)/shard_map/ppermute | solution.py:352
  21.1 5.8 %collective-permute-start.1 = (f32[80,128]{1,0:T(8,128)}, f32[80,128]{1,0:T(8,128)S(1)}, u32[]{:S(2)}, u32[]{:S(2)}) collective-permute-start(f32[80,128]{1,0:T(8,128)} %get-tuple-element.13), channel_id=1, source_target_pairs={{8,16},{16,8},{9,17},{17,9},{10,18},{18,10},{11,19},{19,11},{12,20... | collective-permute-start | bytes 122888 | tf_op jit(solution)/shard_map/ppermute | solution.py:351
  27.6 2.7 %collective-permute-start.2 = (f32[32,128]{1,0:T(8,128)S(1)}, f32[32,128]{1,0:T(8,128)S(1)}, u32[]{:S(2)}, u32[]{:S(2)}) collective-permute-start(f32[32,128]{1,0:T(8,128)S(1)} %get-tuple-element.15), channel_id=1, source_target_pairs={{0,1},{1,0},{2,3},{3,2},{4,5},{5,4},{6,7},{7,6},{8,9},{9,8},{10,11... | collective-permute-start | bytes 49160 | tf_op jit(solution)/shard_map/ppermute | solution.py:365
  29.4 5.0 %collective-permute-start.3 = (f32[32,128]{1,0:T(8,128)S(1)}, f32[32,128]{1,0:T(8,128)S(1)}, u32[]{:S(2)}, u32[]{:S(2)}) collective-permute-start(f32[32,128]{1,0:T(8,128)S(1)} %get-tuple-element.16), channel_id=1, source_target_pairs={{1,2},{2,1},{3,4},{4,3},{5,6},{6,5},{7,0},{0,7},{9,10},{10,9},{11,... | collective-permute-start | bytes 49160 | tf_op jit(solution)/shard_map/ppermute | solution.py:364

commit v9 on v6

--- a/solution.py
+++ b/solution.py
@@ -94,7 +94,7 @@
                 valued[i * COLS : (i + 1) * COLS, at] = jnp.where(column, part, 0.0).astype(jnp.bfloat16)
             place = cells >> 7
             for k in range(LEVELS):
-                match = (iota((ROWS, CAP), 0) + k * ROWS) == place
+                match = iota((ROWS, CAP), 0) == place - k * ROWS
                 hot[k * ROWS : (k + 1) * ROWS, at] = jnp.where(match, 1.0, 0.0).astype(jnp.bfloat16)
         part = lax.dot_general(hot[...], valued[...], (((1,), (1,)), ((), ())), preferred_element_type=jnp.float32)
         part = part[:, 0:COLS] + part[:, COLS : 2 * COLS]

time: 37.1 us -> 37.1 us (level)
  no operation moved by 1% of the time
where the time goes in v9:
time: 37.1 us; the launch traced here: 36.7 us
  starting transfers between devices  15.7 us (42%)
  waiting for transfers between devices  8.71 us (23%)
  Pallas kernels  8.23 us (22%)
  local copies, waits for them, and re-layouts  4.03 us (11%)
    all_to_all x1, starting transfers between devices, body(): lax.all_to_all(obs_misfit, 'col', split_axis=2, concat_axis=1, tiled=True)  5.41 us
    all_to_all x1, starting transfers between devices, body(): got = lax.all_to_all(slots, 'col', split_axis=0, concat_axis=0, tiled=True)  5.11 us
    pallas_call x1, Pallas kernels, body(): pl.pallas_call(functools.partial(first_kernel, sources), out_shape=(tile,...  4.35 us
    ppermute x1, waiting for transfers between devices, body(): lax.ppermute(next_beside, 'col', swaps(1, sources - 1) + round_trip)  4.12 us
    unnamed x20, local copies, waits for them, and re-layouts  3.95 us
    ppermute x1, waiting for transfers between devices, body(): next_swapped = lax.ppermute(next_swap, 'tile', swaps(1, tiles - 1))  3.7 us
    pallas_call x1, Pallas kernels, body(): pl.pallas_call(second_kernel, out_shape=tile, in_specs=[VMEM] * 6 + [SMEM...  2.99 us
    ppermute x1, starting transfers between devices, body(): next_swapped = lax.ppermute(next_swap, 'tile', swaps(1, tiles - 1))  2.09 us
  transfers between devices with their start and end apart: 6, of which 3 were waited for; matrix products, arithmetic and copies ran while one was open for 0% of the time, Pallas kernels for 2%

profile of v9, /device:TPU:29, one launch (start us, length us, event | category | flops | bytes accessed | tf_op | source)
XLA Modules:
  0.0 36.7 jit_solution(1350258845226559151)
XLA Ops:
  0.0 5.4 %all-to-all-start = ((f32[1,1,8,128]{3,1,0,2:T(1,128)}), f32[1,1,8,128]{3,1,0,2:T(1,128)S(1)}, u32[]{:S(2)}, u32[]{:S(2)}) async-start(f32[1,1,8,128]{3,1,0,2:T(1,128)} %bitcast.13), calls=%async_computation | async-start | bytes 8192 | tf_op jit(solution)/shard_map/all_to_all | solution.py:300
  5.4 0.0 copy-start
  5.4 1.4 %copy-done = f32[4,25,32,128]{3,2,1,0:T(8,128)S(1)} copy-done((f32[4,25,32,128]{3,2,1,0:T(8,128)S(1)}, f32[4,25,32,128]{3,2,1,0:T(8,128)}, u32[]{:S(2)}) %copy-start) | copy-done | bytes 1638424
  6.8 0.0 copy-start.4
  6.8 1.0 %copy-done.4 = s32[25,32,128]{2,1,0:T(8,128)S(1)} copy-done((s32[25,32,128]{2,1,0:T(8,128)S(1)}, s32[25,32,128]{2,1,0:T(8,128)}, u32[]{:S(2)}) %copy-start.4) | copy-done | bytes 409624
  7.8 0.0 copy-start.1
  7.8 0.0 copy-start.2
  7.9 0.0 copy-start.3
  7.9 0.0 copy-start.5
  7.9 0.0 copy-start.6
  7.9 0.0 copy-start.7
  7.9 0.2 edge_scales.1.scales
  8.1 0.1 stack.31.where
  8.2 0.0 all-to-all-done
  8.2 1.1 %copy-done.1 = f32[4,25,32,128]{3,2,1,0:T(8,128)S(1)} copy-done((f32[4,25,32,128]{3,2,1,0:T(8,128)S(1)}, f32[4,25,32,128]{3,2,1,0:T(8,128)}, u32[]{:S(2)}) %copy-start.1) | copy-done | bytes 1638424
  9.3 0.2 copy-done.2
  9.5 0.1 copy-done.3
  9.6 0.1 copy-done.5
  9.7 0.0 copy-done.6
  9.7 0.0 copy-done.7
  9.7 0.0 copy-start.8
  9.7 0.0 copy-start.9
  9.7 4.4 %first_step.1 = (f32[25,32,128]{2,1,0:T(8,128)}, f32[80,128]{1,0:T(8,128)}, f32[80,128]{1,0:T(8,128)}, f32[112,128]{1,0:T(8,128)S(1)}, f32[8,80,128]{2,1,0:T(8,128)}) custom-call(f32[8,128]{1,0:T(8,128)S(1)} %bitcast.10, s32[8,128]{1,0:T(8,128)S(1)} %bitcast.11, s32[1,8]{1,0:T(1,128)S(1)} %bitcast.12, f32[25,32,128]{2,1,0:T(8,128)} %adjoint_far.1, ...), custom_call_target="tpu_custom_call" | custom-call | tf_op jit(solution)/shard_map/first_step/pallas_call | solution.py:318
  14.1 5.1 %all-to-all-start.1 = ((f32[8,80,128]{2,1,0:T(8,128)}), f32[8,80,128]{2,1,0:T(8,128)S(1)}, u32[]{:S(2)}, u32[]{:S(2)}) async-start(f32[8,80,128]{2,1,0:T(8,128)} %get-tuple-element.17), calls=%async_computation.1 | async-start | bytes 655360 | tf_op jit(solution)/shard_map/all_to_all | solution.py:352
  19.2 1.2 %collective-permute-start = (f32[80,128]{1,0:T(8,128)}, f32[80,128]{1,0:T(8,128)S(1)}, u32[]{:S(2)}, u32[]{:S(2)}) collective-permute-start(f32[80,128]{1,0:T(8,128)} %get-tuple-element.12), channel_id=1, source_target_pairs={{0,8},{8,0},{16,24},{24,16},{1,9},{9,1},{17,25},{25,17},{2,10},{10... | collective-permute-start | bytes 122888 | tf_op jit(solution)/shard_map/ppermute | solution.py:354
  20.4 2.1 %collective-permute-start.1 = (f32[80,128]{1,0:T(8,128)}, f32[80,128]{1,0:T(8,128)S(1)}, u32[]{:S(2)}, u32[]{:S(2)}) collective-permute-start(f32[80,128]{1,0:T(8,128)} %get-tuple-element.13), channel_id=1, source_target_pairs={{8,16},{16,8},{9,17},{17,9},{10,18},{18,10},{11,19},{19,11},{12,20... | collective-permute-start | bytes 122888 | tf_op jit(solution)/shard_map/ppermute | solution.py:353
  22.5 0.0 collective-permute-done.swapped
  22.6 3.7 %collective-permute-done.1.next_swapped = f32[80,128]{1,0:T(8,128)S(1)} collective-permute-done((f32[80,128]{1,0:T(8,128)}, f32[80,128]{1,0:T(8,128)S(1)}, u32[]{:S(2)}, u32[]{:S(2)}) %collective-permute-start.1) | collective-permute-done | bytes 40992 | tf_op jit(solution)/shard_map/ppermute | solution.py:353
  26.3 0.6 %corners.1 = (f32[32,128]{1,0:T(8,128)S(1)}, f32[32,128]{1,0:T(8,128)S(1)}) custom-call(f32[80,128]{1,0:T(8,128)S(1)} %collective-permute-done.swapped, f32[80,128]{1,0:T(8,128)S(1)} %collective-permute-done.1.next_swapped, f32[112,128]{1,0:T(8,128)S(1)} %get-tuple-element.14.edges, s32[6]{0:T(128)S(1)} %stack.31.where), custom_call_target="tpu_custom_call" | custom-call | flops 1000000 | bytes 4000000 | tf_op jit(solution)/shard_map/corners/pallas_call | solution.py:356
  26.9 1.9 %collective-permute-start.2 = (f32[32,128]{1,0:T(8,128)S(1)}, f32[32,128]{1,0:T(8,128)S(1)}, u32[]{:S(2)}, u32[]{:S(2)}) collective-permute-start(f32[32,128]{1,0:T(8,128)S(1)} %get-tuple-element.15), channel_id=1, source_target_pairs={{0,1},{1,0},{2,3},{3,2},{4,5},{5,4},{6,7},{7,6},{8,9},{9,8},{10,11... | collective-permute-start | bytes 49160 | tf_op jit(solution)/shard_map/ppermute | solution.py:367
  28.8 0.0 collective-permute-start.3
  28.8 0.8 %collective-permute-done.2.beside = f32[32,128]{1,0:T(8,128)S(1)} collective-permute-done((f32[32,128]{1,0:T(8,128)S(1)}, f32[32,128]{1,0:T(8,128)S(1)}, u32[]{:S(2)}, u32[]{:S(2)}) %collective-permute-start.2) | collective-permute-done | bytes 16416 | tf_op jit(solution)/shard_map/ppermute | solution.py:367
  29.6 4.1 %collective-permute-done.3.next_beside = f32[32,128]{1,0:T(8,128)S(1)} collective-permute-done((f32[32,128]{1,0:T(8,128)S(1)}, f32[32,128]{1,0:T(8,128)S(1)}, u32[]{:S(2)}, u32[]{:S(2)}) %collective-permute-start.3) | collective-permute-done | bytes 16416 | tf_op jit(solution)/shard_map/ppermute | solution.py:366
  33.7 0.0 all-to-all-done.1.got
  33.7 0.0 copy-done.8
  33.7 0.0 copy-done.9
  33.7 3.0 %second_step.1 = f32[25,32,128]{2,1,0:T(8,128)} custom-call(f32[80,128]{1,0:T(8,128)S(1)} %collective-permute-done.swapped, f32[80,128]{1,0:T(8,128)S(1)} %collective-permute-done.1.next_swapped, f32[32,128]{1,0:T(8,128)S(1)} %collective-permute-done.2.beside, f32[32,128]{1,0:T(8,128)S(1)} %collective-permute-done.3.next_beside, ...), custom_call_target="tpu_custom_call", output_to_operand_aliasing={{}: (9, {})} | custom-call | tf_op jit(solution)/shard_map/second_step/pallas_call | solution.py:368
Async XLA Ops:
  0.0 8.2 %all-to-all-start = ((f32[1,1,8,128]{3,1,0,2:T(1,128)}), f32[1,1,8,128]{3,1,0,2:T(1,128)S(1)}, u32[]{:S(2)}, u32[]{:S(2)}) async-start(f32[1,1,8,128]{3,1,0,2:T(1,128)} %bitcast.13), calls=%async_computation | async-start | bytes 8192 | tf_op jit(solution)/shard_map/all_to_all | solution.py:300
  5.4 1.4 %copy-start = (f32[4,25,32,128]{3,2,1,0:T(8,128)S(1)}, f32[4,25,32,128]{3,2,1,0:T(8,128)}, u32[]{:S(2)}) copy-start(f32[4,25,32,128]{3,2,1,0:T(8,128)} %side.5) | copy-start | bytes 4915204
  6.8 1.0 %copy-start.4 = (s32[25,32,128]{2,1,0:T(8,128)S(1)}, s32[25,32,128]{2,1,0:T(8,128)}, u32[]{:S(2)}) copy-start(s32[25,32,128]{2,1,0:T(8,128)} %mask.3) | copy-start | bytes 1228804
  7.8 1.4 %copy-start.1 = (f32[4,25,32,128]{3,2,1,0:T(8,128)S(1)}, f32[4,25,32,128]{3,2,1,0:T(8,128)}, u32[]{:S(2)}) copy-start(f32[4,25,32,128]{3,2,1,0:T(8,128)} %side.5) | copy-start | bytes 4915204
  7.8 1.6 %copy-start.2 = (f32[2,25,32,128]{3,2,1,0:T(8,128)S(1)}, f32[2,25,32,128]{3,2,1,0:T(8,128)}, u32[]{:S(2)}) copy-start(f32[2,25,32,128]{3,2,1,0:T(8,128)} %vert.3) | copy-start | bytes 2457604
  7.9 1.7 %copy-start.3 = (f32[25,32,128]{2,1,0:T(8,128)S(1)}, f32[25,32,128]{2,1,0:T(8,128)}, u32[]{:S(2)}) copy-start(f32[25,32,128]{2,1,0:T(8,128)} %centre.3) | copy-start | bytes 1228804
  7.9 1.9 %copy-start.5 = (s32[25,32,128]{2,1,0:T(8,128)S(1)}, s32[25,32,128]{2,1,0:T(8,128)}, u32[]{:S(2)}) copy-start(s32[25,32,128]{2,1,0:T(8,128)} %mask.3) | copy-start | bytes 1228804
  7.9 1.9 %copy-start.6 = (s32[1,1,8,128]{3,2,1,0:T(8,128)S(1)}, s32[1,1,8,128]{3,2,1,0:T(8,128)}, u32[]{:S(2)}) copy-start(s32[1,1,8,128]{3,2,1,0:T(8,128)} %param.16) | copy-start | bytes 12292
  7.9 1.8 %copy-start.7 = (s32[1,1,8]{2,1,0:T(1,128)S(1)}, s32[1,1,8]{2,1,0:T(1,128)}, u32[]{:S(2)}) copy-start(s32[1,1,8]{2,1,0:T(1,128)} %param.17) | copy-start | bytes 100
  9.7 24.0 %copy-start.8 = (s32[8]{0:T(128)S(1)}, s32[8]{0:T(128)}, u32[]{:S(2)}) copy-start(s32[8]{0:T(128)} %partner.1) | copy-start | bytes 100
  9.7 24.0 %copy-start.9 = (s32[8]{0:T(128)S(1)}, s32[8]{0:T(128)}, u32[]{:S(2)}) copy-start(s32[8]{0:T(128)} %flip.1) | copy-start | bytes 100
  14.1 19.6 %all-to-all-start.1 = ((f32[8,80,128]{2,1,0:T(8,128)}), f32[8,80,128]{2,1,0:T(8,128)S(1)}, u32[]{:S(2)}, u32[]{:S(2)}) async-start(f32[8,80,128]{2,1,0:T(8,128)} %get-tuple-element.17), calls=%async_computation.1 | async-start | bytes 655360 | tf_op jit(solution)/shard_map/all_to_all | solution.py:352
  19.2 3.4 %collective-permute-start = (f32[80,128]{1,0:T(8,128)}, f32[80,128]{1,0:T(8,128)S(1)}, u32[]{:S(2)}, u32[]{:S(2)}) collective-permute-start(f32[80,128]{1,0:T(8,128)} %get-tuple-element.12), channel_id=1, source_target_pairs={{0,8},{8,0},{16,24},{24,16},{1,9},{9,1},{17,25},{25,17},{2,10},{10... | collective-permute-start | bytes 122888 | tf_op jit(solution)/shard_map/ppermute | solution.py:354
  20.4 5.8 %collective-permute-start.1 = (f32[80,128]{1,0:T(8,128)}, f32[80,128]{1,0:T(8,128)S(1)}, u32[]{:S(2)}, u32[]{:S(2)}) collective-permute-start(f32[80,128]{1,0:T(8,128)} %get-tuple-element.13), channel_id=1, source_target_pairs={{8,16},{16,8},{9,17},{17,9},{10,18},{18,10},{11,19},{19,11},{12,20... | collective-permute-start | bytes 122888 | tf_op jit(solution)/shard_map/ppermute | solution.py:353
  26.9 2.7 %collective-permute-start.2 = (f32[32,128]{1,0:T(8,128)S(1)}, f32[32,128]{1,0:T(8,128)S(1)}, u32[]{:S(2)}, u32[]{:S(2)}) collective-permute-start(f32[32,128]{1,0:T(8,128)S(1)} %get-tuple-element.15), channel_id=1, source_target_pairs={{0,1},{1,0},{2,3},{3,2},{4,5},{5,4},{6,7},{7,6},{8,9},{9,8},{10,11... | collective-permute-start | bytes 49160 | tf_op jit(solution)/shard_map/ppermute | solution.py:367
  28.8 5.0 %collective-permute-start.3 = (f32[32,128]{1,0:T(8,128)S(1)}, f32[32,128]{1,0:T(8,128)S(1)}, u32[]{:S(2)}, u32[]{:S(2)}) collective-permute-start(f32[32,128]{1,0:T(8,128)S(1)} %get-tuple-element.16), channel_id=1, source_target_pairs={{1,2},{2,1},{3,4},{4,3},{5,6},{6,5},{7,0},{0,7},{9,10},{10,9},{11,... | collective-permute-start | bytes 49160 | tf_op jit(solution)/shard_map/ppermute | solution.py:366
